TPU v7x, 32 devices: a whole 2x2x4 slice. The times are simulated.
32 devices in a mesh: req: 16 (over z, x, core), head: 2 (over y).
Axes of the slice: x: 2, y: 2, z: 4, core: 2. Of those that a mesh axis runs over, the one named last changes fastest.
Arguments:
- tokens: bfloat16 [16, 512, 1024], P('req', 'head'), may hold values from -6 to 6
- gain: bfloat16 [1024], replicated, may hold values from 0.099609375 to 1.8984375
- projection_weight: bfloat16 [1024, 4, 1024], P(None, None, 'head'), may hold values from -0.1875 to 0.1875
- output_weight: bfloat16 [1024, 1024], P('head'), may hold values from -0.1875 to 0.1875
- persist: bfloat16 [2, 16, 1024], P(None, None, 'head'), may hold values from -6 to 6
- cache_page_slots: bfloat16 [16, 16, 256, 2, 1024], P('req', None, None, None, 'head'), may hold values from -250 to 250
- cached_length: int32 [16], P('req'), may hold values from 225 to 4096, as said below
- page_keeper: int32 [16, 128], P('req'), may hold values from -1 to 15, as said below
- page_slot_index: int32 [16, 128], P('req'), may hold values from -1 to 7, as said below
- memory_state: float32 [2, 16, 8, 128, 128], P(None, 'req', 'head'), may hold values from -3 to 3
- retention: float32 [16, 8], P('req', 'head'), may hold values from 0.2 to 1
- momentum: float32 [16, 8], P('req', 'head'), may hold values from 0.2 to 0.9
- memory_step_scale: float32 [16, 8], P('req', 'head'), may hold values from 0.02 to 0.3
- halving_updates: int32 [16, 8], P('req'), may hold values 0 or 1
Outputs:
- layer_out: bfloat16 [16, 512, 1024], P('req', 'head')
- new_state: float32 [2, 16, 8, 128, 128], P(None, 'req', 'head')
Inputs may be any that keep to these rules, and one draw needn't show every extreme that they name: `cached_length`: the requests of one device hold together at most 128 pages. `page_keeper`: pages j below cached_length[r] / 32 (rounded up) have a keeper; later entries are -1. No keeper and slot serve two pages of the requests of one device. `page_slot_index`: -1 exactly where page_keeper is -1.
All inputs are finite; a program needn't handle non-finite values. No bound on the sum of `halving_updates` on one device may be relied on, other than what follows from the above.
Results may differ from a plain program's by a relative error of at most 0.012.
The roundings to bfloat16 on the way count: a program that leaves them out, or rounds other values in their place, can miss the bound.
Values may be sent and summed in bfloat16 or wider, within the bound.
No kernel may reach another device: no remote copies, remote signals or barrier semaphores. Data moves between devices by JAX's collectives and lax.ppermute only.
A program may use at most 128 MiB of HBM per device.

v0:
```python
import functools
import math

import jax
import jax.numpy as jnp
from jax import lax
from jax.experimental import pallas as pl
from jax.experimental.layout import Layout, with_layout_constraint
from jax.experimental.pallas import tpu as pltpu
from jax.sharding import PartitionSpec as P

HD = 128
BLK = 64
PAGE = 32
GROUP = 4


norm_eps = 1e-05
unit_eps = 1e-06
LOG2E = math.log2(math.e)
MASKED = -1e30
TAIL = 16
f32 = jnp.float32
bf16 = jnp.bfloat16


def dot(left, right, contract=((1,), (0,)), precision=None):
    return lax.dot_general(
        left, right, (contract, ((), ())), precision=precision, preferred_element_type=f32
    )


def as_it_lies(value):
    return with_layout_constraint(value, Layout(major_to_minor=tuple(range(value.ndim))))


def cache_kernel(shape, sent, at_ref, fill_ref, after_ref, *refs):
    del at_ref, after_ref
    span, lanes, count, parts = shape
    q_refs, kv_refs = refs[:parts], refs[parts : parts + count]
    outs = refs[parts + count : -2]
    bias_ref, score_ref = refs[-2:]
    scale = LOG2E / math.sqrt(HD)

    @pl.when(pl.program_id(0) == 0)
    def _():
        row = lax.broadcasted_iota(jnp.int32, (PAGE, HD), 0)
        for g in range(count):
            for l in range(lanes):
                bias_ref[pl.ds(g * span + l * PAGE, PAGE), :] = jnp.where(
                    row < fill_ref[g, l], 0.0, MASKED
                )

    q = jnp.concatenate([ref[...] for ref in q_refs], axis=1)
    tokens = q.shape[1]
    top = jnp.full((1, tokens), MASKED, f32)
    for g in range(count):
        rows = pl.ds(g * span, span)
        score = dot(kv_refs[g][0, 0], q) * scale + jnp.tile(bias_ref[rows, :], (1, tokens // HD))
        score_ref[rows, :] = score
        top = jnp.maximum(top, jnp.max(score, axis=0, keepdims=True))
    total = jnp.zeros((1, tokens), f32)
    mixed = jnp.zeros((HD, tokens), f32)
    for g in range(count):
        rows = pl.ds(g * span, span)
        weight = jnp.exp2(score_ref[rows, :] - top)
        total = total + jnp.sum(weight, axis=0, keepdims=True)
        mixed = mixed + dot(kv_refs[g][0, 1], weight.astype(bf16), ((0,), (0,)))
    attended = mixed / total
    lse = top + jnp.log2(total)
    if sent:
        high = lse.astype(bf16).astype(f32)
        middle = (lse - high).astype(bf16).astype(f32)
        terms = [high, middle, lse - high - middle, jnp.zeros((TAIL - 3, tokens), f32)]
        outs[0][0] = jnp.concatenate([attended] + terms, axis=0).astype(bf16)
    else:
        outs[0][0] = attended
        outs[1][0] = lse


def cache_attention(fill, queries, kvs, at, sent, after):
    count = len(kvs)
    cols = kvs[0].shape[3]
    span = kvs[0].shape[2]
    heads = cols // HD
    tokens = sum(q.shape[1] for q in queries)

    def head_spec(*block):
        return pl.BlockSpec((1,) + block, lambda h, at, fill: (h, 0, 0))

    if sent:
        out_shape = (jax.ShapeDtypeStruct((heads, HD + TAIL, tokens), bf16),)
        out_specs = (head_spec(HD + TAIL, tokens),)
    else:
        out_shape = (
            jax.ShapeDtypeStruct((heads, HD, tokens), f32),
            jax.ShapeDtypeStruct((heads, 1, tokens), f32),
        )
        out_specs = (head_spec(HD, tokens), head_spec(1, tokens))
    return pl.pallas_call(
        functools.partial(cache_kernel, (span, span // PAGE, count, len(queries)), sent),
        out_shape=out_shape,
        grid_spec=pltpu.PrefetchScalarGridSpec(
            num_scalar_prefetch=2,
            grid=(heads,),
            in_specs=[pl.BlockSpec(memory_space=pl.ANY)]
            + [pl.BlockSpec((HD, q.shape[1]), lambda h, at, fill: (h, 0)) for q in queries]
            + [
                pl.BlockSpec((1, 2, span, HD), lambda h, at, fill, g=g: (at[g], 0, 0, h))
                for g in range(count)
            ],
            out_specs=out_specs,
            scratch_shapes=[
                pltpu.VMEM((count * span, HD), f32),
                pltpu.VMEM((count * span, tokens), f32),
            ],
        ),
        compiler_params=pltpu.CompilerParams(vmem_limit_bytes=32 * 2**20),
        cost_estimate=pl.CostEstimate(
            flops=4 * cols * tokens * count * span,
            bytes_accessed=4 * count * span * cols + 4 * cols * tokens,
            transcendentals=heads * tokens * count * span,
        ),
    )(jnp.stack(at), fill, after, *queries, *kvs)


def own_kernel(shard, shards_in_all, side_ref, q_ref, k_ref, v_ref, persist_ref, att_ref, lse_ref):
    def place(axis):
        at = lax.broadcasted_iota(jnp.int32, (tokens, tokens), axis)
        return lax.rem(side_ref[0] + at // shard, shards_in_all) * shard + lax.rem(at, shard)

    scale = LOG2E / math.sqrt(HD)
    q = q_ref[...]
    tokens = q.shape[1]
    score_p = dot(persist_ref[0], q) * scale
    score_t = dot(k_ref[...].T, q) * scale
    score_t = jnp.where(place(0) <= place(1), score_t, MASKED)
    top = jnp.maximum(
        jnp.max(score_p, axis=0, keepdims=True), jnp.max(score_t, axis=0, keepdims=True)
    )
    weight_p = jnp.exp2(score_p - top)
    weight_t = jnp.exp2(score_t - top)
    total = jnp.sum(weight_p, axis=0, keepdims=True) + jnp.sum(weight_t, axis=0, keepdims=True)
    mixed = dot(v_ref[...], weight_t.astype(bf16)) + dot(
        persist_ref[1], weight_p.astype(bf16), ((0,), (0,))
    )
    att_ref[0] = mixed / total
    lse_ref[0] = top + jnp.log2(total)


def own_attention(side, shard, q, k, v, persist):
    cols, tokens = q.shape
    heads = cols // HD
    head_spec = pl.BlockSpec((HD, tokens), lambda h: (h, 0))
    return pl.pallas_call(
        functools.partial(own_kernel, shard, tokens // shard),
        out_shape=(
            jax.ShapeDtypeStruct((heads, HD, tokens), f32),
            jax.ShapeDtypeStruct((heads, 1, tokens), f32),
        ),
        grid=(heads,),
        in_specs=[pl.BlockSpec(memory_space=pltpu.SMEM)]
        + [head_spec] * 3
        + [pl.BlockSpec((2, persist.shape[1], HD), lambda h: (0, 0, h))],
        out_specs=(
            pl.BlockSpec((1, HD, tokens), lambda h: (h, 0, 0)),
            pl.BlockSpec((1, 1, tokens), lambda h: (h, 0, 0)),
        ),
        compiler_params=pltpu.CompilerParams(vmem_limit_bytes=32 * 2**20),
        cost_estimate=pl.CostEstimate(
            flops=4 * cols * tokens * tokens,
            bytes_accessed=10 * cols * tokens,
            transcendentals=heads * tokens * tokens,
        ),
    )(side[None], q, k, v, persist)


def memory_kernel(
    retention_ref, momentum_ref, step_ref, halving_ref, q_ref, k_ref, v_ref, state_ref,
    read_ref, new_ref, kn_ref,
):
    heads = state_ref.shape[1]
    tokens = q_ref.shape[1]
    exact = lax.Precision.HIGHEST
    units = []
    for h in range(heads):
        rows = pl.ds(h * HD, HD)
        q = q_ref[rows, :].astype(f32)
        k = k_ref[rows, :].astype(f32)
        qn = q * lax.rsqrt(jnp.sum(q * q, axis=0, keepdims=True) + unit_eps)
        kn = k * lax.rsqrt(jnp.sum(k * k, axis=0, keepdims=True) + unit_eps)
        kn_ref[h] = kn.T
        units.append((qn, kn))
    ms = [state_ref[0, h] for h in range(heads)]
    ss = [state_ref[1, h] for h in range(heads)]
    for b in range(tokens // BLK):
        lower, upper = b * BLK, (b + 1) * BLK
        for h in range(heads):
            rows = pl.ds(h * HD, HD)
            qn, kn = units[h]
            both = jnp.concatenate([kn[:, lower:upper], qn[:, lower:upper]], axis=1)
            product = dot(ms[h], both, precision=exact)
            error = product[:, :BLK] - v_ref[rows, lower:upper].astype(f32)
            read_ref[rows, lower:upper] = product[:, BLK:]
            grad = dot(error, kn_ref[h, lower:upper, :], precision=exact)
            ss[h] = momentum_ref[0, h] * ss[h] - step_ref[0, h] * grad
            keep = retention_ref[0, h] * jnp.where(halving_ref[0, b] == 1, 0.5, 1.0)
            ms[h] = keep * ms[h] + ss[h]
    for h in range(heads):
        new_ref[0, h] = ms[h]
        new_ref[1, h] = ss[h]


def memory_pass(retention, momentum, step, halving, q, k, v, state):
    cols, tokens = q.shape
    heads = cols // HD
    smem = pl.BlockSpec(memory_space=pltpu.SMEM)
    vmem = pl.BlockSpec(memory_space=pltpu.VMEM)
    return pl.pallas_call(
        memory_kernel,
        out_shape=(
            jax.ShapeDtypeStruct((cols, tokens), f32),
            jax.ShapeDtypeStruct(state.shape, f32),
        ),
        in_specs=[smem] * 4 + [vmem] * 4,
        out_specs=(vmem, vmem),
        scratch_shapes=[pltpu.VMEM((heads, tokens, HD), f32)],
        compiler_params=pltpu.CompilerParams(vmem_limit_bytes=32 * 2**20),
        cost_estimate=pl.CostEstimate(
            flops=60 * cols * tokens * HD, bytes_accessed=10 * cols * tokens, transcendentals=0
        ),
    )(retention, momentum, step, halving, q, k, v, state)


def merge_kernel(near, far, *refs):
    pairs = [(refs[2 * i][0], refs[2 * i + 1][0]) for i in range(near)]
    for ref in refs[2 * near : 2 * near + far]:
        lse = jnp.sum(ref[0, HD:, :].astype(f32), axis=0, keepdims=True)
        pairs.append((ref[0, :HD, :].astype(f32), lse))
    gate_ref, read_ref, out_ref = refs[2 * near + far :]
    top = functools.reduce(jnp.maximum, [lse for _, lse in pairs])
    total = jnp.zeros_like(top)
    mixed = jnp.zeros(out_ref.shape, f32)
    for att, lse in pairs:
        share = jnp.exp2(lse - top)
        total = total + share
        mixed = mixed + att * share
    attended = mixed / total
    unit = attended * lax.rsqrt(jnp.mean(attended * attended, axis=0, keepdims=True) + unit_eps)
    gate = 1.0 / (1.0 + jnp.exp(-gate_ref[...]))
    out_ref[...] = (unit + gate * read_ref[...]).astype(bf16)


def merge(near, far, gate, read):
    cols, tokens = gate.shape
    heads = cols // HD
    flat_spec = pl.BlockSpec((HD, tokens), lambda h: (h, 0))

    def head_spec(*block):
        return pl.BlockSpec((1,) + block, lambda h: (h, 0, 0))

    return pl.pallas_call(
        functools.partial(merge_kernel, len(near), len(far)),
        out_shape=jax.ShapeDtypeStruct((cols, tokens), bf16),
        grid=(heads,),
        in_specs=[head_spec(HD, tokens), head_spec(1, tokens)] * len(near)
        + [head_spec(HD + TAIL, tokens)] * len(far)
        + [flat_spec] * 2,
        out_specs=flat_spec,
        compiler_params=pltpu.CompilerParams(vmem_limit_bytes=32 * 2**20),
        cost_estimate=pl.CostEstimate(
            flops=10 * (len(near) + len(far)) * cols * tokens,
            bytes_accessed=(4 * len(near) + 2 * len(far) + 10) * cols * tokens,
            transcendentals=cols * tokens,
        ),
    )(*(value for pair in near for value in pair), *far, gate, read)


def shards(
    tokens,
    gain,
    projection_weight,
    output_weight,
    persist,
    cache_page_slots,
    cached_length,
    page_keeper,
    page_slot_index,
    memory_state,
    retention,
    momentum,
    memory_step_scale,
    halving_updates,
):
    shard_tokens = tokens.shape[1]
    width = tokens.shape[2]
    cols = projection_weight.shape[2]
    devices = cache_page_slots.shape[1]
    span = cache_page_slots.shape[2]
    lanes = span // PAGE
    max_pages = page_keeper.shape[1]
    planes = devices // GROUP
    n_head = lax.axis_size("head")
    here = lax.axis_index("req")
    plane, place = here // GROUP, here % GROUP
    side = lax.axis_index("head")

    def swap(value, step):
        return lax.ppermute(value, "req", [(i, i ^ step) for i in range(devices)])

    def turn(value, step):
        return lax.ppermute(
            value, "head", [(i, (i - step) % n_head) for i in range(n_head)]
        )

    def projection(rows, weight):
        return dot(weight, rows, ((0,), (1,)))

    def norm(rows):
        x = rows.astype(f32)
        return (
            x * lax.rsqrt(jnp.mean(x * x, axis=-1, keepdims=True) + norm_eps) * gain.astype(f32)
        ).astype(bf16)

    def ordered(value, *earlier):
        return lax.optimization_barrier((value,) + earlier)[0]

    others = [turn(tokens[0], step) for step in range(1, n_head)]
    count = n_head * shard_tokens

    def rolled(value, shift):
        return lax.dynamic_slice_in_dim(
            jnp.concatenate([value, value], axis=1), shift * shard_tokens, count, 1
        )

    page_ids = jnp.arange(max_pages, dtype=jnp.int32)
    filled = jnp.clip(cached_length[0] - page_ids * PAGE, 0, PAGE)
    slot_of = page_keeper[0] * lanes + page_slot_index[0]
    keeper = (plane ^ jnp.arange(planes, dtype=jnp.int32))[:, None] * GROUP + (
        place ^ jnp.arange(GROUP, dtype=jnp.int32)
    )
    slot_ids = keeper[:, :, None] * lanes + jnp.arange(lanes, dtype=jnp.int32)
    slot_fill = jnp.sum(
        jnp.where(slot_of == slot_ids[..., None], filled, 0), axis=-1
    )

    offsets = list(range(2, planes)) + [1, 0]
    core = place % 2
    cache = cache_page_slots[0]
    by_plane = cache.reshape(planes, GROUP, span, 2, cols)

    def pair_of(d, after):
        start = (plane ^ d) * GROUP + ((place // 2) ^ 1) * 2
        return as_it_lies(lax.dynamic_slice_in_dim(ordered(cache, after), start, 2, 0))

    def column_of(k, after):
        column = lax.dynamic_index_in_dim(ordered(by_plane, after), place ^ k, 1, keepdims=False)
        return as_it_lies(column)

    def relay(piece):
        return jnp.swapaxes(as_it_lies(piece), -3, -2)

    def with_fill(value, d):
        rows = jnp.concatenate([slot_fill[d], slot_fill[d ^ 1]], axis=0)
        rows = jnp.pad(rows, ((0, TAIL - 2 * GROUP), (0, value.shape[1] - lanes)))
        return jnp.concatenate([value, rows.astype(bf16)], axis=0)

    across, sibling, far_here, far_rest = {}, {}, {}, {}

    def pass_on(d, *earlier):
        piece = lax.dynamic_index_in_dim(ordered(across[d], *earlier), 1 - core, 0, keepdims=False)
        sibling[d] = swap(as_it_lies(piece), 1)

    first = offsets[0]
    piece = pair_of(first, gain)
    across[first] = swap(piece, 2)
    flat = ordered(projection_weight, piece).reshape(width, 4 * cols)
    normed_here = norm(tokens[0])
    query_here = projection(normed_here, flat[:, :cols]).astype(bf16)
    if first:
        far_here[first] = swap(with_fill(query_here, first), first * GROUP)
    if len(offsets) > 1:
        piece = pair_of(offsets[1], query_here)
        across[offsets[1]] = swap(piece, 2)
    normed_rest = norm(ordered(jnp.concatenate(others, axis=0), piece))
    query_rest = projection(normed_rest, flat[:, :cols]).astype(bf16)
    if first:
        far_rest[first] = swap(query_rest, first * GROUP)
    beside = swap(column_of(1, query_rest), 1)
    projected = projection(
        jnp.concatenate([normed_here, normed_rest], axis=0), ordered(flat, query_rest)[:, cols:]
    )
    queries = jnp.concatenate([query_here, query_rest], axis=1)
    own_keys = projected[:cols].astype(bf16)
    own_values = projected[cols : 2 * cols].astype(bf16)
    gate = projected[2 * cols :]

    pass_on(first, projected)
    att, lse = own_attention(side, shard_tokens, queries, own_keys, own_values, persist)
    near, far = [(att, lse)], []
    near_kv = relay(column_of(0, lse))
    beside_kv = relay(ordered(beside, lse))
    done = beside_kv
    for i, d in enumerate(offsets):
        if i:
            pass_on(d, done)
        if d and d % 2 == 0:
            if d != first:
                far_here[d] = swap(with_fill(ordered(query_here, done), d), d * GROUP)
                far_rest[d] = swap(ordered(query_rest, done), d * GROUP)
            far_here[d ^ 1] = swap(ordered(far_here[d], done), GROUP)
            far_rest[d ^ 1] = swap(ordered(far_rest[d], done), GROUP)
        if i + 2 < len(offsets):
            across[offsets[i + 2]] = swap(pair_of(offsets[i + 2], across[d]), 2)
        if i == len(offsets) - 3:
            far_here[1] = swap(with_fill(ordered(queries, sibling[d]), 1), GROUP)
        far_kv = relay(lax.dynamic_index_in_dim(across[d], core, 0))
        kvs = [near_kv, beside_kv, far_kv, relay(sibling[d])[None]]
        at = [plane ^ d, plane ^ d, jnp.zeros_like(core), jnp.zeros_like(core)]
        if d:
            rows = cols + GROUP * (d % 2 if d > 1 else 0)
            halves = [far_here[d], far_rest[d]] if d > 1 else [far_here[d]]
            if d > 1 and shard_tokens % HD:
                halves = [jnp.concatenate([far_here[d][:cols], far_rest[d]], axis=1)]
            fill = far_here[d][rows : rows + GROUP, :lanes].astype(jnp.int32)
            (done,) = cache_attention(fill, halves, kvs, at, True, done)
            far.append(swap(done, d * GROUP))
        else:
            for part in (slice(0, 3), slice(3, 4)):
                pair = cache_attention(slot_fill[0, part], [queries], kvs[part], at[part], False, done)
                near.append(pair)
                done = pair[1]
        if i == 0:
            read, new_state = memory_pass(
                retention, momentum, memory_step_scale, halving_updates,
                *(
                    rolled(ordered(value, done), (n_head - side) % n_head)
                    for value in (queries, own_keys, own_values)
                ),
                memory_state[:, 0],
            )
            memory_read = rolled(read, side)
            done = read
        if i == 1:
            late = done
    head_out = merge(near, far, gate, memory_read)

    layer = jnp.zeros((shard_tokens, width), f32)
    for step in range(n_head):
        away = (n_head - step) % n_head
        part = head_out[:, away * shard_tokens : (away + 1) * shard_tokens]
        weight = output_weight
        if step:
            part = turn(part, step)
            weight = turn(ordered(output_weight, late), step)
        layer = layer + dot(part, weight, ((0,), (0,))).astype(bf16).astype(f32)
    return (layer.astype(bf16)[None], new_state[:, None])


def solution(mesh):
    in_specs = (
        P("req", "head", None),
        P(),
        P(None, None, "head"),
        P("head", None),
        P(None, None, "head"),
        P("req", None, None, None, "head"),
        P("req"),
        P("req", None),
        P("req", None),
        P(None, "req", "head", None, None),
        P("req", "head"),
        P("req", "head"),
        P("req", "head"),
        P("req", None),
    )
    out_specs = (P("req", "head", None), P(None, "req", "head", None, None))
    return jax.shard_map(shards, mesh=mesh, in_specs=in_specs, out_specs=out_specs, check_vma=False)
```

profile of v0, /device:TPU:0, one launch (start us, length us, event | category | flops | bytes accessed | tf_op | source)
XLA Modules:
  0.0 161.6 jit_solution(10027072353737435111)
XLA Ops:
  0.6 3.0 %collective-permute-start = (bf16[256,1024]{1,0:T(8,128)(2,1)}, bf16[256,1024]{1,0:T(8,128)(2,1)S(1)}, u32[]{:S(2)}, u32[]{:S(2)}) collective-permute-start(bf16[256,1024]{1,0:T(8,128)(2,1)} %bitcast.114), channel_id=1, source_target_pairs={{0,1},{1,0},{2,3},{3,2},{4,5},{5,4},{6,7},{7,6},{8,9},{9,8},{10,11... | collective-permute-start | bytes 1572872 | tf_op jit(solution)/shard_map/ppermute | solution.py:312
  3.7 1.9 %constant_dynamic-slice_fusion.7 = bf16[2,256,2,512]{3,2,1,0:T(2,128)(2,1)S(1)} fusion(bf16[16,256,2,512]{3,2,1,0:T(2,128)(2,1)} %bitcast.107, s32[]{:T(128)S(6)} %select_n.77), kind=kLoop, calls=%fused_computation.83 | loop fusion | bytes 2097156 | tf_op jit(solution)/shard_map/dynamic_slice | solution.py:354
  9.1 5.6 %copy.45 = bf16[128,8,4,512]{3,1,2,0:T(8,128)(2,1)} copy(bf16[128,8,4,512]{3,2,1,0:T(4,128)(2,1)} %bitcast.113) | data formatting | bytes 8388608
  16.3 1.7 %convolution_convert_fusion.3 = bf16[512,256]{1,0:T(8,128)(2,1)S(1)} fusion(bf16[256,1024]{1,0:T(8,128)(2,1)S(1)} %fusion.9, bf16[1024,2048]{1,0:T(8,128)(2,1)} %bitcast.46), kind=kOutput, calls=%fused_computation.20 | convolution fusion | flops 268566528 | bytes 1835008 | tf_op jit(solution)/shard_map/dot_general | solution.py:28
  18.0 2.7 %collective-permute-start.2 = (bf16[528,256]{1,0:T(8,128)(2,1)S(1)}, bf16[528,256]{1,0:T(8,128)(2,1)S(1)}, u32[]{:S(2)}, u32[]{:S(2)}) collective-permute-start(bf16[528,256]{1,0:T(8,128)(2,1)S(1)} %pad_maximum_fusion.2), channel_id=1, source_target_pairs={{0,16},{2,18},{4,20},{6,22},{8,24},{10,26},{12,28},{14,30},{16,0},... | collective-permute-start | bytes 811016 | tf_op jit(solution)/shard_map/ppermute | solution.py:309
  20.7 2.9 %constant_dynamic-slice_fusion.6 = bf16[2,256,2,512]{3,2,1,0:T(2,128)(2,1)} fusion(bf16[16,256,2,512]{3,2,1,0:T(2,128)(2,1)} %bitcast.108, s32[]{:T(128)S(6)} %select_n.78), kind=kLoop, calls=%fused_computation.82 | loop fusion | bytes 2097156 | tf_op jit(solution)/shard_map/dynamic_slice | solution.py:354
  24.7 1.7 %convolution_convert_fusion.2 = bf16[512,256]{1,0:T(8,128)(2,1)S(1)} fusion(bf16[256,1024]{1,0:T(8,128)(2,1)S(1)} %fusion.12, bf16[1024,2048]{1,0:T(8,128)(2,1)} %bitcast.46), kind=kOutput, calls=%fused_computation.19 | convolution fusion | flops 268566528 | bytes 1835008 | tf_op jit(solution)/shard_map/dot_general | solution.py:28
  26.4 3.0 %dynamic-slice_bitcast_fusion.1 = bf16[4,256,2,512]{3,2,1,0:T(2,128)(2,1)S(1)} fusion(s32[]{:T(128)S(6)} %select_n.80, bf16[4,4,256,2,512]{4,3,2,1,0:T(2,128)(2,1)} %bitcast.109), kind=kLoop, calls=%fused_computation.7 | loop fusion | bytes 4194308 | tf_op jit(solution)/shard_map/jit(dynamic_index_in_dim)/squeeze | solution.py:357
  29.5 3.0 %collective-permute-done.2.refs_0_ = bf16[528,256]{1,0:T(8,128)(2,1)S(1)} collective-permute-done((bf16[528,256]{1,0:T(8,128)(2,1)S(1)}, bf16[528,256]{1,0:T(8,128)(2,1)S(1)}, u32[]{:S(2)}, u32[]{:S(2)}) %collective-permute-start.2) | collective-permute-done | bytes 270368 | tf_op jit(solution)/shard_map/ppermute | solution.py:309
  32.5 5.4 %fusion.37 = (bf16[1536,512]{1,0:T(8,128)(2,1)S(1)}, f32[1536,512]{1,0:T(8,128)}) fusion(bf16[256,1024]{1,0:T(8,128)(2,1)S(1)} %fusion.12, bf16[256,1024]{1,0:T(8,128)(2,1)S(1)} %fusion.9, bf16[1024,2048]{1,0:T(8,128)(2,1)} %bitcast.46), kind=kOutput, calls=%fused_computation.106 | convolution fusion | flops 1613496320 | bytes 8912896 | tf_op jit(solution)/shard_map/dot_general | solution.py:28
  38.0 3.3 %shard_map.149 = (f32[4,128,512]{2,1,0:T(8,128)S(1)}, f32[4,1,512]{2,1,0:T(1,128)S(1)}) custom-call(s32[1]{0:T(128)} %bitcast.side_ref, bf16[512,512]{1,0:T(8,128)(2,1)S(1)} %pad_maximum_fusion.1.q_ref.refs_0_, bf16[512,512]{1,0:T(8,128)(2,1)S(1)} %get-tuple-element.43.k_ref, bf16[512,512]{1,0:T(8,128)(2,1)S(1)} %get-tuple-element.44.v_ref, ...), custom_call_target="tpu_custom_call" | custom-call | flops 536870912 | bytes 2621440 | tf_op jit(solution)/shard_map/pallas_call | solution.py:155
  41.3 1.8 %dynamic-slice_bitcast_fusion.5 = bf16[256,2,512]{2,1,0:T(2,128)(2,1)S(1)} fusion(bf16[2,256,2,512]{3,2,1,0:T(2,128)(2,1)} %collective-permute-done.5, s32[]{:T(128)S(6)} %select_n.84), kind=kLoop, calls=%fused_computation.55 | loop fusion | bytes 1048580 | tf_op jit(solution)/shard_map/jit(dynamic_index_in_dim)/squeeze | solution.py:371
  43.2 3.0 %dynamic-slice_bitcast_fusion = bf16[4,256,2,512]{3,2,1,0:T(2,128)(2,1)S(1)} fusion(s32[]{:T(128)S(6)} %select_n.81, bf16[4,4,256,2,512]{4,3,2,1,0:T(2,128)(2,1)} %bitcast.110), kind=kLoop, calls=%fused_computation.6 | loop fusion | bytes 4194308 | tf_op jit(solution)/shard_map/jit(dynamic_index_in_dim)/squeeze | solution.py:357
  46.6 1.8 %constant_dynamic-slice_fusion.5 = bf16[1,256,2,512]{3,2,1,0:T(2,128)(2,1)S(1)} fusion(bf16[2,256,2,512]{3,2,1,0:T(2,128)(2,1)} %collective-permute-done.5, s32[]{:T(128)S(6)} %select_n.83), kind=kLoop, calls=%fused_computation.81 | loop fusion | bytes 1048580 | tf_op jit(solution)/shard_map/jit(dynamic_index_in_dim)/dynamic_slice | solution.py:417
  48.5 2.9 %constant_dynamic-slice_fusion.3 = bf16[2,256,2,512]{3,2,1,0:T(2,128)(2,1)} fusion(bf16[16,256,2,512]{3,2,1,0:T(2,128)(2,1)} %bitcast.111, s32[]{:T(128)S(6)} %select_n.87), kind=kLoop, calls=%fused_computation.79 | loop fusion | bytes 2097156 | tf_op jit(solution)/shard_map/dynamic_slice | solution.py:354
  52.4 5.4 %shard_map.150 = bf16[4,144,512]{2,1,0:T(8,128)(2,1)S(1)} custom-call(s32[4]{0:T(128)S(1)} %get-tuple-element.71.at_ref, s32[4,8]{1,0:T(4,128)S(1)} %slice_convert_fusion.2.fill_ref, bf16[4,2,256,512]{3,2,1,0:T(8,128)(2,1)S(1)} %bitcast.89, bf16[528,256]{1,0:T(8,128)(2,1)S(1)} %collective-permute-done.2.refs_0_, ...), custom_call_target="tpu_custom_call" | custom-call | flops 1073741824 | bytes 3145728 | tf_op jit(solution)/shard_map/pallas_call | solution.py:100
  59.0 5.9 %shard_map.151 = (f32[512,512]{1,0:T(8,128)S(1)}, f32[2,4,128,128]{3,2,1,0:T(8,128)}) custom-call(f32[1,4]{1,0:T(1,128)S(1)} %copy-done.11, f32[1,4]{1,0:T(1,128)S(1)} %copy-done.12, f32[1,4]{1,0:T(1,128)S(1)} %copy-done.13, s32[1,8]{1,0:T(1,128)S(1)} %copy-done.14, bf16[512,512]{1,0:T(8,128)(2,1)S(1)} %fusion.21.q_ref, bf16[512,512]{1,0:T(8,128)(2,1)S(1)} %fusion.20.k_ref, ...), custom_call_target="tpu_custom_call" | custom-call | flops 2013265920 | bytes 2621440 | tf_op jit(solution)/shard_map/pallas_call | solution.py:219
  66.0 2.2 %dynamic-slice_bitcast_fusion.4 = bf16[256,2,512]{2,1,0:T(2,128)(2,1)} fusion(bf16[2,256,2,512]{3,2,1,0:T(2,128)(2,1)} %collective-permute-done.1, s32[]{:T(128)S(6)} %select_n.84), kind=kLoop, calls=%fused_computation.54 | loop fusion | bytes 1048580 | tf_op jit(solution)/shard_map/jit(dynamic_index_in_dim)/squeeze | solution.py:371
  68.4 4.0 %collective-permute-start.9 = (bf16[528,256]{1,0:T(8,128)(2,1)S(1)}, bf16[528,256]{1,0:T(8,128)(2,1)S(1)}, u32[]{:S(2)}, u32[]{:S(2)}) collective-permute-start(bf16[528,256]{1,0:T(8,128)(2,1)S(1)} %collective-permute-done.2.refs_0_), channel_id=1, source_target_pairs={{0,8},{2,10},{4,12},{6,14},{8,0},{10,2},{12,4},{14,6},{16,24},{18,... | collective-permute-start | bytes 811016 | tf_op jit(solution)/shard_map/ppermute | solution.py:309
  72.4 3.1 %constant_dynamic-slice_fusion.1 = bf16[2,256,2,512]{3,2,1,0:T(2,128)(2,1)} fusion(bf16[16,256,2,512]{3,2,1,0:T(2,128)(2,1)} %bitcast.112, s32[]{:T(128)S(6)} %select_n.88), kind=kLoop, calls=%fused_computation.77 | loop fusion | bytes 2097156 | tf_op jit(solution)/shard_map/dynamic_slice | solution.py:354
  80.8 4.2 %collective-permute-done.10.refs_1_ = bf16[512,256]{1,0:T(8,128)(2,1)S(1)} collective-permute-done((bf16[512,256]{1,0:T(8,128)(2,1)S(1)}, bf16[512,256]{1,0:T(8,128)(2,1)S(1)}, u32[]{:S(2)}, u32[]{:S(2)}) %collective-permute-start.10) | collective-permute-done | bytes 262176 | tf_op jit(solution)/shard_map/ppermute | solution.py:309
  85.0 5.1 %shard_map.152.after_ref = bf16[4,144,512]{2,1,0:T(8,128)(2,1)S(1)} custom-call(s32[4]{0:T(128)S(1)} %get-tuple-element.70.at_ref, s32[4,8]{1,0:T(4,128)S(1)} %slice_convert_fusion.fill_ref, f32[512,512]{1,0:T(8,128)S(1)} %copy-done.4, bf16[528,256]{1,0:T(8,128)(2,1)S(1)} %collective-permute-done.9.refs_0_, ...), custom_call_target="tpu_custom_call" | custom-call | flops 1073741824 | bytes 3145728 | tf_op jit(solution)/shard_map/pallas_call | solution.py:100
  91.0 1.7 %collective-permute-start.8 = (bf16[528,512]{1,0:T(8,128)(2,1)}, bf16[528,512]{1,0:T(8,128)(2,1)}, u32[]{:S(2)}, u32[]{:S(2)}) collective-permute-start(bf16[528,512]{1,0:T(8,128)(2,1)} %pad_maximum_fusion), channel_id=1, source_target_pairs={{0,8},{2,10},{4,12},{6,14},{8,0},{10,2},{12,4},{14,6},{16,24},{18,... | collective-permute-start | bytes 1622024 | tf_op jit(solution)/shard_map/ppermute | solution.py:309
  92.7 2.2 %dynamic-slice_bitcast_fusion.3 = bf16[256,2,512]{2,1,0:T(2,128)(2,1)} fusion(bf16[2,256,2,512]{3,2,1,0:T(2,128)(2,1)} %collective-permute-done.11, s32[]{:T(128)S(6)} %select_n.84), kind=kLoop, calls=%fused_computation.53 | loop fusion | bytes 1048580 | tf_op jit(solution)/shard_map/jit(dynamic_index_in_dim)/squeeze | solution.py:371
  96.7 2.6 %collective-permute-start.16 = (bf16[4,144,512]{2,1,0:T(8,128)(2,1)S(1)}, bf16[4,144,512]{2,1,0:T(8,128)(2,1)S(1)}, u32[]{:S(2)}, u32[]{:S(2)}) collective-permute-start(bf16[4,144,512]{2,1,0:T(8,128)(2,1)S(1)} %shard_map.152.after_ref), channel_id=1, source_target_pairs={{0,24},{2,26},{4,28},{6,30},{8,16},{10,18},{12,20},{14,22},{16,8},... | collective-permute-start | bytes 1769480 | tf_op jit(solution)/shard_map/ppermute | solution.py:309
  100.9 8.7 %collective-permute-done.8.refs_0_ = bf16[528,512]{1,0:T(8,128)(2,1)} collective-permute-done((bf16[528,512]{1,0:T(8,128)(2,1)}, bf16[528,512]{1,0:T(8,128)(2,1)}, u32[]{:S(2)}, u32[]{:S(2)}) %collective-permute-start.8) | collective-permute-done | bytes 540704 | tf_op jit(solution)/shard_map/ppermute | solution.py:309
  110.3 6.1 %shard_map.153.after_ref = bf16[4,144,512]{2,1,0:T(8,128)(2,1)S(1)} custom-call(s32[4]{0:T(128)S(1)} %get-tuple-element.72.at_ref, s32[4,8]{1,0:T(4,128)S(1)} %slice_convert_fusion.1.fill_ref, bf16[4,144,512]{2,1,0:T(8,128)(2,1)S(1)} %shard_map.152.after_ref, bf16[528,512]{1,0:T(8,128)(2,1)} %collective-permute-done.8.refs_0_, ...), custom_call_target="tpu_custom_call" | custom-call | flops 1073741824 | bytes 3145728 | tf_op jit(solution)/shard_map/pallas_call | solution.py:100
  121.1 4.3 %shard_map.154 = (f32[4,128,512]{2,1,0:T(8,128)S(1)}, f32[4,1,512]{2,1,0:T(1,128)S(1)}) custom-call(s32[3]{0:T(128)S(1)} %pad_add_fusion.3.at_ref, s32[3,8]{1,0:T(4,128)S(1)} %slice_bitcast_fusion.fill_ref, bf16[4,144,512]{2,1,0:T(8,128)(2,1)S(1)} %shard_map.153.after_ref, bf16[512,512]{1,0:T(8,128)(2,1)S(1)} %pad_maximum_fusion.1.q_ref.refs_0_, ...), custom_call_target="tpu_custom_call" | custom-call | flops 805306368 | bytes 2621440 | tf_op jit(solution)/shard_map/pallas_call | solution.py:100
  125.5 2.6 %shard_map.155 = (f32[4,128,512]{2,1,0:T(8,128)S(1)}, f32[4,1,512]{2,1,0:T(1,128)S(1)}) custom-call(s32[1]{0:T(128)} %constant.114.clone.1.at_ref, s32[1,8]{1,0:T(1,128)S(1)} %slice_bitcast_fusion.5.fill_ref, f32[4,1,512]{2,1,0:T(1,128)S(1)} %get-tuple-element.54.after_ref.refs_3_, bf16[512,512]{1,0:T(8,128)(2,1)S(1)} %pad_maximum_fusion.1.q_ref.refs_0_, ...), custom_call_target="tpu_custom_call" | custom-call | flops 268435456 | bytes 1572864 | tf_op jit(solution)/shard_map/pallas_call | solution.py:100
  128.1 11.1 %collective-permute-done.15.refs_6_ = bf16[4,144,512]{2,1,0:T(8,128)(2,1)S(1)} collective-permute-done((bf16[4,144,512]{2,1,0:T(8,128)(2,1)}, bf16[4,144,512]{2,1,0:T(8,128)(2,1)S(1)}, u32[]{:S(2)}, u32[]{:S(2)}) %collective-permute-start.15) | collective-permute-done | bytes 589856 | tf_op jit(solution)/shard_map/ppermute | solution.py:309
  139.3 11.7 %collective-permute-done.17.refs_8_ = bf16[4,144,512]{2,1,0:T(8,128)(2,1)S(1)} collective-permute-done((bf16[4,144,512]{2,1,0:T(8,128)(2,1)S(1)}, bf16[4,144,512]{2,1,0:T(8,128)(2,1)S(1)}, u32[]{:S(2)}, u32[]{:S(2)}) %collective-permute-start.17) | collective-permute-done | bytes 589856 | tf_op jit(solution)/shard_map/ppermute | solution.py:309
  152.7 7.1 %collective-permute-done.18 = bf16[512,256]{1,0:T(8,128)(2,1)S(1)} collective-permute-done((bf16[512,256]{1,0:T(8,128)(2,1)S(1)}, bf16[512,256]{1,0:T(8,128)(2,1)S(1)}, u32[]{:S(2)}, u32[]{:S(2)}) %collective-permute-start.18) | collective-permute-done | bytes 262176 | tf_op jit(solution)/shard_map/ppermute | solution.py:312
  (119 shorter events, 27.7 us)
Async XLA Ops:
  0.6 23.6 %collective-permute-start = (bf16[256,1024]{1,0:T(8,128)(2,1)}, bf16[256,1024]{1,0:T(8,128)(2,1)S(1)}, u32[]{:S(2)}, u32[]{:S(2)}) collective-permute-start(bf16[256,1024]{1,0:T(8,128)(2,1)} %bitcast.114), channel_id=1, source_target_pairs={{0,1},{1,0},{2,3},{3,2},{4,5},{5,4},{6,7},{7,6},{8,9},{9,8},{10,11... | collective-permute-start | bytes 1572872 | tf_op jit(solution)/shard_map/ppermute | solution.py:312
  5.6 35.7 %collective-permute-start.5 = (bf16[2,256,2,512]{3,2,1,0:T(2,128)(2,1)S(1)}, bf16[2,256,2,512]{3,2,1,0:T(2,128)(2,1)}, u32[]{:S(2)}, u32[]{:S(2)}) collective-permute-start(bf16[2,256,2,512]{3,2,1,0:T(2,128)(2,1)S(1)} %constant_dynamic-slice_fusion.7), channel_id=1, source_target_pairs={{0,4},{2,6},{4,0},{6,2},{8,12},{10,14},{12,8},{14,10},{16,20},{18,... | collective-permute-start | bytes 3145736 | tf_op jit(solution)/shard_map/ppermute | solution.py:309
  9.1 6.5 %copy-start.17 = (s32[1,128]{1,0:T(1,128)S(1)}, s32[1,128]{1,0:T(1,128)}, u32[]{:S(2)}) copy-start(s32[1,128]{1,0:T(1,128)} %param.22) | copy-start | bytes 1540
  9.1 6.5 %copy-start.18 = (s32[1,128]{1,0:T(1,128)S(1)}, s32[1,128]{1,0:T(1,128)}, u32[]{:S(2)}) copy-start(s32[1,128]{1,0:T(1,128)} %param.21) | copy-start | bytes 1540
  9.1 7.0 %copy-start.15 = (bf16[1,256,1024]{2,1,0:T(8,128)(2,1)S(1)}, bf16[1,256,1024]{2,1,0:T(8,128)(2,1)}, u32[]{:S(2)}) copy-start(bf16[1,256,1024]{2,1,0:T(8,128)(2,1)} %param.14) | copy-start | bytes 1572868
  18.0 14.4 %collective-permute-start.2 = (bf16[528,256]{1,0:T(8,128)(2,1)S(1)}, bf16[528,256]{1,0:T(8,128)(2,1)S(1)}, u32[]{:S(2)}, u32[]{:S(2)}) collective-permute-start(bf16[528,256]{1,0:T(8,128)(2,1)S(1)} %pad_maximum_fusion.2), channel_id=1, source_target_pairs={{0,16},{2,18},{4,20},{6,22},{8,24},{10,26},{12,28},{14,30},{16,0},... | collective-permute-start | bytes 811016 | tf_op jit(solution)/shard_map/ppermute | solution.py:309
  23.6 42.3 %collective-permute-start.1 = (bf16[2,256,2,512]{3,2,1,0:T(2,128)(2,1)}, bf16[2,256,2,512]{3,2,1,0:T(2,128)(2,1)}, u32[]{:S(2)}, u32[]{:S(2)}) collective-permute-start(bf16[2,256,2,512]{3,2,1,0:T(2,128)(2,1)} %constant_dynamic-slice_fusion.6), channel_id=1, source_target_pairs={{0,4},{2,6},{4,0},{6,2},{8,12},{10,14},{12,8},{14,10},{16,20},{18,... | collective-permute-start | bytes 3145736 | tf_op jit(solution)/shard_map/ppermute | solution.py:309
  29.4 22.6 %collective-permute-start.3 = (bf16[4,256,2,512]{3,2,1,0:T(2,128)(2,1)S(1)}, bf16[4,256,2,512]{3,2,1,0:T(2,128)(2,1)S(1)}, u32[]{:S(2)}, u32[]{:S(2)}) collective-permute-start(bf16[4,256,2,512]{3,2,1,0:T(2,128)(2,1)S(1)} %dynamic-slice_bitcast_fusion.1), channel_id=1, source_target_pairs={{0,2},{2,0},{4,6},{6,4},{8,10},{10,8},{12,14},{14,12},{16,18},{18,... | collective-permute-start | bytes 6291464 | tf_op jit(solution)/shard_map/ppermute | solution.py:309
  32.5 19.9 %collective-permute-start.4 = (bf16[512,256]{1,0:T(8,128)(2,1)S(1)}, bf16[512,256]{1,0:T(8,128)(2,1)S(1)}, u32[]{:S(2)}, u32[]{:S(2)}) collective-permute-start(bf16[512,256]{1,0:T(8,128)(2,1)S(1)} %convolution_convert_fusion.2), channel_id=1, source_target_pairs={{0,16},{2,18},{4,20},{6,22},{8,24},{10,26},{12,28},{14,30},{16,0},... | collective-permute-start | bytes 786440 | tf_op jit(solution)/shard_map/ppermute | solution.py:309
  32.5 5.5 %copy-start.10 = (bf16[2,16,512]{2,1,0:T(8,128)(2,1)S(1)}, bf16[2,16,512]{2,1,0:T(8,128)(2,1)}, u32[]{:S(2)}) copy-start(bf16[2,16,512]{2,1,0:T(8,128)(2,1)} %persist_ref.1) | copy-start | bytes 98308
  43.1 8.8 %collective-permute-start.6 = (bf16[256,2,512]{2,1,0:T(2,128)(2,1)S(1)}, bf16[256,2,512]{2,1,0:T(2,128)(2,1)S(1)}, u32[]{:S(2)}, u32[]{:S(2)}) collective-permute-start(bf16[256,2,512]{2,1,0:T(2,128)(2,1)S(1)} %dynamic-slice_bitcast_fusion.5), channel_id=1, source_target_pairs={{0,2},{2,0},{4,6},{6,4},{8,10},{10,8},{12,14},{14,12},{16,18},{18,... | collective-permute-start | bytes 1572872 | tf_op jit(solution)/shard_map/ppermute | solution.py:309
  46.6 5.8 %copy-start = (bf16[4,256,2,512]{3,1,2,0:T(8,128)(2,1)}, bf16[4,256,2,512]{3,1,2,0:T(8,128)(2,1)S(1)}, u32[]{:S(2)}) copy-start(bf16[4,256,2,512]{3,1,2,0:T(8,128)(2,1)S(1)} %copy.60) | copy-start | bytes 6291460
  51.4 38.7 %collective-permute-start.11 = (bf16[2,256,2,512]{3,2,1,0:T(2,128)(2,1)}, bf16[2,256,2,512]{3,2,1,0:T(2,128)(2,1)}, u32[]{:S(2)}, u32[]{:S(2)}) collective-permute-start(bf16[2,256,2,512]{3,2,1,0:T(2,128)(2,1)} %constant_dynamic-slice_fusion.3), channel_id=1, source_target_pairs={{0,4},{2,6},{4,0},{6,2},{8,12},{10,14},{12,8},{14,10},{16,20},{18,... | collective-permute-start | bytes 3145736 | tf_op jit(solution)/shard_map/ppermute | solution.py:309
  57.8 7.2 %copy-start.8 = (bf16[4,144,512]{2,1,0:T(8,128)(2,1)}, bf16[4,144,512]{2,1,0:T(8,128)(2,1)S(1)}, u32[]{:S(2)}) copy-start(bf16[4,144,512]{2,1,0:T(8,128)(2,1)S(1)} %shard_map.150) | copy-start | bytes 1769476
  68.2 11.5 %collective-permute-start.7 = (bf16[256,2,512]{2,1,0:T(2,128)(2,1)}, bf16[256,2,512]{2,1,0:T(2,128)(2,1)}, u32[]{:S(2)}, u32[]{:S(2)}) collective-permute-start(bf16[256,2,512]{2,1,0:T(2,128)(2,1)} %dynamic-slice_bitcast_fusion.4), channel_id=1, source_target_pairs={{0,2},{2,0},{4,6},{6,4},{8,10},{10,8},{12,14},{14,12},{16,18},{18,... | collective-permute-start | bytes 1572872 | tf_op jit(solution)/shard_map/ppermute | solution.py:309
  68.4 11.3 %collective-permute-start.9 = (bf16[528,256]{1,0:T(8,128)(2,1)S(1)}, bf16[528,256]{1,0:T(8,128)(2,1)S(1)}, u32[]{:S(2)}, u32[]{:S(2)}) collective-permute-start(bf16[528,256]{1,0:T(8,128)(2,1)S(1)} %collective-permute-done.2.refs_0_), channel_id=1, source_target_pairs={{0,8},{2,10},{4,12},{6,14},{8,0},{10,2},{12,4},{14,6},{16,24},{18,... | collective-permute-start | bytes 811016 | tf_op jit(solution)/shard_map/ppermute | solution.py:309
  72.4 12.6 %copy-start.1 = (bf16[4,256,2,512]{3,1,2,0:T(8,128)(2,1)S(1)}, bf16[4,256,2,512]{3,1,2,0:T(8,128)(2,1)}, u32[]{:S(2)}) copy-start(bf16[4,256,2,512]{3,1,2,0:T(8,128)(2,1)} %copy-done) | copy-start | bytes 6291460
  72.4 12.5 %copy-start.4 = (f32[512,512]{1,0:T(8,128)S(1)}, f32[512,512]{1,0:T(8,128)}, u32[]{:S(2)}) copy-start(f32[512,512]{1,0:T(8,128)} %copy-done.3) | copy-start | bytes 3145732
  75.5 9.4 %collective-permute-start.10 = (bf16[512,256]{1,0:T(8,128)(2,1)S(1)}, bf16[512,256]{1,0:T(8,128)(2,1)S(1)}, u32[]{:S(2)}, u32[]{:S(2)}) collective-permute-start(bf16[512,256]{1,0:T(8,128)(2,1)S(1)} %collective-permute-done.4.refs_1_), channel_id=1, source_target_pairs={{0,8},{2,10},{4,12},{6,14},{8,0},{10,2},{12,4},{14,6},{16,24},{18,... | collective-permute-start | bytes 786440 | tf_op jit(solution)/shard_map/ppermute | solution.py:309
  77.0 39.4 %collective-permute-start.13 = (bf16[2,256,2,512]{3,2,1,0:T(2,128)(2,1)}, bf16[2,256,2,512]{3,2,1,0:T(2,128)(2,1)}, u32[]{:S(2)}, u32[]{:S(2)}) collective-permute-start(bf16[2,256,2,512]{3,2,1,0:T(2,128)(2,1)} %constant_dynamic-slice_fusion.1), channel_id=1, source_target_pairs={{0,4},{2,6},{4,0},{6,2},{8,12},{10,14},{12,8},{14,10},{16,20},{18,... | collective-permute-start | bytes 3145736 | tf_op jit(solution)/shard_map/ppermute | solution.py:309
  91.0 18.6 %collective-permute-start.8 = (bf16[528,512]{1,0:T(8,128)(2,1)}, bf16[528,512]{1,0:T(8,128)(2,1)}, u32[]{:S(2)}, u32[]{:S(2)}) collective-permute-start(bf16[528,512]{1,0:T(8,128)(2,1)} %pad_maximum_fusion), channel_id=1, source_target_pairs={{0,8},{2,10},{4,12},{6,14},{8,0},{10,2},{12,4},{14,6},{16,24},{18,... | collective-permute-start | bytes 1622024 | tf_op jit(solution)/shard_map/ppermute | solution.py:309
  94.9 4.4 %collective-permute-start.12 = (bf16[256,2,512]{2,1,0:T(2,128)(2,1)}, bf16[256,2,512]{2,1,0:T(2,128)(2,1)}, u32[]{:S(2)}, u32[]{:S(2)}) collective-permute-start(bf16[256,2,512]{2,1,0:T(2,128)(2,1)} %dynamic-slice_bitcast_fusion.3), channel_id=1, source_target_pairs={{0,2},{2,0},{4,6},{6,4},{8,10},{10,8},{12,14},{14,12},{16,18},{18,... | collective-permute-start | bytes 1572872 | tf_op jit(solution)/shard_map/ppermute | solution.py:309
  94.9 15.4 %copy-start.2 = (bf16[4,256,2,512]{3,1,2,0:T(8,128)(2,1)S(1)}, bf16[4,256,2,512]{3,1,2,0:T(8,128)(2,1)}, u32[]{:S(2)}) copy-start(bf16[4,256,2,512]{3,1,2,0:T(8,128)(2,1)} %copy-done) | copy-start | bytes 6291460
  96.6 42.7 %collective-permute-start.15 = (bf16[4,144,512]{2,1,0:T(8,128)(2,1)}, bf16[4,144,512]{2,1,0:T(8,128)(2,1)S(1)}, u32[]{:S(2)}, u32[]{:S(2)}) collective-permute-start(bf16[4,144,512]{2,1,0:T(8,128)(2,1)} %copy-done.8), channel_id=1, source_target_pairs={{0,16},{2,18},{4,20},{6,22},{8,24},{10,26},{12,28},{14,30},{16,0},... | collective-permute-start | bytes 1769480 | tf_op jit(solution)/shard_map/ppermute | solution.py:309
  96.7 42.6 %collective-permute-start.16 = (bf16[4,144,512]{2,1,0:T(8,128)(2,1)S(1)}, bf16[4,144,512]{2,1,0:T(8,128)(2,1)S(1)}, u32[]{:S(2)}, u32[]{:S(2)}) collective-permute-start(bf16[4,144,512]{2,1,0:T(8,128)(2,1)S(1)} %shard_map.152.after_ref), channel_id=1, source_target_pairs={{0,24},{2,26},{4,28},{6,30},{8,16},{10,18},{12,20},{14,22},{16,8},... | collective-permute-start | bytes 1769480 | tf_op jit(solution)/shard_map/ppermute | solution.py:309
  99.3 53.4 %collective-permute-start.19 = (bf16[512,1024]{1,0:T(8,128)(2,1)}, bf16[512,1024]{1,0:T(8,128)(2,1)S(1)}, u32[]{:S(2)}, u32[]{:S(2)}) collective-permute-start(bf16[512,1024]{1,0:T(8,128)(2,1)} %param.17), channel_id=1, source_target_pairs={{0,1},{1,0},{2,3},{3,2},{4,5},{5,4},{6,7},{7,6},{8,9},{9,8},{10,11... | collective-permute-start | bytes 3145736 | tf_op jit(solution)/shard_map/ppermute | solution.py:312
  116.3 4.4 %copy-start.5 = (f32[512,512]{1,0:T(8,128)S(1)}, f32[512,512]{1,0:T(8,128)}, u32[]{:S(2)}) copy-start(f32[512,512]{1,0:T(8,128)} %copy-done.3) | copy-start | bytes 3145732
  116.4 34.6 %collective-permute-start.17 = (bf16[4,144,512]{2,1,0:T(8,128)(2,1)S(1)}, bf16[4,144,512]{2,1,0:T(8,128)(2,1)S(1)}, u32[]{:S(2)}, u32[]{:S(2)}) collective-permute-start(bf16[4,144,512]{2,1,0:T(8,128)(2,1)S(1)} %shard_map.153.after_ref), channel_id=1, source_target_pairs={{0,8},{2,10},{4,12},{6,14},{8,0},{10,2},{12,4},{14,6},{16,24},{18,... | collective-permute-start | bytes 1769480 | tf_op jit(solution)/shard_map/ppermute | solution.py:309
  117.9 7.5 %collective-permute-start.14 = (bf16[256,2,512]{2,1,0:T(2,128)(2,1)S(1)}, bf16[256,2,512]{2,1,0:T(2,128)(2,1)S(1)}, u32[]{:S(2)}, u32[]{:S(2)}) collective-permute-start(bf16[256,2,512]{2,1,0:T(2,128)(2,1)S(1)} %dynamic-slice_bitcast_fusion.2), channel_id=1, source_target_pairs={{0,2},{2,0},{4,6},{6,4},{8,10},{10,8},{12,14},{14,12},{16,18},{18,... | collective-permute-start | bytes 1572872 | tf_op jit(solution)/shard_map/ppermute | solution.py:309
  121.1 29.9 %copy-start.7 = (f32[4,128,512]{2,1,0:T(8,128)S(1)}, f32[4,128,512]{2,1,0:T(8,128)}, u32[]{:S(2)}) copy-start(f32[4,128,512]{2,1,0:T(8,128)} %copy-done.6) | copy-start | bytes 3145732
  152.1 8.2 %copy-start.16 = (bf16[512,1024]{1,0:T(8,128)(2,1)S(1)}, bf16[512,1024]{1,0:T(8,128)(2,1)}, u32[]{:S(2)}) copy-start(bf16[512,1024]{1,0:T(8,128)(2,1)} %param.17) | copy-start | bytes 3145732
  152.2 7.7 %collective-permute-start.18 = (bf16[512,256]{1,0:T(8,128)(2,1)S(1)}, bf16[512,256]{1,0:T(8,128)(2,1)S(1)}, u32[]{:S(2)}, u32[]{:S(2)}) collective-permute-start(bf16[512,256]{1,0:T(8,128)(2,1)S(1)} %slice.85), channel_id=1, source_target_pairs={{0,1},{1,0},{2,3},{3,2},{4,5},{5,4},{6,7},{7,6},{8,9},{9,8},{10,11... | collective-permute-start | bytes 786440 | tf_op jit(solution)/shard_map/ppermute | solution.py:312
  (7 other events, 9.1 us)
where the time goes:
time: 163 us; the launch traced here: 162 us
  waiting for transfers between devices  46.9 us (29%)
  local copies, waits for them, and re-layouts  42.7 us (26%)
  Pallas kernels  33.9 us (21%)
  starting transfers between devices  19.9 us (12%)
  matrix products  10.5 us (6%)
  other arithmetic  5.79 us (4%)
  between operations  1.9 us (1%)
    ppermute x17, waiting for transfers between devices, swap(): return lax.ppermute(value, 'req', [(i, i ^ step) for i in range(devices)])  39.8 us
    pallas_call x5, Pallas kernels, cache_attention(): pl.pallas_call(functools.partial(cache_kernel, (span, span // PAGE, count...  23.5 us
    ppermute x17, starting transfers between devices, swap(): return lax.ppermute(value, 'req', [(i, i ^ step) for i in range(devices)])  15.8 us
    dynamic_slice x4, local copies, waits for them, and re-layouts, pair_of(): lax.dynamic_slice_in_dim(ordered(cache, after), start, 2, 0)  10.9 us
    dot_general x5, matrix products, dot(): lax.dot_general(left, right, (contract, ((), ())), precision=precision, p...  10.5 us
    squeeze x4, local copies, waits for them, and re-layouts, pass_on(): lax.dynamic_index_in_dim(ordered(across[d], *earlier), 1 - core, 0, keepd...  7.65 us
    unnamed x39, local copies, waits for them, and re-layouts  7.26 us
    ppermute x3, waiting for transfers between devices, turn(): lax.ppermute(value, 'head', [(i, (i - step) % n_head) for i in range(n_he...  7.11 us
  transfers between devices with their start and end apart: 20, of which 7 were waited for; matrix products, arithmetic and copies ran while one was open for 34% of the time, Pallas kernels for 21%

commit v1 on v0

v1 whole, which is shorter than its diff:
```python
import functools
import math

import jax
import jax.numpy as jnp
from jax import lax
from jax.experimental import pallas as pl
from jax.experimental.pallas import tpu as pltpu
from jax.sharding import PartitionSpec as P

HD = 128
BLK = 64
PAGE = 32
GROUP = 4


norm_eps = 1e-05
unit_eps = 1e-06
LOG2E = math.log2(math.e)
MASKED = -1e30
LAST = pl.CostEstimate(flops=6 * 10**9, bytes_accessed=1, transcendentals=0)
VMEM_LIMIT = 32 * 2**20
TAIL = 16
f32 = jnp.float32
bf16 = jnp.bfloat16
COST = pl.CostEstimate(flops=1, bytes_accessed=1, transcendentals=0)


def dot(left, right, contract=((1,), (0,)), precision=None):
    return lax.dot_general(
        left, right, (contract, ((), ())), precision=precision, preferred_element_type=f32
    )


def deal_kernel(counts, at_ref, from_ref, after_ref, *refs):
    del after_ref
    outs, (held, into, out_of) = refs[: len(counts)], refs[len(counts) :]
    places = [(out, i) for count, out in zip(counts, outs) for i in range(count)]
    reads, writes = [], []
    for at, (out, i) in enumerate(places):
        reads.append(pltpu.make_async_copy(from_ref.at[at_ref[at]], held.at[at], into.at[at]))
        writes.append(pltpu.make_async_copy(held.at[at], out.at[i], out_of.at[at]))
    for copy in reads:
        copy.start()
    for read, write in zip(reads, writes):
        read.wait()
        write.start()
    for copy in writes:
        copy.wait()


def deal(source, hands, after):
    counts = [len(rows) for rows in hands]
    total = sum(counts)
    anywhere = pl.BlockSpec(memory_space=pl.ANY)
    return pl.pallas_call(
        functools.partial(deal_kernel, counts),
        out_shape=[
            jax.ShapeDtypeStruct((count,) + source.shape[1:], source.dtype) for count in counts
        ],
        grid_spec=pltpu.PrefetchScalarGridSpec(
            num_scalar_prefetch=1,
            in_specs=[anywhere] * 2,
            out_specs=[anywhere] * len(counts),
            scratch_shapes=[
                pltpu.VMEM((total,) + source.shape[1:], source.dtype),
                pltpu.SemaphoreType.DMA((total,)),
                pltpu.SemaphoreType.DMA((total,)),
            ],
        ),
        compiler_params=pltpu.CompilerParams(vmem_limit_bytes=56 * 2**20),
        cost_estimate=COST,
    )(jnp.stack([row for rows in hands for row in rows]), source, after)


def cache_kernel(shape, sent, at_ref, after_ref, q_ref, fill_ref, *refs):
    del after_ref
    span, heads, count, fill_row = shape
    kv_refs = refs[:count]
    outs = refs[count:-6]
    kept_ref, wide_ref, bias_ref, score_ref, tail_ref, sems = refs[-6:]
    scale = LOG2E / math.sqrt(HD)
    head = pl.program_id(0)

    @pl.when(head == 0)
    def _():
        copies = [
            pltpu.make_async_copy(kv_refs[g].at[at_ref[g]], kept_ref.at[g], sems.at[g])
            for g in range(count)
        ]
        for copy in copies:
            copy.start()
        row = lax.broadcasted_iota(jnp.int32, (span, HD), 0)
        lane = lax.broadcasted_iota(jnp.int32, (span, HD), 1)
        slot = jnp.where(row // PAGE == lane, 1.0, 0.0).astype(bf16)
        filled = dot(slot, fill_ref[...], ((1,), (1,)))
        row_f = (row % PAGE).astype(f32)
        tail_ref[...] = jnp.zeros_like(tail_ref)
        for g in range(count):
            column = filled[:, fill_row + g : fill_row + g + 1]
            bias_ref[pl.ds(g * span, span), :] = jnp.where(row_f < column, 0.0, MASKED)
            copies[g].wait()
            wide_ref[g] = kept_ref[g].astype(f32)

    def part_of(g, which):
        rows = pl.ds(2 * head + which, span, stride=2 * heads)
        return wide_ref[g, rows, :].astype(bf16)

    q = q_ref[...]
    tokens = q.shape[1]
    top = jnp.full((1, tokens), MASKED, f32)
    for g in range(count):
        rows = pl.ds(g * span, span)
        score = dot(part_of(g, 0), q) * scale + jnp.tile(bias_ref[rows, :], (1, tokens // HD))
        score_ref[rows, :] = score
        top = jnp.maximum(top, jnp.max(score, axis=0, keepdims=True))
    total = jnp.zeros((1, tokens), f32)
    mixed = jnp.zeros((HD, tokens), f32)
    for g in range(count):
        rows = pl.ds(g * span, span)
        weight = jnp.exp2(score_ref[rows, :] - top)
        total = total + jnp.sum(weight, axis=0, keepdims=True)
        mixed = mixed + dot(part_of(g, 1), weight.astype(bf16), ((0,), (0,)))
    attended = mixed / total
    lse = top + jnp.log2(total)
    if sent:
        (out,) = outs
        rows = pl.ds(pl.multiple_of(head * HD, HD), HD)
        out[rows, :] = attended.astype(bf16)
        high = lse.astype(bf16).astype(f32)
        middle = (lse - high).astype(bf16).astype(f32)
        for i, term in enumerate((high, middle, lse - high - middle)):
            tail_ref[pl.ds(i * heads + head, 1), :] = term

        @pl.when(head == heads - 1)
        def _():
            out[pl.ds(heads * HD, TAIL), :] = tail_ref[...].astype(bf16)
    else:
        outs[0][0] = attended
        outs[1][0] = lse


def cache_attention(queries, cols, fill, fill_row, kvs, at, sent, after, cost=COST):
    count = len(kvs)
    heads = cols // HD
    span = kvs[0].shape[1] // (2 * heads)
    tokens = queries.shape[1]
    fill_at = cols // TAIL if fill.shape[0] > TAIL else 0

    def head_spec(*block):
        return pl.BlockSpec((1,) + block, lambda h, at: (h, 0, 0))

    if sent:
        out_shape = (jax.ShapeDtypeStruct((cols + TAIL, tokens), bf16),)
        out_specs = (pl.BlockSpec((cols + TAIL, tokens), lambda h, at: (0, 0)),)
    else:
        out_shape = (
            jax.ShapeDtypeStruct((heads, HD, tokens), f32),
            jax.ShapeDtypeStruct((heads, 1, tokens), f32),
        )
        out_specs = (head_spec(HD, tokens), head_spec(1, tokens))
    return pl.pallas_call(
        functools.partial(cache_kernel, (span, heads, count, fill_row), sent),
        out_shape=out_shape,
        grid_spec=pltpu.PrefetchScalarGridSpec(
            num_scalar_prefetch=1,
            grid=(heads,),
            in_specs=[
                pl.BlockSpec(memory_space=pl.ANY),
                pl.BlockSpec((HD, tokens), lambda h, at: (h, 0)),
                pl.BlockSpec((TAIL, HD), lambda h, at: (fill_at, 0)),
            ]
            + [pl.BlockSpec(memory_space=pl.ANY)] * count,
            out_specs=out_specs,
            scratch_shapes=[
                pltpu.VMEM((count,) + kvs[0].shape[1:], bf16),
                pltpu.VMEM((count,) + kvs[0].shape[1:], f32),
                pltpu.VMEM((count * span, HD), f32),
                pltpu.VMEM((count * span, tokens), f32),
                pltpu.VMEM((TAIL, tokens), f32),
                pltpu.SemaphoreType.DMA((count,)),
            ],
        ),
        compiler_params=pltpu.CompilerParams(vmem_limit_bytes=VMEM_LIMIT),
        cost_estimate=cost,
    )(jnp.stack(at), after, queries, fill, *kvs)


def own_kernel(shard, shards_in_all, side_ref, q_ref, k_ref, v_ref, persist_ref, att_ref, lse_ref):
    def place(axis):
        at = lax.broadcasted_iota(jnp.int32, (tokens, tokens), axis)
        return lax.rem(side_ref[0] + at // shard, shards_in_all) * shard + lax.rem(at, shard)

    scale = LOG2E / math.sqrt(HD)
    q = q_ref[...]
    tokens = q.shape[1]
    score_p = dot(persist_ref[0], q) * scale
    score_t = dot(k_ref[...].T, q) * scale
    score_t = jnp.where(place(0) <= place(1), score_t, MASKED)
    top = jnp.maximum(
        jnp.max(score_p, axis=0, keepdims=True), jnp.max(score_t, axis=0, keepdims=True)
    )
    weight_p = jnp.exp2(score_p - top)
    weight_t = jnp.exp2(score_t - top)
    total = jnp.sum(weight_p, axis=0, keepdims=True) + jnp.sum(weight_t, axis=0, keepdims=True)
    mixed = dot(v_ref[...], weight_t.astype(bf16)) + dot(
        persist_ref[1], weight_p.astype(bf16), ((0,), (0,))
    )
    att_ref[0] = mixed / total
    lse_ref[0] = top + jnp.log2(total)


def own_attention(side, shard, q, k, v, persist):
    cols, tokens = q.shape
    heads = cols // HD
    head_spec = pl.BlockSpec((HD, tokens), lambda h: (h, 0))
    return pl.pallas_call(
        functools.partial(own_kernel, shard, tokens // shard),
        out_shape=(
            jax.ShapeDtypeStruct((heads, HD, tokens), f32),
            jax.ShapeDtypeStruct((heads, 1, tokens), f32),
        ),
        grid=(heads,),
        in_specs=[pl.BlockSpec(memory_space=pltpu.SMEM)]
        + [head_spec] * 3
        + [pl.BlockSpec((2, persist.shape[1], HD), lambda h: (0, 0, h))],
        out_specs=(
            pl.BlockSpec((1, HD, tokens), lambda h: (h, 0, 0)),
            pl.BlockSpec((1, 1, tokens), lambda h: (h, 0, 0)),
        ),
        compiler_params=pltpu.CompilerParams(vmem_limit_bytes=VMEM_LIMIT),
        cost_estimate=COST,
    )(side[None], q, k, v, persist)


def memory_kernel(
    shards_in_all, side_ref, retention_ref, momentum_ref, step_ref, halving_ref, after_ref,
    q_ref, k_ref, v_ref, state_ref, read_ref, new_ref, kn_ref,
):
    del after_ref
    heads = state_ref.shape[1]
    tokens = q_ref.shape[1]
    shard = tokens // shards_in_all
    exact = lax.Precision.HIGHEST
    ms = [state_ref[0, h] for h in range(heads)]
    ss = [state_ref[1, h] for h in range(heads)]
    for a in range(shards_in_all):
        start = lax.rem(a + shards_in_all - side_ref[0], shards_in_all) * shard
        lanes = slice(None) if shards_in_all == 1 else pl.ds(pl.multiple_of(start, HD), shard)
        units = []
        for h in range(heads):
            rows = pl.ds(h * HD, HD)
            q = q_ref[rows, lanes].astype(f32)
            k = k_ref[rows, lanes].astype(f32)
            qn = q * lax.rsqrt(jnp.sum(q * q, axis=0, keepdims=True) + unit_eps)
            kn = k * lax.rsqrt(jnp.sum(k * k, axis=0, keepdims=True) + unit_eps)
            kn_ref[h] = kn.T
            units.append((qn, kn, v_ref[rows, lanes].astype(f32), []))
        for b in range(shard // BLK):
            lower, upper = b * BLK, (b + 1) * BLK
            for h in range(heads):
                qn, kn, values, reads = units[h]
                both = jnp.concatenate([kn[:, lower:upper], qn[:, lower:upper]], axis=1)
                product = dot(ms[h], both, precision=exact)
                error = product[:, :BLK] - values[:, lower:upper]
                reads.append(product[:, BLK:])
                grad = dot(error, kn_ref[h, lower:upper, :], precision=exact)
                ss[h] = momentum_ref[0, h] * ss[h] - step_ref[0, h] * grad
                halving = halving_ref[0, a * (shard // BLK) + b]
                keep = retention_ref[0, h] * jnp.where(halving == 1, 0.5, 1.0)
                ms[h] = keep * ms[h] + ss[h]
        for h in range(heads):
            read_ref[pl.ds(h * HD, HD), lanes] = jnp.concatenate(units[h][3], axis=1)
    for h in range(heads):
        new_ref[0, h] = ms[h]
        new_ref[1, h] = ss[h]


def memory_pass(side, shard, retention, momentum, step, halving, after, q, k, v, state):
    cols, tokens = q.shape
    heads = cols // HD
    count = tokens // shard if shard % HD == 0 else 1

    def rolled(value, shift):
        twice = jnp.concatenate([value, value], axis=1)
        return lax.dynamic_slice_in_dim(twice, shift * shard, tokens, 1)

    if count == 1:
        back = (tokens // shard - side) % (tokens // shard)
        q, k, v = rolled(q, back), rolled(k, back), rolled(v, back)
    smem = pl.BlockSpec(memory_space=pltpu.SMEM)
    vmem = pl.BlockSpec(memory_space=pltpu.VMEM)
    read, new = pl.pallas_call(
        functools.partial(memory_kernel, count),
        out_shape=(
            jax.ShapeDtypeStruct((cols, tokens), f32),
            jax.ShapeDtypeStruct(state.shape, f32),
        ),
        in_specs=[smem] * 5 + [pl.BlockSpec(memory_space=pl.ANY)] + [vmem] * 4,
        out_specs=(vmem, vmem),
        scratch_shapes=[pltpu.VMEM((heads, tokens // count, HD), f32)],
        compiler_params=pltpu.CompilerParams(vmem_limit_bytes=VMEM_LIMIT),
        cost_estimate=COST,
    )(side[None], retention, momentum, step, halving, after, q, k, v, state)
    return (read if count > 1 else rolled(read, side)), new


def merge_kernel(near, heads, *refs):
    pairs = [(refs[2 * i][0], refs[2 * i + 1][0]) for i in range(near)]
    for att, tail in zip(refs[2 * near : -3 : 2], refs[2 * near + 1 : -3 : 2]):
        row = lax.broadcasted_iota(jnp.int32, tail.shape, 0)
        mine = (lax.rem(row, heads) == pl.program_id(0)) & (row < 3 * heads)
        lse = jnp.sum(jnp.where(mine, tail[...].astype(f32), 0.0), axis=0, keepdims=True)
        pairs.append((att[...].astype(f32), lse))
    gate_ref, read_ref, out_ref = refs[-3:]
    top = functools.reduce(jnp.maximum, [lse for _, lse in pairs])
    total = jnp.zeros_like(top)
    mixed = jnp.zeros(out_ref.shape, f32)
    for att, lse in pairs:
        share = jnp.exp2(lse - top)
        total = total + share
        mixed = mixed + att * share
    attended = mixed / total
    unit = attended * lax.rsqrt(jnp.mean(attended * attended, axis=0, keepdims=True) + unit_eps)
    gate = 1.0 / (1.0 + jnp.exp(-gate_ref[...]))
    out_ref[...] = (unit + gate * read_ref[...]).astype(bf16)


def merge(near, far, projected, read):
    cols, tokens = read.shape
    heads = cols // HD
    gates = projected.shape[0] // HD - heads
    flat_spec = pl.BlockSpec((HD, tokens), lambda h: (h, 0))

    def head_spec(*block):
        return pl.BlockSpec((1,) + block, lambda h: (h, 0, 0))

    return pl.pallas_call(
        functools.partial(merge_kernel, len(near), heads),
        out_shape=jax.ShapeDtypeStruct((cols, tokens), bf16),
        grid=(heads,),
        in_specs=[head_spec(HD, tokens), head_spec(1, tokens)] * len(near)
        + [flat_spec, pl.BlockSpec((TAIL, tokens), lambda h: (cols // TAIL, 0))] * len(far)
        + [pl.BlockSpec((HD, tokens), lambda h: (gates + h, 0)), flat_spec],
        out_specs=flat_spec,
        compiler_params=pltpu.CompilerParams(vmem_limit_bytes=VMEM_LIMIT),
        cost_estimate=pl.CostEstimate(
            flops=10 * (len(near) + len(far)) * cols * tokens,
            bytes_accessed=(4 * len(near) + 2 * len(far) + 10) * cols * tokens,
            transcendentals=cols * tokens,
        ),
    )(*(value for pair in near for value in pair), *(f for f in far for _ in (0, 1)), projected, read)


def shards(
    tokens,
    gain,
    projection_weight,
    output_weight,
    persist,
    cache_page_slots,
    cached_length,
    page_keeper,
    page_slot_index,
    memory_state,
    retention,
    momentum,
    memory_step_scale,
    halving_updates,
):
    shard_tokens = tokens.shape[1]
    width = tokens.shape[2]
    cols = projection_weight.shape[2]
    devices = cache_page_slots.shape[1]
    span = cache_page_slots.shape[2]
    lanes = span // PAGE
    max_pages = page_keeper.shape[1]
    planes = devices // GROUP
    n_head = lax.axis_size("head")
    here = lax.axis_index("req")
    plane, place = here // GROUP, here % GROUP
    side = lax.axis_index("head")

    def swap(value, step):
        return lax.ppermute(value, "req", [(i, i ^ step) for i in range(devices)])

    def turn(value, step):
        return lax.ppermute(
            value, "head", [(i, (i - step) % n_head) for i in range(n_head)]
        )

    def projection(rows, weight):
        return dot(weight, rows, ((0,), (1,)))

    def norm(rows):
        x = rows.astype(f32)
        return (
            x * lax.rsqrt(jnp.mean(x * x, axis=-1, keepdims=True) + norm_eps) * gain.astype(f32)
        ).astype(bf16)

    def ordered(value, *earlier):
        return lax.optimization_barrier((value,) + earlier)[0]

    others = [turn(tokens[0], step) for step in range(1, n_head)]

    page_ids = jnp.arange(max_pages, dtype=jnp.int32)
    filled = jnp.clip(cached_length[0] - page_ids * PAGE, 0, PAGE)
    slot_of = page_keeper[0] * lanes + page_slot_index[0]
    keeper = (plane ^ jnp.arange(planes, dtype=jnp.int32))[:, None] * GROUP + (
        place ^ jnp.arange(GROUP, dtype=jnp.int32)
    )
    slot_ids = keeper[:, :, None] * lanes + jnp.arange(lanes, dtype=jnp.int32)
    slot_fill = jnp.sum(
        jnp.where(slot_of == slot_ids[..., None], filled, 0), axis=-1
    )

    offsets = list(range(2, planes)) + [1, 0]
    core = place % 2
    cache = cache_page_slots[0]
    heads = cols // HD
    cache = cache.reshape(devices, span, 2, heads, HD).transpose(0, 1, 3, 2, 4)
    cache = cache.reshape(devices, span * heads * 2, HD)

    hands = []
    for d in offsets:
        start = (plane ^ d) * GROUP + ((place // 2) ^ 1) * 2
        hands.append([start, start + 1])
    for k in (1, 0):
        hands.append([z * GROUP + (place ^ k) for z in range(planes)])
    pieces = dict(zip(offsets, deal(cache, hands[:1], gain)))

    def with_fill(value, d):
        rows = jnp.concatenate([slot_fill[d], slot_fill[d ^ 1]], axis=0)
        rows = jnp.pad(rows, ((0, TAIL - 2 * GROUP), (0, value.shape[1] - lanes)))
        return jnp.concatenate([value, rows.astype(bf16)], axis=0)

    across, sibling, far_here, far_rest = {}, {}, {}, {}

    def pass_on(d, *earlier):
        piece = ordered(across[d], *earlier)
        sibling[d] = swap(lax.dynamic_index_in_dim(piece, 1 - core, 0), 1)

    first, second = offsets[:2]
    across[first] = swap(pieces[first], 2)
    flat = ordered(projection_weight, pieces[first]).reshape(width, 4 * cols)
    normed_here = norm(tokens[0])
    query_here = projection(normed_here, flat[:, :cols]).astype(bf16)
    far_here[first] = swap(with_fill(query_here, first), first * GROUP)
    far_here[1] = swap(with_fill(query_here, 1), GROUP)
    *rest, column, own = deal(cache, hands[1:], query_here)
    pieces |= zip(offsets[1:], rest)
    beside = swap(ordered(column, far_here[1]), 1)
    across[second] = swap(pieces[second], 2)
    normed_rest = norm(ordered(jnp.concatenate(others, axis=0), query_here))
    query_rest = projection(normed_rest, flat[:, :cols]).astype(bf16)
    far_rest[first] = swap(query_rest, first * GROUP)
    projected = projection(
        jnp.concatenate([normed_here, normed_rest], axis=0), ordered(flat, query_rest)[:, cols:]
    )
    queries = jnp.concatenate([query_here, query_rest], axis=1)
    own_keys = projected[:cols].astype(bf16)
    own_values = projected[cols : 2 * cols].astype(bf16)
    far_rest[1] = swap(ordered(query_rest, far_here[1], own_values), GROUP)
    sent = [far_here[first], far_here[1], far_rest[first], far_rest[1]]

    att, lse = own_attention(side, shard_tokens, queries, own_keys, own_values, persist)
    near, far = [(att, lse)], []
    pass_on(first, lse, *sent)
    asked = {}
    done = lse
    fill_here = jnp.pad(slot_fill[0], ((0, TAIL - GROUP), (0, HD - lanes))).astype(bf16)
    for i, d in enumerate(offsets):
        if i and d:
            pass_on(d, att)
        if d == 1 or (d and d % 2 == 0):
            if d not in far_here:
                far_here[d] = swap(with_fill(ordered(query_here, done), d), d * GROUP)
                far_rest[d] = swap(ordered(query_rest, done), d * GROUP)
            here_rows = jnp.pad(ordered(far_here[d], *sent), ((0, TAIL), (0, 0)))
            rest_rows = jnp.pad(ordered(far_rest[d], *sent), ((0, 2 * TAIL), (0, 0)))
            asked[d] = jnp.concatenate([here_rows, rest_rows], axis=1)
            if d > 1:
                asked[d ^ 1] = swap(asked[d], GROUP)
        if i + 2 < len(offsets):
            earlier = sent if i == 0 else [done]
            if i == 0:
                across[offsets[i + 2]] = swap(ordered(pieces[offsets[i + 2]], across[d], *earlier), 2)
        kvs = [own, beside, across[d], sibling.get(d)]
        at = [plane ^ d, plane ^ d, core, jnp.zeros_like(core)]
        if d:
            if d == 1:
                done = ordered(done, far[0])
            row = GROUP * (d % 2 if d > 1 else 0)
            (done,) = cache_attention(
                asked[d], cols, asked[d], row, kvs, at, True, done, LAST if d == 1 else COST
            )
            att = done
            far.append(swap(done, d * GROUP))
            if 0 < i < len(offsets) - 2:
                across[offsets[i + 2]] = swap(ordered(pieces[offsets[i + 2]], done), 2)
        else:
            for part in (slice(0, 2), slice(2, 3), slice(3, 4)):
                pair = cache_attention(
                    queries, cols, fill_here, part.start, kvs[part], at[part], False, done
                )
                near.append(pair)
                done = pair[1]
                if part.start == 0:
                    pass_on(d, done)
                    kvs[3] = sibling[d]
        if i == 0:
            memory_read, new_state = memory_pass(
                side, shard_tokens, retention, momentum, memory_step_scale, halving_updates,
                done, queries, own_keys, own_values, memory_state[:, 0],
            )
            done = memory_read
        if d == 1:
            late = across[d]
    head_out = merge(near, far, projected, memory_read)

    layer = jnp.zeros((shard_tokens, width), f32)
    for step in range(n_head):
        away = (n_head - step) % n_head
        part = head_out[:, away * shard_tokens : (away + 1) * shard_tokens]
        weight = output_weight
        if step:
            part = turn(part, step)
            weight = turn(ordered(output_weight, late), step)
        layer = layer + dot(part, weight, ((0,), (0,))).astype(bf16).astype(f32)
    return (layer.astype(bf16)[None], new_state[:, None])


def solution(mesh):
    in_specs = (
        P("req", "head", None),
        P(),
        P(None, None, "head"),
        P("head", None),
        P(None, None, "head"),
        P("req", None, None, None, "head"),
        P("req"),
        P("req", None),
        P("req", None),
        P(None, "req", "head", None, None),
        P("req", "head"),
        P("req", "head"),
        P("req", "head"),
        P("req", None),
    )
    out_specs = (P("req", "head", None), P(None, "req", "head", None, None))
    return jax.shard_map(shards, mesh=mesh, in_specs=in_specs, out_specs=out_specs, check_vma=False)
```

time: 163 us -> 135 us (0.83)
  the two profiles are of different devices: /device:TPU:0 before, /device:TPU:2 now
where the time goes in v1:
time: 135 us
  Pallas kernels  47.5 us (35%)
  waiting for transfers between devices  46.7 us (35%)
  starting transfers between devices  17.3 us (13%)
  other arithmetic  9.06 us (7%)
  matrix products  6.94 us (5%)
  local copies, waits for them, and re-layouts  5.41 us (4%)
  between operations  1.8 us (1%)
    ppermute x17, waiting for transfers between devices, swap(): return lax.ppermute(value, 'req', [(i, i ^ step) for i in range(devices)])  39.3 us
    pallas_call x6, Pallas kernels, cache_attention(): pl.pallas_call(functools.partial(cache_kernel, (span, heads, count, fill_...  27 us
    ppermute x17, starting transfers between devices, swap(): return lax.ppermute(value, 'req', [(i, i ^ step) for i in range(devices)])  15.1 us
    pallas_call x2, Pallas kernels, deal(): pl.pallas_call(functools.partial(deal_kernel, counts), out_shape=[jax.Sha...  9.91 us
    ppermute x3, waiting for transfers between devices, turn(): lax.ppermute(value, 'head', [(i, (i - step) % n_head) for i in range(n_he...  7.37 us
    dot_general x5, matrix products, dot(): lax.dot_general(left, right, (contract, ((), ())), precision=precision, p...  6.94 us
    pallas_call x1, Pallas kernels, memory_pass(): pl.pallas_call(functools.partial(memory_kernel, count), out_shape=(jax.Sh...  6 us
    pallas_call x1, Pallas kernels, own_attention(): pl.pallas_call(functools.partial(own_kernel, shard, tokens // shard), out...  3.29 us
  transfers between devices with their start and end apart: 20, of which 8 were waited for; matrix products, arithmetic and copies ran while one was open for 14% of the time, Pallas kernels for 35%

profile of v1, /device:TPU:2, one launch (start us, length us, event | category | flops | bytes accessed | tf_op | source)
XLA Modules:
  0.0 134.7 jit_solution(888216639220234198)
XLA Ops:
  0.6 1.6 %collective-permute-start = (bf16[256,1024]{1,0:T(8,128)(2,1)}, bf16[256,1024]{1,0:T(8,128)(2,1)S(1)}, u32[]{:S(2)}, u32[]{:S(2)}) collective-permute-start(bf16[256,1024]{1,0:T(8,128)(2,1)} %bitcast.62), channel_id=1, source_target_pairs={{0,1},{1,0},{2,3},{3,2},{4,5},{5,4},{6,7},{7,6},{8,9},{9,8},{10,11... | collective-permute-start | bytes 1572872 | tf_op jit(solution)/shard_map/ppermute | solution.py:388
  2.2 1.3 fusion.11
  6.7 3.2 %shard_map.149 = bf16[2,2048,128]{2,1,0:T(8,128)(2,1)} custom-call(s32[2]{0:T(128)} %pad_add_fusion.3.at_ref, bf16[16,2048,128]{2,1,0:T(8,128)(2,1)} %bitcast.56, bf16[1024]{0:T(1024)(128)(2,1)} %after_ref.1), custom_call_target="tpu_custom_call" | custom-call | flops 1 | bytes 1 | tf_op jit(solution)/shard_map/pallas_call | solution.py:56
  10.0 1.4 %copy.23 = bf16[128,8,4,512]{3,1,2,0:T(8,128)(2,1)S(1)} copy(bf16[128,8,4,512]{3,2,1,0:T(4,128)(2,1)S(1)} %bitcast.58) | data formatting | bytes 8388608
  12.2 1.2 pad_maximum_fusion.2
  13.7 1.6 %collective-permute-start.2 = (bf16[528,256]{1,0:T(8,128)(2,1)S(1)}, bf16[528,256]{1,0:T(8,128)(2,1)S(1)}, u32[]{:S(2)}, u32[]{:S(2)}) collective-permute-start(bf16[528,256]{1,0:T(8,128)(2,1)S(1)} %get-tuple-element.72), channel_id=1, source_target_pairs={{0,8},{2,10},{4,12},{6,14},{8,0},{10,2},{12,4},{14,6},{16,24},{18,... | collective-permute-start | bytes 811016 | tf_op jit(solution)/shard_map/ppermute | solution.py:385
  16.4 2.6 %collective-permute-start.1 = (bf16[528,256]{1,0:T(8,128)(2,1)}, bf16[528,256]{1,0:T(8,128)(2,1)}, u32[]{:S(2)}, u32[]{:S(2)}) collective-permute-start(bf16[528,256]{1,0:T(8,128)(2,1)} %get-tuple-element.73), channel_id=1, source_target_pairs={{0,16},{2,18},{4,20},{6,22},{8,24},{10,26},{12,28},{14,30},{16,0},... | collective-permute-start | bytes 811016 | tf_op jit(solution)/shard_map/ppermute | solution.py:385
  19.0 6.7 %shard_map.151 = (bf16[2,2048,128]{2,1,0:T(8,128)(2,1)}, bf16[2,2048,128]{2,1,0:T(8,128)(2,1)}, bf16[2,2048,128]{2,1,0:T(8,128)(2,1)}, bf16[4,2048,128]{2,1,0:T(8,128)(2,1)}, bf16[4,2048,128]{2,1,0:T(8,128)(2,1)}) custom-call(s32[14]{0:T(128)} %stack.114.at_ref, bf16[16,2048,128]{2,1,0:T(8,128)(2,1)} %bitcast.57, bf16[512,256]{1,0:T(8,128)(2,1)} %copy-done.11), custom_call_target="tpu_custom_call" | custom-call | flops 1 | bytes 1 | tf_op jit(solution)/shard_map/pallas_call | solution.py:56
  25.7 1.6 %collective-permute-start.9 = (bf16[2,2048,128]{2,1,0:T(8,128)(2,1)}, bf16[2,2048,128]{2,1,0:T(8,128)(2,1)}, u32[]{:S(2)}, u32[]{:S(2)}) collective-permute-start(bf16[2,2048,128]{2,1,0:T(8,128)(2,1)} %get-tuple-element.47), channel_id=1, source_target_pairs={{0,4},{2,6},{4,0},{6,2},{8,12},{10,14},{12,8},{14,10},{16,20},{18,... | collective-permute-start | bytes 3145736 | tf_op jit(solution)/shard_map/ppermute | solution.py:385
  28.4 1.2 convolution_convert_fusion.2
  30.2 3.5 %fusion.39 = (bf16[1536,512]{1,0:T(8,128)(2,1)S(1)}, f32[1536,512]{1,0:T(8,128)}) fusion(bf16[256,1024]{1,0:T(8,128)(2,1)S(1)} %fusion.16, bf16[256,1024]{1,0:T(8,128)(2,1)S(1)} %copy-done.16, bf16[1024,2048]{1,0:T(8,128)(2,1)S(1)} %bitcast.61), kind=kOutput, calls=%fused_computation.76 | convolution fusion | flops 1613496320 | bytes 8912896 | tf_op jit(solution)/shard_map/dot_general | solution.py:30
  33.8 1.4 %collective-permute-start.4 = (bf16[512,256]{1,0:T(8,128)(2,1)}, bf16[512,256]{1,0:T(8,128)(2,1)}, u32[]{:S(2)}, u32[]{:S(2)}) collective-permute-start(bf16[512,256]{1,0:T(8,128)(2,1)} %convolution_convert_fusion.2), channel_id=1, source_target_pairs={{0,8},{2,10},{4,12},{6,14},{8,0},{10,2},{12,4},{14,6},{16,24},{18,... | collective-permute-start | bytes 786440 | tf_op jit(solution)/shard_map/ppermute | solution.py:385
  36.3 3.3 %shard_map.150 = (f32[4,128,512]{2,1,0:T(8,128)S(1)}, f32[4,1,512]{2,1,0:T(1,128)S(1)}) custom-call(s32[1]{0:T(128)} %bitcast.side_ref, bf16[512,512]{1,0:T(8,128)(2,1)S(1)} %pad_maximum_fusion.q_ref, bf16[512,512]{1,0:T(8,128)(2,1)S(1)} %get-tuple-element.71.k_ref, bf16[512,512]{1,0:T(8,128)(2,1)S(1)} %get-tuple-element.70.v_ref, ...), custom_call_target="tpu_custom_call" | custom-call | flops 1 | bytes 1 | tf_op jit(solution)/shard_map/pallas_call | solution.py:217
  39.6 5.5 %collective-permute-done.3 = bf16[512,256]{1,0:T(8,128)(2,1)} collective-permute-done((bf16[512,256]{1,0:T(8,128)(2,1)}, bf16[512,256]{1,0:T(8,128)(2,1)}, u32[]{:S(2)}, u32[]{:S(2)}) %collective-permute-start.3) | collective-permute-done | bytes 262176 | tf_op jit(solution)/shard_map/ppermute | solution.py:385
  45.1 3.0 %collective-permute-done.4 = bf16[512,256]{1,0:T(8,128)(2,1)} collective-permute-done((bf16[512,256]{1,0:T(8,128)(2,1)}, bf16[512,256]{1,0:T(8,128)(2,1)}, u32[]{:S(2)}, u32[]{:S(2)}) %collective-permute-start.4) | collective-permute-done | bytes 262176 | tf_op jit(solution)/shard_map/ppermute | solution.py:385
  48.1 1.1 constant_dynamic-slice_fusion.3
  51.2 6.4 %shard_map.152.after_ref = bf16[528,512]{1,0:T(8,128)(2,1)S(1)} custom-call(s32[4]{0:T(128)S(1)} %pad_add_fusion.at_ref, f32[4,1,512]{2,1,0:T(1,128)S(1)} %get-tuple-element.38.after_ref.refs_1_, bf16[544,512]{1,0:T(8,128)(2,1)S(1)} %fusion.22.q_ref.fill_ref, bf16[544,512]{1,0:T(8,128)(2,1)S(1)} %fusion.22.q_ref.fill_ref, bf16[4,2048,128]{2,1,0:T(8,128)(2,1)S(1)} %copy-done, ...), custom_call_target="tpu_custom_call" | custom-call | flops 1 | bytes 1 | tf_op jit(solution)/shard_map/pallas_call | solution.py:162
  57.6 6.5 %collective-permute-done.9.refs_2_ = bf16[2,2048,128]{2,1,0:T(8,128)(2,1)} collective-permute-done((bf16[2,2048,128]{2,1,0:T(8,128)(2,1)}, bf16[2,2048,128]{2,1,0:T(8,128)(2,1)}, u32[]{:S(2)}, u32[]{:S(2)}) %collective-permute-start.9) | collective-permute-done | bytes 1048608 | tf_op jit(solution)/shard_map/ppermute | solution.py:385
  65.4 2.6 %collective-permute-start.11 = (bf16[528,512]{1,0:T(8,128)(2,1)S(1)}, bf16[528,512]{1,0:T(8,128)(2,1)S(1)}, u32[]{:S(2)}, u32[]{:S(2)}) collective-permute-start(bf16[528,512]{1,0:T(8,128)(2,1)S(1)} %shard_map.152.after_ref), channel_id=1, source_target_pairs={{0,16},{2,18},{4,20},{6,22},{8,24},{10,26},{12,28},{14,30},{16,0},... | collective-permute-start | bytes 1622024 | tf_op jit(solution)/shard_map/ppermute | solution.py:385
  68.0 6.0 %shard_map.153 = (f32[512,512]{1,0:T(8,128)S(1)}, f32[2,4,128,128]{3,2,1,0:T(8,128)}) custom-call(s32[1]{0:T(128)} %bitcast.side_ref, f32[1,4]{1,0:T(1,128)S(1)} %copy-done.4, f32[1,4]{1,0:T(1,128)S(1)} %copy-done.5, f32[1,4]{1,0:T(1,128)S(1)} %copy-done.6, s32[1,8]{1,0:T(1,128)S(1)} %copy-done.7, bf16[528,512]{1,0:T(8,128)(2,1)S(1)} %shard_map.152.after_ref, ...), custom_call_target="tpu_custom_call" | custom-call | flops 1 | bytes 1 | tf_op jit(solution)/shard_map/pallas_call | solution.py:293
  74.0 6.4 %shard_map.154.after_ref = bf16[528,512]{1,0:T(8,128)(2,1)S(1)} custom-call(s32[4]{0:T(128)S(1)} %pad_add_fusion.1.at_ref, f32[512,512]{1,0:T(8,128)S(1)} %get-tuple-element.46.after_ref.refs_15_, bf16[544,512]{1,0:T(8,128)(2,1)S(1)} %collective-permute-done.8.q_ref.fill_ref, bf16[544,512]{1,0:T(8,128)(2,1)S(1)} %collective-permute-done.8.q_ref.fill_ref, ...), custom_call_target="tpu_custom_call" | custom-call | flops 1 | bytes 1 | tf_op jit(solution)/shard_map/pallas_call | solution.py:162
  80.4 4.3 %collective-permute-done.12.refs_2_ = bf16[2,2048,128]{2,1,0:T(8,128)(2,1)S(1)} collective-permute-done((bf16[2,2048,128]{2,1,0:T(8,128)(2,1)S(1)}, bf16[2,2048,128]{2,1,0:T(8,128)(2,1)S(1)}, u32[]{:S(2)}, u32[]{:S(2)}) %collective-permute-start.12) | collective-permute-done | bytes 1048608 | tf_op jit(solution)/shard_map/ppermute | solution.py:385
  87.2 2.5 %collective-permute-start.16 = (bf16[528,512]{1,0:T(8,128)(2,1)S(1)}, bf16[528,512]{1,0:T(8,128)(2,1)S(1)}, u32[]{:S(2)}, u32[]{:S(2)}) collective-permute-start(bf16[528,512]{1,0:T(8,128)(2,1)S(1)} %shard_map.154.after_ref), channel_id=1, source_target_pairs={{0,24},{2,26},{4,28},{6,30},{8,16},{10,18},{12,20},{14,22},{16,8},... | collective-permute-start | bytes 1622024 | tf_op jit(solution)/shard_map/ppermute | solution.py:385
  89.7 14.4 %collective-permute-done.11.refs_8_.refs_9_ = bf16[528,512]{1,0:T(8,128)(2,1)S(1)} collective-permute-done((bf16[528,512]{1,0:T(8,128)(2,1)S(1)}, bf16[528,512]{1,0:T(8,128)(2,1)S(1)}, u32[]{:S(2)}, u32[]{:S(2)}) %collective-permute-start.11) | collective-permute-done | bytes 540704 | tf_op jit(solution)/shard_map/ppermute | solution.py:385
  104.0 5.8 %shard_map.155.after_ref = bf16[528,512]{1,0:T(8,128)(2,1)S(1)} custom-call(s32[4]{0:T(128)S(1)} %pad_add_fusion.2.at_ref, bf16[528,512]{1,0:T(8,128)(2,1)S(1)} %shard_map.154.after_ref, bf16[544,512]{1,0:T(8,128)(2,1)S(1)} %fusion.23.q_ref.fill_ref, bf16[544,512]{1,0:T(8,128)(2,1)S(1)} %fusion.23.q_ref.fill_ref, bf16[4,2048,128]{2,1,0:T(8,128)(2,1)S(1)} %copy-done, ...), custom_call_target="tpu_custom_call" | custom-call | flops 6000000000 | bytes 1 | tf_op jit(solution)/shard_map/pallas_call | solution.py:162
  110.1 3.9 %shard_map.156 = (f32[4,128,512]{2,1,0:T(8,128)S(1)}, f32[4,1,512]{2,1,0:T(1,128)S(1)}) custom-call(s32[2]{0:T(128)S(1)} %pad_add_fusion.4.at_ref, bf16[528,512]{1,0:T(8,128)(2,1)S(1)} %shard_map.155.after_ref, bf16[512,512]{1,0:T(8,128)(2,1)S(1)} %pad_maximum_fusion.q_ref, bf16[16,128]{1,0:T(8,128)(2,1)S(1)} %pad.34.fill_ref, ...), custom_call_target="tpu_custom_call" | custom-call | flops 1 | bytes 1 | tf_op jit(solution)/shard_map/pallas_call | solution.py:162
  114.1 2.3 %shard_map.157 = (f32[4,128,512]{2,1,0:T(8,128)S(1)}, f32[4,1,512]{2,1,0:T(1,128)S(1)}) custom-call(s32[1]{0:T(128)} %bitcast.9.at_ref, f32[4,1,512]{2,1,0:T(1,128)S(1)} %get-tuple-element.56.after_ref.refs_3_, bf16[512,512]{1,0:T(8,128)(2,1)S(1)} %pad_maximum_fusion.q_ref, bf16[16,128]{1,0:T(8,128)(2,1)S(1)} %pad.34.fill_ref, ...), custom_call_target="tpu_custom_call" | custom-call | flops 1 | bytes 1 | tf_op jit(solution)/shard_map/pallas_call | solution.py:162
  116.4 2.3 %shard_map.158 = (f32[4,128,512]{2,1,0:T(8,128)S(1)}, f32[4,1,512]{2,1,0:T(1,128)S(1)}) custom-call(s32[1]{0:T(128)} %constant.88.clone.1.at_ref, f32[4,1,512]{2,1,0:T(1,128)S(1)} %get-tuple-element.60.after_ref.refs_5_, bf16[512,512]{1,0:T(8,128)(2,1)S(1)} %pad_maximum_fusion.q_ref, bf16[16,128]{1,0:T(8,128)(2,1)S(1)} %pad.34.fill_ref, ...), custom_call_target="tpu_custom_call" | custom-call | flops 1 | bytes 1 | tf_op jit(solution)/shard_map/pallas_call | solution.py:162
  118.7 5.5 %collective-permute-done.17.refs_12_.refs_13_ = bf16[528,512]{1,0:T(8,128)(2,1)S(1)} collective-permute-done((bf16[528,512]{1,0:T(8,128)(2,1)S(1)}, bf16[528,512]{1,0:T(8,128)(2,1)S(1)}, u32[]{:S(2)}, u32[]{:S(2)}) %collective-permute-start.17) | collective-permute-done | bytes 540704 | tf_op jit(solution)/shard_map/ppermute | solution.py:385
  124.2 1.3 shard_map.159
  125.6 7.4 %collective-permute-done.18 = bf16[512,256]{1,0:T(8,128)(2,1)S(1)} collective-permute-done((bf16[512,256]{1,0:T(8,128)(2,1)S(1)}, bf16[512,256]{1,0:T(8,128)(2,1)S(1)}, u32[]{:S(2)}, u32[]{:S(2)}) %collective-permute-start.18) | collective-permute-done | bytes 262176 | tf_op jit(solution)/shard_map/ppermute | solution.py:388
  133.4 1.3 fusion.6
  (102 shorter events, 14.1 us)
Async XLA Ops:
  0.6 27.4 %collective-permute-start = (bf16[256,1024]{1,0:T(8,128)(2,1)}, bf16[256,1024]{1,0:T(8,128)(2,1)S(1)}, u32[]{:S(2)}, u32[]{:S(2)}) collective-permute-start(bf16[256,1024]{1,0:T(8,128)(2,1)} %bitcast.62), channel_id=1, source_target_pairs={{0,1},{1,0},{2,3},{3,2},{4,5},{5,4},{6,7},{7,6},{8,9},{9,8},{10,11... | collective-permute-start | bytes 1572872 | tf_op jit(solution)/shard_map/ppermute | solution.py:388
  12.2 6.8 %copy-start.11 = (bf16[512,256]{1,0:T(8,128)(2,1)}, bf16[512,256]{1,0:T(8,128)(2,1)S(1)}, u32[]{:S(2)}) copy-start(bf16[512,256]{1,0:T(8,128)(2,1)S(1)} %convolution_convert_fusion.3.after_ref) | copy-start | bytes 786436
  13.7 13.6 %collective-permute-start.2 = (bf16[528,256]{1,0:T(8,128)(2,1)S(1)}, bf16[528,256]{1,0:T(8,128)(2,1)S(1)}, u32[]{:S(2)}, u32[]{:S(2)}) collective-permute-start(bf16[528,256]{1,0:T(8,128)(2,1)S(1)} %get-tuple-element.72), channel_id=1, source_target_pairs={{0,8},{2,10},{4,12},{6,14},{8,0},{10,2},{12,4},{14,6},{16,24},{18,... | collective-permute-start | bytes 811016 | tf_op jit(solution)/shard_map/ppermute | solution.py:385
  15.2 32.9 %collective-permute-start.6 = (bf16[2,2048,128]{2,1,0:T(8,128)(2,1)}, bf16[2,2048,128]{2,1,0:T(8,128)(2,1)}, u32[]{:S(2)}, u32[]{:S(2)}) collective-permute-start(bf16[2,2048,128]{2,1,0:T(8,128)(2,1)} %shard_map.149), channel_id=1, source_target_pairs={{0,4},{2,6},{4,0},{6,2},{8,12},{10,14},{12,8},{14,10},{16,20},{18,... | collective-permute-start | bytes 3145736 | tf_op jit(solution)/shard_map/ppermute | solution.py:385
  16.4 12.0 %copy-start.10 = (bf16[128,8,4,512]{3,1,2,0:T(8,128)(2,1)S(1)}, bf16[128,8,4,512]{3,1,2,0:T(8,128)(2,1)}, u32[]{:S(2)}) copy-start(bf16[128,8,4,512]{3,1,2,0:T(8,128)(2,1)} %copy-done.9) | copy-start | bytes 12582916
  16.4 17.3 %collective-permute-start.1 = (bf16[528,256]{1,0:T(8,128)(2,1)}, bf16[528,256]{1,0:T(8,128)(2,1)}, u32[]{:S(2)}, u32[]{:S(2)}) collective-permute-start(bf16[528,256]{1,0:T(8,128)(2,1)} %get-tuple-element.73), channel_id=1, source_target_pairs={{0,16},{2,18},{4,20},{6,22},{8,24},{10,26},{12,28},{14,30},{16,0},... | collective-permute-start | bytes 811016 | tf_op jit(solution)/shard_map/ppermute | solution.py:385
  25.7 38.4 %collective-permute-start.9 = (bf16[2,2048,128]{2,1,0:T(8,128)(2,1)}, bf16[2,2048,128]{2,1,0:T(8,128)(2,1)}, u32[]{:S(2)}, u32[]{:S(2)}) collective-permute-start(bf16[2,2048,128]{2,1,0:T(8,128)(2,1)} %get-tuple-element.47), channel_id=1, source_target_pairs={{0,4},{2,6},{4,0},{6,2},{8,12},{10,14},{12,8},{14,10},{16,20},{18,... | collective-permute-start | bytes 3145736 | tf_op jit(solution)/shard_map/ppermute | solution.py:385
  28.0 23.2 %collective-permute-start.5 = (bf16[4,2048,128]{2,1,0:T(8,128)(2,1)}, bf16[4,2048,128]{2,1,0:T(8,128)(2,1)S(1)}, u32[]{:S(2)}, u32[]{:S(2)}) collective-permute-start(bf16[4,2048,128]{2,1,0:T(8,128)(2,1)} %get-tuple-element.44), channel_id=1, source_target_pairs={{0,2},{2,0},{4,6},{6,4},{8,10},{10,8},{12,14},{14,12},{16,18},{18,... | collective-permute-start | bytes 6291464 | tf_op jit(solution)/shard_map/ppermute | solution.py:385
  29.6 15.5 %collective-permute-start.3 = (bf16[512,256]{1,0:T(8,128)(2,1)}, bf16[512,256]{1,0:T(8,128)(2,1)}, u32[]{:S(2)}, u32[]{:S(2)}) collective-permute-start(bf16[512,256]{1,0:T(8,128)(2,1)} %convolution_convert_fusion.2), channel_id=1, source_target_pairs={{0,16},{2,18},{4,20},{6,22},{8,24},{10,26},{12,28},{14,30},{16,0},... | collective-permute-start | bytes 786440 | tf_op jit(solution)/shard_map/ppermute | solution.py:385
  33.8 14.3 %collective-permute-start.4 = (bf16[512,256]{1,0:T(8,128)(2,1)}, bf16[512,256]{1,0:T(8,128)(2,1)}, u32[]{:S(2)}, u32[]{:S(2)}) collective-permute-start(bf16[512,256]{1,0:T(8,128)(2,1)} %convolution_convert_fusion.2), channel_id=1, source_target_pairs={{0,8},{2,10},{4,12},{6,14},{8,0},{10,2},{12,4},{14,6},{16,24},{18,... | collective-permute-start | bytes 786440 | tf_op jit(solution)/shard_map/ppermute | solution.py:385
  35.2 14.1 %copy-start.20 = (bf16[2,2048,128]{2,1,0:T(8,128)(2,1)S(1)}, bf16[2,2048,128]{2,1,0:T(8,128)(2,1)}, u32[]{:S(2)}) copy-start(bf16[2,2048,128]{2,1,0:T(8,128)(2,1)} %get-tuple-element.53) | copy-start | bytes 3145732
  36.3 14.9 %copy-start = (bf16[4,2048,128]{2,1,0:T(8,128)(2,1)S(1)}, bf16[4,2048,128]{2,1,0:T(8,128)(2,1)}, u32[]{:S(2)}) copy-start(bf16[4,2048,128]{2,1,0:T(8,128)(2,1)} %get-tuple-element.42.refs_0_) | copy-start | bytes 6291460
  49.2 2.0 %collective-permute-start.7 = (bf16[1,2048,128]{2,1,0:T(8,128)(2,1)S(1)}, bf16[1,2048,128]{2,1,0:T(8,128)(2,1)S(1)}, u32[]{:S(2)}, u32[]{:S(2)}) collective-permute-start(bf16[1,2048,128]{2,1,0:T(8,128)(2,1)S(1)} %constant_dynamic-slice_fusion.3), channel_id=1, source_target_pairs={{0,2},{2,0},{4,6},{6,4},{8,10},{10,8},{12,14},{14,12},{16,18},{18,... | collective-permute-start | bytes 1572872 | tf_op jit(solution)/shard_map/ppermute | solution.py:385
  49.3 35.5 %collective-permute-start.12 = (bf16[2,2048,128]{2,1,0:T(8,128)(2,1)S(1)}, bf16[2,2048,128]{2,1,0:T(8,128)(2,1)S(1)}, u32[]{:S(2)}, u32[]{:S(2)}) collective-permute-start(bf16[2,2048,128]{2,1,0:T(8,128)(2,1)S(1)} %copy-done.20), channel_id=1, source_target_pairs={{0,4},{2,6},{4,0},{6,2},{8,12},{10,14},{12,8},{14,10},{16,20},{18,... | collective-permute-start | bytes 3145736 | tf_op jit(solution)/shard_map/ppermute | solution.py:385
  51.0 23.0 %collective-permute-start.8 = (bf16[544,512]{1,0:T(8,128)(2,1)S(1)}, bf16[544,512]{1,0:T(8,128)(2,1)S(1)}, u32[]{:S(2)}, u32[]{:S(2)}) collective-permute-start(bf16[544,512]{1,0:T(8,128)(2,1)S(1)} %fusion.22.q_ref.fill_ref), channel_id=1, source_target_pairs={{0,8},{2,10},{4,12},{6,14},{8,0},{10,2},{12,4},{14,6},{16,24},{18,... | collective-permute-start | bytes 1671176 | tf_op jit(solution)/shard_map/ppermute | solution.py:385
  51.2 16.8 %copy-start.2 = (f32[2,1,4,128,128]{4,3,2,1,0:T(8,128)S(1)}, f32[2,1,4,128,128]{4,3,2,1,0:T(8,128)}, u32[]{:S(2)}) copy-start(f32[2,1,4,128,128]{4,3,2,1,0:T(8,128)} %param.23) | copy-start | bytes 1572868
  51.2 16.8 %copy-start.4 = (f32[1,4]{1,0:T(1,128)S(1)}, f32[1,4]{1,0:T(1,128)}, u32[]{:S(2)}) copy-start(f32[1,4]{1,0:T(1,128)} %retention_ref.1) | copy-start | bytes 52
  51.2 16.8 %copy-start.5 = (f32[1,4]{1,0:T(1,128)S(1)}, f32[1,4]{1,0:T(1,128)}, u32[]{:S(2)}) copy-start(f32[1,4]{1,0:T(1,128)} %momentum_ref.1) | copy-start | bytes 52
  51.2 16.8 %copy-start.6 = (f32[1,4]{1,0:T(1,128)S(1)}, f32[1,4]{1,0:T(1,128)}, u32[]{:S(2)}) copy-start(f32[1,4]{1,0:T(1,128)} %step_ref.1) | copy-start | bytes 52
  51.2 16.8 %copy-start.7 = (s32[1,8]{1,0:T(1,128)S(1)}, s32[1,8]{1,0:T(1,128)}, u32[]{:S(2)}) copy-start(s32[1,8]{1,0:T(1,128)} %halving_ref.1) | copy-start | bytes 100
  65.2 8.8 %collective-permute-start.10 = (bf16[1,2048,128]{2,1,0:T(8,128)(2,1)S(1)}, bf16[1,2048,128]{2,1,0:T(8,128)(2,1)S(1)}, u32[]{:S(2)}, u32[]{:S(2)}) collective-permute-start(bf16[1,2048,128]{2,1,0:T(8,128)(2,1)S(1)} %constant_dynamic-slice_fusion.2), channel_id=1, source_target_pairs={{0,2},{2,0},{4,6},{6,4},{8,10},{10,8},{12,14},{14,12},{16,18},{18,... | collective-permute-start | bytes 1572872 | tf_op jit(solution)/shard_map/ppermute | solution.py:385
  65.4 38.7 %collective-permute-start.11 = (bf16[528,512]{1,0:T(8,128)(2,1)S(1)}, bf16[528,512]{1,0:T(8,128)(2,1)S(1)}, u32[]{:S(2)}, u32[]{:S(2)}) collective-permute-start(bf16[528,512]{1,0:T(8,128)(2,1)S(1)} %shard_map.152.after_ref), channel_id=1, source_target_pairs={{0,16},{2,18},{4,20},{6,22},{8,24},{10,26},{12,28},{14,30},{16,0},... | collective-permute-start | bytes 1622024 | tf_op jit(solution)/shard_map/ppermute | solution.py:385
  74.0 10.9 %copy-start.19 = (bf16[2,2048,128]{2,1,0:T(8,128)(2,1)S(1)}, bf16[2,2048,128]{2,1,0:T(8,128)(2,1)}, u32[]{:S(2)}) copy-start(bf16[2,2048,128]{2,1,0:T(8,128)(2,1)} %get-tuple-element.58) | copy-start | bytes 3145732
  74.0 11.6 %copy-start.18 = (bf16[528,256]{1,0:T(8,128)(2,1)S(1)}, bf16[528,256]{1,0:T(8,128)(2,1)}, u32[]{:S(2)}) copy-start(bf16[528,256]{1,0:T(8,128)(2,1)} %copy-done.17) | copy-start | bytes 811012
  84.8 19.3 %collective-permute-start.13 = (bf16[1,2048,128]{2,1,0:T(8,128)(2,1)S(1)}, bf16[1,2048,128]{2,1,0:T(8,128)(2,1)S(1)}, u32[]{:S(2)}, u32[]{:S(2)}) collective-permute-start(bf16[1,2048,128]{2,1,0:T(8,128)(2,1)S(1)} %constant_dynamic-slice_fusion.1), channel_id=1, source_target_pairs={{0,2},{2,0},{4,6},{6,4},{8,10},{10,8},{12,14},{14,12},{16,18},{18,... | collective-permute-start | bytes 1572872 | tf_op jit(solution)/shard_map/ppermute | solution.py:385
  84.9 29.1 %collective-permute-start.14 = (bf16[2,2048,128]{2,1,0:T(8,128)(2,1)S(1)}, bf16[2,2048,128]{2,1,0:T(8,128)(2,1)S(1)}, u32[]{:S(2)}, u32[]{:S(2)}) collective-permute-start(bf16[2,2048,128]{2,1,0:T(8,128)(2,1)S(1)} %copy-done.19), channel_id=1, source_target_pairs={{0,4},{2,6},{4,0},{6,2},{8,12},{10,14},{12,8},{14,10},{16,20},{18,... | collective-permute-start | bytes 3145736 | tf_op jit(solution)/shard_map/ppermute | solution.py:385
  86.6 38.9 %collective-permute-start.19 = (bf16[512,1024]{1,0:T(8,128)(2,1)S(1)}, bf16[512,1024]{1,0:T(8,128)(2,1)S(1)}, u32[]{:S(2)}, u32[]{:S(2)}) collective-permute-start(bf16[512,1024]{1,0:T(8,128)(2,1)S(1)} %copy-done.14), channel_id=1, source_target_pairs={{0,1},{1,0},{2,3},{3,2},{4,5},{5,4},{6,7},{7,6},{8,9},{9,8},{10,11... | collective-permute-start | bytes 3145736 | tf_op jit(solution)/shard_map/ppermute | solution.py:388
  87.2 31.5 %collective-permute-start.16 = (bf16[528,512]{1,0:T(8,128)(2,1)S(1)}, bf16[528,512]{1,0:T(8,128)(2,1)S(1)}, u32[]{:S(2)}, u32[]{:S(2)}) collective-permute-start(bf16[528,512]{1,0:T(8,128)(2,1)S(1)} %shard_map.154.after_ref), channel_id=1, source_target_pairs={{0,24},{2,26},{4,28},{6,30},{8,16},{10,18},{12,20},{14,22},{16,8},... | collective-permute-start | bytes 1622024 | tf_op jit(solution)/shard_map/ppermute | solution.py:385
  109.9 14.3 %collective-permute-start.17 = (bf16[528,512]{1,0:T(8,128)(2,1)S(1)}, bf16[528,512]{1,0:T(8,128)(2,1)S(1)}, u32[]{:S(2)}, u32[]{:S(2)}) collective-permute-start(bf16[528,512]{1,0:T(8,128)(2,1)S(1)} %shard_map.155.after_ref), channel_id=1, source_target_pairs={{0,8},{2,10},{4,12},{6,14},{8,0},{10,2},{12,4},{14,6},{16,24},{18,... | collective-permute-start | bytes 1622024 | tf_op jit(solution)/shard_map/ppermute | solution.py:385
  113.9 10.2 %copy-start.1 = (f32[1536,512]{1,0:T(8,128)S(1)}, f32[1536,512]{1,0:T(8,128)}, u32[]{:S(2)}) copy-start(f32[1536,512]{1,0:T(8,128)} %get-tuple-element.78.refs_14_) | copy-start | bytes 9437188
  114.0 2.4 %collective-permute-start.15 = (bf16[1,2048,128]{2,1,0:T(8,128)(2,1)S(1)}, bf16[1,2048,128]{2,1,0:T(8,128)(2,1)S(1)}, u32[]{:S(2)}, u32[]{:S(2)}) collective-permute-start(bf16[1,2048,128]{2,1,0:T(8,128)(2,1)S(1)} %constant_dynamic-slice_fusion), channel_id=1, source_target_pairs={{0,2},{2,0},{4,6},{6,4},{8,10},{10,8},{12,14},{14,12},{16,18},{18,... | collective-permute-start | bytes 1572872 | tf_op jit(solution)/shard_map/ppermute | solution.py:385
  125.5 7.5 %collective-permute-start.18 = (bf16[512,256]{1,0:T(8,128)(2,1)S(1)}, bf16[512,256]{1,0:T(8,128)(2,1)S(1)}, u32[]{:S(2)}, u32[]{:S(2)}) collective-permute-start(bf16[512,256]{1,0:T(8,128)(2,1)S(1)} %slice.55), channel_id=1, source_target_pairs={{0,1},{1,0},{2,3},{3,2},{4,5},{5,4},{6,7},{7,6},{8,9},{9,8},{10,11... | collective-permute-start | bytes 786440 | tf_op jit(solution)/shard_map/ppermute | solution.py:388
  (9 other events, 24.3 us)

commit v2 on v1

--- a/solution.py
+++ b/solution.py
@@ -19,7 +19,7 @@
 LOG2E = math.log2(math.e)
 MASKED = -1e30
 LAST = pl.CostEstimate(flops=6 * 10**9, bytes_accessed=1, transcendentals=0)
-VMEM_LIMIT = 32 * 2**20
+VMEM_LIMIT = 16 * 2**20
 TAIL = 16
 f32 = jnp.float32
 bf16 = jnp.bfloat16
@@ -30,6 +30,20 @@
     return lax.dot_general(
         left, right, (contract, ((), ())), precision=precision, preferred_element_type=f32
     )
+
+
+def fence_kernel(*refs):
+    refs[-1][...] = jnp.zeros_like(refs[-1])
+
+
+def fence(*earlier):
+    return pl.pallas_call(
+        fence_kernel,
+        out_shape=jax.ShapeDtypeStruct((8, HD), f32),
+        in_specs=[pl.BlockSpec(memory_space=pl.ANY)] * len(earlier),
+        compiler_params=pltpu.CompilerParams(vmem_limit_bytes=2**20),
+        cost_estimate=LAST,
+    )(*earlier)
 
 
 def deal_kernel(counts, at_ref, from_ref, after_ref, *refs):
@@ -49,7 +63,7 @@
         copy.wait()
 
 
-def deal(source, hands, after):
+def deal(source, hands, after, vmem_limit):
     counts = [len(rows) for rows in hands]
     total = sum(counts)
     anywhere = pl.BlockSpec(memory_space=pl.ANY)
@@ -68,7 +82,7 @@
                 pltpu.SemaphoreType.DMA((total,)),
             ],
         ),
-        compiler_params=pltpu.CompilerParams(vmem_limit_bytes=56 * 2**20),
+        compiler_params=pltpu.CompilerParams(vmem_limit_bytes=vmem_limit),
         cost_estimate=COST,
     )(jnp.stack([row for rows in hands for row in rows]), source, after)
 
@@ -140,7 +154,7 @@
         outs[1][0] = lse
 
 
-def cache_attention(queries, cols, fill, fill_row, kvs, at, sent, after, cost=COST):
+def cache_attention(queries, cols, fill, fill_row, kvs, at, sent, after):
     count = len(kvs)
     heads = cols // HD
     span = kvs[0].shape[1] // (2 * heads)
@@ -182,7 +196,7 @@
             ],
         ),
         compiler_params=pltpu.CompilerParams(vmem_limit_bytes=VMEM_LIMIT),
-        cost_estimate=cost,
+        cost_estimate=COST,
     )(jnp.stack(at), after, queries, fill, *kvs)
 
 
@@ -427,18 +441,24 @@
         hands.append([start, start + 1])
     for k in (1, 0):
         hands.append([z * GROUP + (place ^ k) for z in range(planes)])
-    pieces = dict(zip(offsets, deal(cache, hands[:1], gain)))
+    *pieces, column, own = deal(cache, hands, gain, 56 * 2**20)
+    pieces = dict(zip(offsets, pieces))
 
     def with_fill(value, d):
         rows = jnp.concatenate([slot_fill[d], slot_fill[d ^ 1]], axis=0)
-        rows = jnp.pad(rows, ((0, TAIL - 2 * GROUP), (0, value.shape[1] - lanes)))
+        tail = TAIL if d == 1 else 2 * TAIL
+        rows = jnp.pad(rows, ((0, tail - 2 * GROUP), (0, value.shape[1] - lanes)))
         return jnp.concatenate([value, rows.astype(bf16)], axis=0)
 
     across, sibling, far_here, far_rest = {}, {}, {}, {}
 
     def pass_on(d, *earlier):
         piece = ordered(across[d], *earlier)
-        sibling[d] = swap(lax.dynamic_index_in_dim(piece, 1 - core, 0), 1)
+        if d:
+            (piece,) = deal(piece, [[1 - core]], gain, 2 * 2**20)
+        else:
+            piece = lax.dynamic_index_in_dim(piece, 1 - core, 0)
+        sibling[d] = swap(piece, 1)
 
     first, second = offsets[:2]
     across[first] = swap(pieces[first], 2)
@@ -447,13 +467,11 @@
     query_here = projection(normed_here, flat[:, :cols]).astype(bf16)
     far_here[first] = swap(with_fill(query_here, first), first * GROUP)
     far_here[1] = swap(with_fill(query_here, 1), GROUP)
-    *rest, column, own = deal(cache, hands[1:], query_here)
-    pieces |= zip(offsets[1:], rest)
-    beside = swap(ordered(column, far_here[1]), 1)
-    across[second] = swap(pieces[second], 2)
+    beside = swap(column, 1)
     normed_rest = norm(ordered(jnp.concatenate(others, axis=0), query_here))
     query_rest = projection(normed_rest, flat[:, :cols]).astype(bf16)
     far_rest[first] = swap(query_rest, first * GROUP)
+    across[second] = swap(ordered(pieces[second], query_rest, beside), 2)
     projected = projection(
         jnp.concatenate([normed_here, normed_rest], axis=0), ordered(flat, query_rest)[:, cols:]
     )
@@ -461,72 +479,76 @@
     own_keys = projected[:cols].astype(bf16)
     own_values = projected[cols : 2 * cols].astype(bf16)
     far_rest[1] = swap(ordered(query_rest, far_here[1], own_values), GROUP)
-    sent = [far_here[first], far_here[1], far_rest[first], far_rest[1]]
 
     att, lse = own_attention(side, shard_tokens, queries, own_keys, own_values, persist)
     near, far = [(att, lse)], []
-    pass_on(first, lse, *sent)
+    fill_here = jnp.pad(slot_fill[0], ((0, TAIL - GROUP), (0, HD - lanes))).astype(bf16)
+    pass_on(first, lse)
+
+    def whole_of(d):
+        rest_rows = ((0, far_here[d].shape[0] - cols), (0, 0))
+        rest_rows = jnp.pad(far_rest[d], rest_rows)
+        return jnp.concatenate([far_here[d], rest_rows], axis=1)
+
     asked = {}
-    done = lse
-    fill_here = jnp.pad(slot_fill[0], ((0, TAIL - GROUP), (0, HD - lanes))).astype(bf16)
+    done = fence(lse)
     for i, d in enumerate(offsets):
         if i and d:
-            pass_on(d, att)
-        if d == 1 or (d and d % 2 == 0):
+            pass_on(d, done)
+        if d == 1:
+            asked[1] = whole_of(1)
+        if d and d % 2 == 0:
             if d not in far_here:
                 far_here[d] = swap(with_fill(ordered(query_here, done), d), d * GROUP)
                 far_rest[d] = swap(ordered(query_rest, done), d * GROUP)
-            here_rows = jnp.pad(ordered(far_here[d], *sent), ((0, TAIL), (0, 0)))
-            rest_rows = jnp.pad(ordered(far_rest[d], *sent), ((0, 2 * TAIL), (0, 0)))
-            asked[d] = jnp.concatenate([here_rows, rest_rows], axis=1)
-            if d > 1:
-                asked[d ^ 1] = swap(asked[d], GROUP)
+            asked[d] = whole_of(d)
+            asked[d ^ 1] = swap(asked[d], GROUP)
         if i + 2 < len(offsets):
-            earlier = sent if i == 0 else [done]
-            if i == 0:
-                across[offsets[i + 2]] = swap(ordered(pieces[offsets[i + 2]], across[d], *earlier), 2)
+            earlier = [across[d], far_here[d], far_rest[d]] if i == 0 else [done, far_rest[1]]
+            across[offsets[i + 2]] = swap(ordered(pieces[offsets[i + 2]], *earlier), 2)
         kvs = [own, beside, across[d], sibling.get(d)]
         at = [plane ^ d, plane ^ d, core, jnp.zeros_like(core)]
         if d:
-            if d == 1:
-                done = ordered(done, far[0])
+            if d != first:
+                done = fence(done)
             row = GROUP * (d % 2 if d > 1 else 0)
             (done,) = cache_attention(
-                asked[d], cols, asked[d], row, kvs, at, True, done, LAST if d == 1 else COST
+                asked[d], cols, asked[d], row, kvs, at, True, done
             )
-            att = done
             far.append(swap(done, d * GROUP))
-            if 0 < i < len(offsets) - 2:
-                across[offsets[i + 2]] = swap(ordered(pieces[offsets[i + 2]], done), 2)
+            if i == len(offsets) - 3:
+                weights = [output_weight] + [
+                    turn(ordered(output_weight, done), step) for step in range(1, n_head)
+                ]
         else:
-            for part in (slice(0, 2), slice(2, 3), slice(3, 4)):
+            pair = cache_attention(
+                queries, cols, fill_here, 0, kvs[:2], at[:2], False, done
+            )
+            near.append(pair)
+            done = fence(pair[1], far[0])
+            pass_on(d, done)
+            kvs[3] = sibling[d]
+            for part in (slice(2, 3), slice(3, 4)):
                 pair = cache_attention(
                     queries, cols, fill_here, part.start, kvs[part], at[part], False, done
                 )
                 near.append(pair)
                 done = pair[1]
-                if part.start == 0:
-                    pass_on(d, done)
-                    kvs[3] = sibling[d]
         if i == 0:
             memory_read, new_state = memory_pass(
                 side, shard_tokens, retention, momentum, memory_step_scale, halving_updates,
                 done, queries, own_keys, own_values, memory_state[:, 0],
             )
             done = memory_read
-        if d == 1:
-            late = across[d]
     head_out = merge(near, far, projected, memory_read)
 
     layer = jnp.zeros((shard_tokens, width), f32)
     for step in range(n_head):
         away = (n_head - step) % n_head
         part = head_out[:, away * shard_tokens : (away + 1) * shard_tokens]
-        weight = output_weight
         if step:
             part = turn(part, step)
-            weight = turn(ordered(output_weight, late), step)
-        layer = layer + dot(part, weight, ((0,), (0,))).astype(bf16).astype(f32)
+        layer = layer + dot(part, weights[step], ((0,), (0,))).astype(bf16).astype(f32)
     return (layer.astype(bf16)[None], new_state[:, None])
 
 

time: 135 us -> 121 us (0.90)
  the two profiles are of different devices: /device:TPU:2 before, /device:TPU:0 now
where the time goes in v2:
time: 121 us
  Pallas kernels  44.7 us (37%)
  waiting for transfers between devices  36.9 us (30%)
  starting transfers between devices  19.3 us (16%)
  matrix products  7.71 us (6%)
  other arithmetic  7.39 us (6%)
  local copies, waits for them, and re-layouts  3.27 us (3%)
  between operations  1.84 us (2%)
    ppermute x17, waiting for transfers between devices, swap(): return lax.ppermute(value, 'req', [(i, i ^ step) for i in range(devices)])  28.6 us
    pallas_call x6, Pallas kernels, cache_attention(): pl.pallas_call(functools.partial(cache_kernel, (span, heads, count, fill_...  25.9 us
    ppermute x17, starting transfers between devices, swap(): return lax.ppermute(value, 'req', [(i, i ^ step) for i in range(devices)])  15.7 us
    ppermute x3, waiting for transfers between devices, turn(): lax.ppermute(value, 'head', [(i, (i - step) % n_head) for i in range(n_he...  8.32 us
    pallas_call x4, Pallas kernels, deal(): pl.pallas_call(functools.partial(deal_kernel, counts), out_shape=[jax.Sha...  8.1 us
    dot_general x5, matrix products, dot(): lax.dot_general(left, right, (contract, ((), ())), precision=precision, p...  7.71 us
    pallas_call x1, Pallas kernels, memory_pass(): pl.pallas_call(functools.partial(memory_kernel, count), out_shape=(jax.Sh...  5.99 us
    ppermute x3, starting transfers between devices, turn(): lax.ppermute(value, 'head', [(i, (i - step) % n_head) for i in range(n_he...  3.56 us
  transfers between devices with their start and end apart: 20, of which 9 were waited for; matrix products, arithmetic and copies ran while one was open for 13% of the time, Pallas kernels for 37%

profile of v2, /device:TPU:0, one launch (start us, length us, event | category | flops | bytes accessed | tf_op | source)
XLA Modules:
  0.0 121.1 jit_solution(14903870080322149298)
XLA Ops:
  0.6 3.0 %collective-permute-start = (bf16[256,1024]{1,0:T(8,128)(2,1)}, bf16[256,1024]{1,0:T(8,128)(2,1)}, u32[]{:S(2)}, u32[]{:S(2)}) collective-permute-start(bf16[256,1024]{1,0:T(8,128)(2,1)} %bitcast.62), channel_id=1, source_target_pairs={{0,1},{1,0},{2,3},{3,2},{4,5},{5,4},{6,7},{7,6},{8,9},{9,8},{10,11... | collective-permute-start | bytes 1572872 | tf_op jit(solution)/shard_map/ppermute | solution.py:402
  4.3 7.8 %shard_map.149 = (bf16[2,2048,128]{2,1,0:T(8,128)(2,1)}, bf16[2,2048,128]{2,1,0:T(8,128)(2,1)}, bf16[2,2048,128]{2,1,0:T(8,128)(2,1)}, bf16[2,2048,128]{2,1,0:T(...) custom-call(s32[16]{0:T(128)} %stack.106.at_ref, bf16[16,2048,128]{2,1,0:T(8,128)(2,1)} %bitcast.57, ...), custom_call_target="tpu_custom_call" | custom-call | flops 1 | bytes 1 | tf_op jit(solution)/shard_map/pallas_call | solution.py:70
  12.1 1.6 %collective-permute-start.4 = (bf16[2,2048,128]{2,1,0:T(8,128)(2,1)}, bf16[2,2048,128]{2,1,0:T(8,128)(2,1)S(1)}, u32[]{:S(2)}, u32[]{:S(2)}) collective-permute-start(bf16[2,2048,128]{2,1,0:T(8,128)(2,1)} %get-tuple-element.30), channel_id=1, source_target_pairs={{0,4},{2,6},{4,0},{6,2},{8,12},{10,14},{12,8},{14,10},{16,20},{18,... | collective-permute-start | bytes 3145736 | tf_op jit(solution)/shard_map/ppermute | solution.py:399
  15.2 1.4 %copy.23 = bf16[128,8,4,512]{3,1,2,0:T(8,128)(2,1)S(1)} copy(bf16[128,8,4,512]{3,2,1,0:T(4,128)(2,1)S(1)} %bitcast.58) | data formatting | bytes 8388608
  19.1 1.6 %collective-permute-start.9 = (bf16[528,256]{1,0:T(8,128)(2,1)}, bf16[528,256]{1,0:T(8,128)(2,1)}, u32[]{:S(2)}, u32[]{:S(2)}) collective-permute-start(bf16[528,256]{1,0:T(8,128)(2,1)} %pad_maximum_fusion.2), channel_id=1, source_target_pairs={{0,8},{2,10},{4,12},{6,14},{8,0},{10,2},{12,4},{14,6},{16,24},{18,... | collective-permute-start | bytes 811016 | tf_op jit(solution)/shard_map/ppermute | solution.py:399
  21.5 2.6 %collective-permute-start.1 = (bf16[544,256]{1,0:T(8,128)(2,1)}, bf16[544,256]{1,0:T(8,128)(2,1)}, u32[]{:S(2)}, u32[]{:S(2)}) collective-permute-start(bf16[544,256]{1,0:T(8,128)(2,1)} %pad_maximum_fusion.1), channel_id=1, source_target_pairs={{0,16},{2,18},{4,20},{6,22},{8,24},{10,26},{12,28},{14,30},{16,0},... | collective-permute-start | bytes 835592 | tf_op jit(solution)/shard_map/ppermute | solution.py:399
  24.3 1.2 %fusion.12 = f32[256]{0:T(256)S(1)} fusion(bf16[256,1024]{1,0:T(8,128)(2,1)} %collective-permute-done), kind=kLoop, calls=%fused_computation.22 | loop fusion | flops 786176 | bytes 525312 | tf_op jit(solution)/shard_map/reduce_sum | solution.py:412
  25.6 1.2 %fusion.14 = bf16[256,1024]{1,0:T(8,128)(2,1)S(1)} fusion(bf16[256,1024]{1,0:T(8,128)(2,1)} %collective-permute-done, f32[256]{0:T(256)S(1)} %add_rsqrt_fusion, f32[1024]{0:T(1024)S(1)} %convert_element_type.47), kind=kLoop, calls=%fused_computation.24 | loop fusion | flops 1048576 | bytes 1053696 | tf_op jit(solution)/shard_map/convert_element_type | solution.py:413
  26.8 1.7 %convolution_convert_fusion.2 = bf16[512,256]{1,0:T(8,128)(2,1)S(1)} fusion(bf16[256,1024]{1,0:T(8,128)(2,1)S(1)} %fusion.14, bf16[1024,2048]{1,0:T(8,128)(2,1)} %bitcast.60), kind=kOutput, calls=%fused_computation.13 | convolution fusion | flops 268566528 | bytes 1835008 | tf_op jit(solution)/shard_map/dot_general | solution.py:30
  29.0 3.8 %fusion.38 = (bf16[1536,512]{1,0:T(8,128)(2,1)S(1)}, f32[1536,512]{1,0:T(8,128)S(1)}) fusion(bf16[256,1024]{1,0:T(8,128)(2,1)S(1)} %fusion.14, bf16[256,1024]{1,0:T(8,128)(2,1)S(1)} %copy-done.13, bf16[1024,2048]{1,0:T(8,128)(2,1)} %bitcast.61), kind=kOutput, calls=%fused_computation.73 | convolution fusion | flops 1613496320 | bytes 8912896 | tf_op jit(solution)/shard_map/dot_general | solution.py:30
  34.0 3.3 %shard_map.150 = (f32[4,128,512]{2,1,0:T(8,128)S(1)}, f32[4,1,512]{2,1,0:T(1,128)S(1)}) custom-call(s32[1]{0:T(128)} %bitcast.side_ref, bf16[512,512]{1,0:T(8,128)(2,1)S(1)} %pad_maximum_fusion.q_ref, bf16[512,512]{1,0:T(8,128)(2,1)S(1)} %get-tuple-element.63.k_ref, bf16[512,512]{1,0:T(8,128)(2,1)S(1)} %get-tuple-element.62.v_ref, ...), custom_call_target="tpu_custom_call" | custom-call | flops 1 | bytes 1 | tf_op jit(solution)/shard_map/pallas_call | solution.py:231
  37.3 1.2 collective-permute-done.4.from_ref.refs_2_
  38.7 5.1 %collective-permute-done.1 = bf16[544,256]{1,0:T(8,128)(2,1)} collective-permute-done((bf16[544,256]{1,0:T(8,128)(2,1)}, bf16[544,256]{1,0:T(8,128)(2,1)}, u32[]{:S(2)}, u32[]{:S(2)}) %collective-permute-start.1) | collective-permute-done | bytes 278560 | tf_op jit(solution)/shard_map/ppermute | solution.py:399
  43.8 4.8 %collective-permute-done.2 = bf16[512,256]{1,0:T(8,128)(2,1)S(1)} collective-permute-done((bf16[512,256]{1,0:T(8,128)(2,1)S(1)}, bf16[512,256]{1,0:T(8,128)(2,1)S(1)}, u32[]{:S(2)}, u32[]{:S(2)}) %collective-permute-start.2) | collective-permute-done | bytes 262176 | tf_op jit(solution)/shard_map/ppermute | solution.py:399
  51.6 5.8 %shard_map.153.after_ref = bf16[528,512]{1,0:T(8,128)(2,1)S(1)} custom-call(s32[4]{0:T(128)S(1)} %pad_add_fusion.at_ref, f32[8,128]{1,0:T(8,128)S(1)} %shard_map.151.after_ref, bf16[544,512]{1,0:T(8,128)(2,1)S(1)} %fusion.20.q_ref.fill_ref, bf16[544,512]{1,0:T(8,128)(2,1)S(1)} %fusion.20.q_ref.fill_ref, bf16[4,2048,128]{2,1,0:T(8,128)(2,1)S(1)} %copy-done, ...), custom_call_target="tpu_custom_call" | custom-call | flops 1 | bytes 1 | tf_op jit(solution)/shard_map/pallas_call | solution.py:176
  57.4 3.1 %collective-permute-start.13 = (bf16[528,512]{1,0:T(8,128)(2,1)S(1)}, bf16[528,512]{1,0:T(8,128)(2,1)S(1)}, u32[]{:S(2)}, u32[]{:S(2)}) collective-permute-start(bf16[528,512]{1,0:T(8,128)(2,1)S(1)} %shard_map.153.after_ref), channel_id=1, source_target_pairs={{0,16},{2,18},{4,20},{6,22},{8,24},{10,26},{12,28},{14,30},{16,0},... | collective-permute-start | bytes 1622024 | tf_op jit(solution)/shard_map/ppermute | solution.py:399
  60.5 6.0 %shard_map.154 = (f32[512,512]{1,0:T(8,128)S(1)}, f32[2,4,128,128]{3,2,1,0:T(8,128)}) custom-call(s32[1]{0:T(128)} %bitcast.side_ref, f32[1,4]{1,0:T(1,128)S(1)} %copy-done.4, f32[1,4]{1,0:T(1,128)S(1)} %copy-done.5, f32[1,4]{1,0:T(1,128)S(1)} %copy-done.6, s32[1,8]{1,0:T(1,128)S(1)} %copy-done.7, bf16[528,512]{1,0:T(8,128)(2,1)S(1)} %shard_map.153.after_ref, ...), custom_call_target="tpu_custom_call" | custom-call | flops 1 | bytes 1 | tf_op jit(solution)/shard_map/pallas_call | solution.py:307
  66.5 1.5 %collective-permute-start.14 = (bf16[2,2048,128]{2,1,0:T(8,128)(2,1)S(1)}, bf16[2,2048,128]{2,1,0:T(8,128)(2,1)S(1)}, u32[]{:S(2)}, u32[]{:S(2)}) collective-permute-start(bf16[2,2048,128]{2,1,0:T(8,128)(2,1)S(1)} %copy-done.14), channel_id=1, source_target_pairs={{0,4},{2,6},{4,0},{6,2},{8,12},{10,14},{12,8},{14,10},{16,20},{18,... | collective-permute-start | bytes 3145736 | tf_op jit(solution)/shard_map/ppermute | solution.py:399
  68.8 1.3 %collective-permute-done.8.refs_3_ = bf16[1,2048,128]{2,1,0:T(8,128)(2,1)S(1)} collective-permute-done((bf16[1,2048,128]{2,1,0:T(8,128)(2,1)S(1)}, bf16[1,2048,128]{2,1,0:T(8,128)(2,1)S(1)}, u32[]{:S(2)}, u32[]{:S(2)}) %collective-permute-start.8) | collective-permute-done | bytes 524320 | tf_op jit(solution)/shard_map/ppermute | solution.py:399
  70.1 5.8 %shard_map.157.refs_0_ = bf16[528,512]{1,0:T(8,128)(2,1)S(1)} custom-call(s32[4]{0:T(128)S(1)} %pad_add_fusion.1.at_ref, f32[8,128]{1,0:T(8,128)S(1)} %shard_map.155.after_ref, bf16[544,512]{1,0:T(8,128)(2,1)S(1)} %collective-permute-done.6.q_ref.fill_ref, bf16[544,512]{1,0:T(8,128)(2,1)S(1)} %collective-permute-done.6.q_ref.fill_ref, ...), custom_call_target="tpu_custom_call" | custom-call | flops 1 | bytes 1 | tf_op jit(solution)/shard_map/pallas_call | solution.py:176
  75.9 1.3 %collective-permute-start.16 = (bf16[528,512]{1,0:T(8,128)(2,1)S(1)}, bf16[528,512]{1,0:T(8,128)(2,1)S(1)}, u32[]{:S(2)}, u32[]{:S(2)}) collective-permute-start(bf16[528,512]{1,0:T(8,128)(2,1)S(1)} %shard_map.157.refs_0_), channel_id=1, source_target_pairs={{0,24},{2,26},{4,28},{6,30},{8,16},{10,18},{12,20},{14,22},{16,8},... | collective-permute-start | bytes 1622024 | tf_op jit(solution)/shard_map/ppermute | solution.py:399
  77.2 6.2 %collective-permute-done.11.from_ref.refs_2_ = bf16[2,2048,128]{2,1,0:T(8,128)(2,1)S(1)} collective-permute-done((bf16[2,2048,128]{2,1,0:T(8,128)(2,1)S(1)}, bf16[2,2048,128]{2,1,0:T(8,128)(2,1)S(1)}, u32[]{:S(2)}, u32[]{:S(2)}) %collective-permute-start.11) | collective-permute-done | bytes 1048608 | tf_op jit(solution)/shard_map/ppermute | solution.py:399
  83.7 1.8 %collective-permute-done.12.refs_3_ = bf16[1,2048,128]{2,1,0:T(8,128)(2,1)S(1)} collective-permute-done((bf16[1,2048,128]{2,1,0:T(8,128)(2,1)S(1)}, bf16[1,2048,128]{2,1,0:T(8,128)(2,1)S(1)}, u32[]{:S(2)}, u32[]{:S(2)}) %collective-permute-start.12) | collective-permute-done | bytes 524320 | tf_op jit(solution)/shard_map/ppermute | solution.py:399
  85.5 5.8 %shard_map.160.after_ref = bf16[528,512]{1,0:T(8,128)(2,1)S(1)} custom-call(s32[4]{0:T(128)S(1)} %pad_add_fusion.2.at_ref, f32[8,128]{1,0:T(8,128)S(1)} %shard_map.158.after_ref, bf16[528,512]{1,0:T(8,128)(2,1)S(1)} %fusion.21.q_ref.fill_ref, bf16[528,512]{1,0:T(8,128)(2,1)S(1)} %fusion.21.q_ref.fill_ref, bf16[4,2048,128]{2,1,0:T(8,128)(2,1)S(1)} %copy-done, ...), custom_call_target="tpu_custom_call" | custom-call | flops 1 | bytes 1 | tf_op jit(solution)/shard_map/pallas_call | solution.py:176
  91.3 1.6 %collective-permute-start.17 = (bf16[528,512]{1,0:T(8,128)(2,1)S(1)}, bf16[528,512]{1,0:T(8,128)(2,1)S(1)}, u32[]{:S(2)}, u32[]{:S(2)}) collective-permute-start(bf16[528,512]{1,0:T(8,128)(2,1)S(1)} %shard_map.160.after_ref), channel_id=1, source_target_pairs={{0,8},{2,10},{4,12},{6,14},{8,0},{10,2},{12,4},{14,6},{16,24},{18,... | collective-permute-start | bytes 1622024 | tf_op jit(solution)/shard_map/ppermute | solution.py:399
  93.0 3.9 %shard_map.161 = (f32[4,128,512]{2,1,0:T(8,128)S(1)}, f32[4,1,512]{2,1,0:T(1,128)S(1)}) custom-call(s32[2]{0:T(128)S(1)} %pad_add_fusion.3.at_ref, bf16[528,512]{1,0:T(8,128)(2,1)S(1)} %shard_map.160.after_ref, bf16[512,512]{1,0:T(8,128)(2,1)S(1)} %pad_maximum_fusion.q_ref, bf16[16,128]{1,0:T(8,128)(2,1)S(1)} %pad.27.fill_ref, ...), custom_call_target="tpu_custom_call" | custom-call | flops 1 | bytes 1 | tf_op jit(solution)/shard_map/pallas_call | solution.py:176
  96.9 7.6 %collective-permute-done.14.refs_0_ = bf16[2,2048,128]{2,1,0:T(8,128)(2,1)S(1)} collective-permute-done((bf16[2,2048,128]{2,1,0:T(8,128)(2,1)S(1)}, bf16[2,2048,128]{2,1,0:T(8,128)(2,1)S(1)}, u32[]{:S(2)}, u32[]{:S(2)}) %collective-permute-start.14) | collective-permute-done | bytes 1048608 | tf_op jit(solution)/shard_map/ppermute | solution.py:399
  104.6 2.3 %shard_map.163 = (f32[4,128,512]{2,1,0:T(8,128)S(1)}, f32[4,1,512]{2,1,0:T(1,128)S(1)}) custom-call(s32[1]{0:T(128)} %bitcast.23.at_ref, f32[8,128]{1,0:T(8,128)S(1)} %shard_map.162.after_ref, bf16[512,512]{1,0:T(8,128)(2,1)S(1)} %pad_maximum_fusion.q_ref, bf16[16,128]{1,0:T(8,128)(2,1)S(1)} %pad.27.fill_ref, ...), custom_call_target="tpu_custom_call" | custom-call | flops 1 | bytes 1 | tf_op jit(solution)/shard_map/pallas_call | solution.py:176
  106.9 2.3 %shard_map.164 = (f32[4,128,512]{2,1,0:T(8,128)S(1)}, f32[4,1,512]{2,1,0:T(1,128)S(1)}) custom-call(s32[1]{0:T(128)} %constant.84.clone.1.at_ref, f32[4,1,512]{2,1,0:T(1,128)S(1)} %get-tuple-element.52.after_ref.refs_5_, bf16[512,512]{1,0:T(8,128)(2,1)S(1)} %pad_maximum_fusion.q_ref, bf16[16,128]{1,0:T(8,128)(2,1)S(1)} %pad.27.fill_ref, ...), custom_call_target="tpu_custom_call" | custom-call | flops 1 | bytes 1 | tf_op jit(solution)/shard_map/pallas_call | solution.py:176
  109.2 1.4 %shard_map.165 = bf16[512,512]{1,0:T(8,128)(2,1)S(1)} custom-call(f32[4,128,512]{2,1,0:T(8,128)S(1)} %get-tuple-element.34.refs_0_, f32[4,1,512]{2,1,0:T(1,128)S(1)} %get-tuple-element.35.refs_0_.refs_1_, f32[4,128,512]{2,1,0:T(8,128)S(1)} %get-tuple-element.47.refs_2_, f32[4,1,512]{2,1,0:T(1,128)S(1)} %get-tuple-element.48.refs_0_.refs_3_, ...), custom_call_target="tpu_custom_call" | custom-call | flops 18350080 | bytes 8388608 | tf_op jit(solution)/shard_map/pallas_call | solution.py:352
  111.0 8.3 %collective-permute-done.18 = bf16[512,256]{1,0:T(8,128)(2,1)S(1)} collective-permute-done((bf16[512,256]{1,0:T(8,128)(2,1)S(1)}, bf16[512,256]{1,0:T(8,128)(2,1)S(1)}, u32[]{:S(2)}, u32[]{:S(2)}) %collective-permute-start.18) | collective-permute-done | bytes 262176 | tf_op jit(solution)/shard_map/ppermute | solution.py:402
  119.8 1.3 %fusion.6 = bf16[1,256,1024]{2,1,0:T(8,128)(2,1)} fusion(f32[256,1024]{1,0:T(8,128)S(1)} %fusion.2, bf16[512,1024]{1,0:T(8,128)(2,1)S(1)} %copy-done.11, bf16[512,512]{1,0:T(8,128)(2,1)S(1)} %shard_map.165), kind=kOutput, calls=%fused_computation.12 | convolution fusion | flops 269484032 | bytes 2883584 | tf_op jit(solution)/shard_map/dot_general | solution.py:30
  (101 shorter events, 11.7 us)
Async XLA Ops:
  0.6 23.7 %collective-permute-start = (bf16[256,1024]{1,0:T(8,128)(2,1)}, bf16[256,1024]{1,0:T(8,128)(2,1)}, u32[]{:S(2)}, u32[]{:S(2)}) collective-permute-start(bf16[256,1024]{1,0:T(8,128)(2,1)} %bitcast.62), channel_id=1, source_target_pairs={{0,1},{1,0},{2,3},{3,2},{4,5},{5,4},{6,7},{7,6},{8,9},{9,8},{10,11... | collective-permute-start | bytes 1572872 | tf_op jit(solution)/shard_map/ppermute | solution.py:402
  4.3 9.4 %copy-start.2 = (bf16[1024]{0:T(1024)(128)(2,1)S(1)}, bf16[1024]{0:T(1024)(128)(2,1)}, u32[]{:S(2)}) copy-start(bf16[1024]{0:T(1024)(128)(2,1)} %after_ref.7) | copy-start | bytes 6148
  4.3 9.4 %copy-start.10 = (bf16[1,256,1024]{2,1,0:T(8,128)(2,1)S(1)}, bf16[1,256,1024]{2,1,0:T(8,128)(2,1)}, u32[]{:S(2)}) copy-start(bf16[1,256,1024]{2,1,0:T(8,128)(2,1)} %param.14) | copy-start | bytes 1572868
  4.3 10.4 %copy-start.17 = (s32[1,128]{1,0:T(1,128)S(1)}, s32[1,128]{1,0:T(1,128)}, u32[]{:S(2)}) copy-start(s32[1,128]{1,0:T(1,128)} %param.22) | copy-start | bytes 1540
  4.3 10.4 %copy-start.18 = (s32[1,128]{1,0:T(1,128)S(1)}, s32[1,128]{1,0:T(1,128)}, u32[]{:S(2)}) copy-start(s32[1,128]{1,0:T(1,128)} %param.21) | copy-start | bytes 1540
  4.3 10.9 %copy-start.8 = (bf16[1024,4,512]{2,1,0:T(4,128)(2,1)S(1)}, bf16[1024,4,512]{2,1,0:T(4,128)(2,1)}, u32[]{:S(2)}) copy-start(bf16[1024,4,512]{2,1,0:T(4,128)(2,1)} %param.16) | copy-start | bytes 12582916
  12.1 26.4 %collective-permute-start.4 = (bf16[2,2048,128]{2,1,0:T(8,128)(2,1)}, bf16[2,2048,128]{2,1,0:T(8,128)(2,1)S(1)}, u32[]{:S(2)}, u32[]{:S(2)}) collective-permute-start(bf16[2,2048,128]{2,1,0:T(8,128)(2,1)} %get-tuple-element.30), channel_id=1, source_target_pairs={{0,4},{2,6},{4,0},{6,2},{8,12},{10,14},{12,8},{14,10},{16,20},{18,... | collective-permute-start | bytes 3145736 | tf_op jit(solution)/shard_map/ppermute | solution.py:399
  13.7 19.1 %collective-permute-start.3 = (bf16[4,2048,128]{2,1,0:T(8,128)(2,1)}, bf16[4,2048,128]{2,1,0:T(8,128)(2,1)S(1)}, u32[]{:S(2)}, u32[]{:S(2)}) collective-permute-start(bf16[4,2048,128]{2,1,0:T(8,128)(2,1)} %get-tuple-element.37), channel_id=1, source_target_pairs={{0,2},{2,0},{4,6},{6,4},{8,10},{10,8},{12,14},{14,12},{16,18},{18,... | collective-permute-start | bytes 6291464 | tf_op jit(solution)/shard_map/ppermute | solution.py:399
  19.1 14.3 %collective-permute-start.9 = (bf16[528,256]{1,0:T(8,128)(2,1)}, bf16[528,256]{1,0:T(8,128)(2,1)}, u32[]{:S(2)}, u32[]{:S(2)}) collective-permute-start(bf16[528,256]{1,0:T(8,128)(2,1)} %pad_maximum_fusion.2), channel_id=1, source_target_pairs={{0,8},{2,10},{4,12},{6,14},{8,0},{10,2},{12,4},{14,6},{16,24},{18,... | collective-permute-start | bytes 811016 | tf_op jit(solution)/shard_map/ppermute | solution.py:399
  21.5 22.3 %collective-permute-start.1 = (bf16[544,256]{1,0:T(8,128)(2,1)}, bf16[544,256]{1,0:T(8,128)(2,1)}, u32[]{:S(2)}, u32[]{:S(2)}) collective-permute-start(bf16[544,256]{1,0:T(8,128)(2,1)} %pad_maximum_fusion.1), channel_id=1, source_target_pairs={{0,16},{2,18},{4,20},{6,22},{8,24},{10,26},{12,28},{14,30},{16,0},... | collective-permute-start | bytes 835592 | tf_op jit(solution)/shard_map/ppermute | solution.py:399
  28.6 20.0 %collective-permute-start.2 = (bf16[512,256]{1,0:T(8,128)(2,1)S(1)}, bf16[512,256]{1,0:T(8,128)(2,1)S(1)}, u32[]{:S(2)}, u32[]{:S(2)}) collective-permute-start(bf16[512,256]{1,0:T(8,128)(2,1)S(1)} %convolution_convert_fusion.2), channel_id=1, source_target_pairs={{0,16},{2,18},{4,20},{6,22},{8,24},{10,26},{12,28},{14,30},{16,0},... | collective-permute-start | bytes 786440 | tf_op jit(solution)/shard_map/ppermute | solution.py:399
  32.8 35.2 %collective-permute-start.7 = (bf16[2,2048,128]{2,1,0:T(8,128)(2,1)S(1)}, bf16[2,2048,128]{2,1,0:T(8,128)(2,1)S(1)}, u32[]{:S(2)}, u32[]{:S(2)}) collective-permute-start(bf16[2,2048,128]{2,1,0:T(8,128)(2,1)S(1)} %copy-done.16), channel_id=1, source_target_pairs={{0,4},{2,6},{4,0},{6,2},{8,12},{10,14},{12,8},{14,10},{16,20},{18,... | collective-permute-start | bytes 3145736 | tf_op jit(solution)/shard_map/ppermute | solution.py:399
  33.5 15.1 %copy-start.15 = (bf16[2,2048,128]{2,1,0:T(8,128)(2,1)S(1)}, bf16[2,2048,128]{2,1,0:T(8,128)(2,1)}, u32[]{:S(2)}) copy-start(bf16[2,2048,128]{2,1,0:T(8,128)(2,1)} %get-tuple-element.45) | copy-start | bytes 3145732
  33.5 17.0 %collective-permute-start.10 = (bf16[512,256]{1,0:T(8,128)(2,1)S(1)}, bf16[512,256]{1,0:T(8,128)(2,1)S(1)}, u32[]{:S(2)}, u32[]{:S(2)}) collective-permute-start(bf16[512,256]{1,0:T(8,128)(2,1)S(1)} %convolution_convert_fusion.2), channel_id=1, source_target_pairs={{0,8},{2,10},{4,12},{6,14},{8,0},{10,2},{12,4},{14,6},{16,24},{18,... | collective-permute-start | bytes 786440 | tf_op jit(solution)/shard_map/ppermute | solution.py:399
  38.6 12.9 %collective-permute-start.5 = (bf16[1,2048,128]{2,1,0:T(8,128)(2,1)S(1)}, bf16[1,2048,128]{2,1,0:T(8,128)(2,1)S(1)}, u32[]{:S(2)}, u32[]{:S(2)}) collective-permute-start(bf16[1,2048,128]{2,1,0:T(8,128)(2,1)S(1)} %shard_map.152), channel_id=1, source_target_pairs={{0,2},{2,0},{4,6},{6,4},{8,10},{10,8},{12,14},{14,12},{16,18},{18,... | collective-permute-start | bytes 1572872 | tf_op jit(solution)/shard_map/ppermute | solution.py:399
  48.6 34.8 %collective-permute-start.11 = (bf16[2,2048,128]{2,1,0:T(8,128)(2,1)S(1)}, bf16[2,2048,128]{2,1,0:T(8,128)(2,1)S(1)}, u32[]{:S(2)}, u32[]{:S(2)}) collective-permute-start(bf16[2,2048,128]{2,1,0:T(8,128)(2,1)S(1)} %copy-done.15), channel_id=1, source_target_pairs={{0,4},{2,6},{4,0},{6,2},{8,12},{10,14},{12,8},{14,10},{16,20},{18,... | collective-permute-start | bytes 3145736 | tf_op jit(solution)/shard_map/ppermute | solution.py:399
  50.4 18.4 %collective-permute-start.6 = (bf16[544,512]{1,0:T(8,128)(2,1)S(1)}, bf16[544,512]{1,0:T(8,128)(2,1)S(1)}, u32[]{:S(2)}, u32[]{:S(2)}) collective-permute-start(bf16[544,512]{1,0:T(8,128)(2,1)S(1)} %fusion.20.q_ref.fill_ref), channel_id=1, source_target_pairs={{0,8},{2,10},{4,12},{6,14},{8,0},{10,2},{12,4},{14,6},{16,24},{18,... | collective-permute-start | bytes 1671176 | tf_op jit(solution)/shard_map/ppermute | solution.py:399
  51.5 9.0 %copy-start.1 = (f32[2,1,4,128,128]{4,3,2,1,0:T(8,128)S(1)}, f32[2,1,4,128,128]{4,3,2,1,0:T(8,128)}, u32[]{:S(2)}) copy-start(f32[2,1,4,128,128]{4,3,2,1,0:T(8,128)} %param.23) | copy-start | bytes 1572868
  51.5 9.0 %copy-start.4 = (f32[1,4]{1,0:T(1,128)S(1)}, f32[1,4]{1,0:T(1,128)}, u32[]{:S(2)}) copy-start(f32[1,4]{1,0:T(1,128)} %retention_ref.1) | copy-start | bytes 52
  51.5 9.0 %copy-start.5 = (f32[1,4]{1,0:T(1,128)S(1)}, f32[1,4]{1,0:T(1,128)}, u32[]{:S(2)}) copy-start(f32[1,4]{1,0:T(1,128)} %momentum_ref.1) | copy-start | bytes 52
  51.5 9.0 %copy-start.6 = (f32[1,4]{1,0:T(1,128)S(1)}, f32[1,4]{1,0:T(1,128)}, u32[]{:S(2)}) copy-start(f32[1,4]{1,0:T(1,128)} %step_ref.1) | copy-start | bytes 52
  57.4 9.1 %copy-start.14 = (bf16[2,2048,128]{2,1,0:T(8,128)(2,1)S(1)}, bf16[2,2048,128]{2,1,0:T(8,128)(2,1)}, u32[]{:S(2)}) copy-start(bf16[2,2048,128]{2,1,0:T(8,128)(2,1)} %get-tuple-element.50) | copy-start | bytes 3145732
  57.4 39.5 %collective-permute-start.13 = (bf16[528,512]{1,0:T(8,128)(2,1)S(1)}, bf16[528,512]{1,0:T(8,128)(2,1)S(1)}, u32[]{:S(2)}, u32[]{:S(2)}) collective-permute-start(bf16[528,512]{1,0:T(8,128)(2,1)S(1)} %shard_map.153.after_ref), channel_id=1, source_target_pairs={{0,16},{2,18},{4,20},{6,22},{8,24},{10,26},{12,28},{14,30},{16,0},... | collective-permute-start | bytes 1622024 | tf_op jit(solution)/shard_map/ppermute | solution.py:399
  66.5 37.9 %collective-permute-start.14 = (bf16[2,2048,128]{2,1,0:T(8,128)(2,1)S(1)}, bf16[2,2048,128]{2,1,0:T(8,128)(2,1)S(1)}, u32[]{:S(2)}, u32[]{:S(2)}) collective-permute-start(bf16[2,2048,128]{2,1,0:T(8,128)(2,1)S(1)} %copy-done.14), channel_id=1, source_target_pairs={{0,4},{2,6},{4,0},{6,2},{8,12},{10,14},{12,8},{14,10},{16,20},{18,... | collective-permute-start | bytes 3145736 | tf_op jit(solution)/shard_map/ppermute | solution.py:399
  68.1 2.0 %collective-permute-start.8 = (bf16[1,2048,128]{2,1,0:T(8,128)(2,1)S(1)}, bf16[1,2048,128]{2,1,0:T(8,128)(2,1)S(1)}, u32[]{:S(2)}, u32[]{:S(2)}) collective-permute-start(bf16[1,2048,128]{2,1,0:T(8,128)(2,1)S(1)} %shard_map.156), channel_id=1, source_target_pairs={{0,2},{2,0},{4,6},{6,4},{8,10},{10,8},{12,14},{14,12},{16,18},{18,... | collective-permute-start | bytes 1572872 | tf_op jit(solution)/shard_map/ppermute | solution.py:399
  68.2 15.4 %copy-start.11 = (bf16[512,1024]{1,0:T(8,128)(2,1)S(1)}, bf16[512,1024]{1,0:T(8,128)(2,1)}, u32[]{:S(2)}) copy-start(bf16[512,1024]{1,0:T(8,128)(2,1)} %param.17) | copy-start | bytes 3145732
  75.9 33.3 %collective-permute-start.16 = (bf16[528,512]{1,0:T(8,128)(2,1)S(1)}, bf16[528,512]{1,0:T(8,128)(2,1)S(1)}, u32[]{:S(2)}, u32[]{:S(2)}) collective-permute-start(bf16[528,512]{1,0:T(8,128)(2,1)S(1)} %shard_map.157.refs_0_), channel_id=1, source_target_pairs={{0,24},{2,26},{4,28},{6,30},{8,16},{10,18},{12,20},{14,22},{16,8},... | collective-permute-start | bytes 1622024 | tf_op jit(solution)/shard_map/ppermute | solution.py:399
  83.5 2.0 %collective-permute-start.12 = (bf16[1,2048,128]{2,1,0:T(8,128)(2,1)S(1)}, bf16[1,2048,128]{2,1,0:T(8,128)(2,1)S(1)}, u32[]{:S(2)}, u32[]{:S(2)}) collective-permute-start(bf16[1,2048,128]{2,1,0:T(8,128)(2,1)S(1)} %shard_map.159), channel_id=1, source_target_pairs={{0,2},{2,0},{4,6},{6,4},{8,10},{10,8},{12,14},{14,12},{16,18},{18,... | collective-permute-start | bytes 1572872 | tf_op jit(solution)/shard_map/ppermute | solution.py:399
  83.6 27.4 %collective-permute-start.19 = (bf16[512,1024]{1,0:T(8,128)(2,1)S(1)}, bf16[512,1024]{1,0:T(8,128)(2,1)S(1)}, u32[]{:S(2)}, u32[]{:S(2)}) collective-permute-start(bf16[512,1024]{1,0:T(8,128)(2,1)S(1)} %copy-done.11), channel_id=1, source_target_pairs={{0,1},{1,0},{2,3},{3,2},{4,5},{5,4},{6,7},{7,6},{8,9},{9,8},{10,11... | collective-permute-start | bytes 3145736 | tf_op jit(solution)/shard_map/ppermute | solution.py:402
  91.3 17.8 %collective-permute-start.17 = (bf16[528,512]{1,0:T(8,128)(2,1)S(1)}, bf16[528,512]{1,0:T(8,128)(2,1)S(1)}, u32[]{:S(2)}, u32[]{:S(2)}) collective-permute-start(bf16[528,512]{1,0:T(8,128)(2,1)S(1)} %shard_map.160.after_ref), channel_id=1, source_target_pairs={{0,8},{2,10},{4,12},{6,14},{8,0},{10,2},{12,4},{14,6},{16,24},{18,... | collective-permute-start | bytes 1622024 | tf_op jit(solution)/shard_map/ppermute | solution.py:399
  104.5 2.4 %collective-permute-start.15 = (bf16[1,2048,128]{2,1,0:T(8,128)(2,1)S(1)}, bf16[1,2048,128]{2,1,0:T(8,128)(2,1)S(1)}, u32[]{:S(2)}, u32[]{:S(2)}) collective-permute-start(bf16[1,2048,128]{2,1,0:T(8,128)(2,1)S(1)} %constant_dynamic-slice_fusion), channel_id=1, source_target_pairs={{0,2},{2,0},{4,6},{6,4},{8,10},{10,8},{12,14},{14,12},{16,18},{18,... | collective-permute-start | bytes 1572872 | tf_op jit(solution)/shard_map/ppermute | solution.py:399
  110.6 8.7 %collective-permute-start.18 = (bf16[512,256]{1,0:T(8,128)(2,1)S(1)}, bf16[512,256]{1,0:T(8,128)(2,1)S(1)}, u32[]{:S(2)}, u32[]{:S(2)}) collective-permute-start(bf16[512,256]{1,0:T(8,128)(2,1)S(1)} %slice.55), channel_id=1, source_target_pairs={{0,1},{1,0},{2,3},{3,2},{4,5},{5,4},{6,7},{7,6},{8,9},{9,8},{10,11... | collective-permute-start | bytes 786440 | tf_op jit(solution)/shard_map/ppermute | solution.py:402
  (7 other events, 27.5 us)

commit v3 on v2

--- a/solution.py
+++ b/solution.py
@@ -441,8 +441,7 @@
         hands.append([start, start + 1])
     for k in (1, 0):
         hands.append([z * GROUP + (place ^ k) for z in range(planes)])
-    *pieces, column, own = deal(cache, hands, gain, 56 * 2**20)
-    pieces = dict(zip(offsets, pieces))
+    pieces = dict(zip(offsets, deal(cache, hands[:1], gain, 56 * 2**20)))
 
     def with_fill(value, d):
         rows = jnp.concatenate([slot_fill[d], slot_fill[d ^ 1]], axis=0)
@@ -467,11 +466,13 @@
     query_here = projection(normed_here, flat[:, :cols]).astype(bf16)
     far_here[first] = swap(with_fill(query_here, first), first * GROUP)
     far_here[1] = swap(with_fill(query_here, 1), GROUP)
-    beside = swap(column, 1)
     normed_rest = norm(ordered(jnp.concatenate(others, axis=0), query_here))
     query_rest = projection(normed_rest, flat[:, :cols]).astype(bf16)
     far_rest[first] = swap(query_rest, first * GROUP)
-    across[second] = swap(ordered(pieces[second], query_rest, beside), 2)
+    *rest, column, own = deal(cache, hands[1:], query_rest, 56 * 2**20)
+    pieces |= zip(offsets[1:], rest)
+    across[second] = swap(pieces[second], 2)
+    beside = swap(column, 1)
     projected = projection(
         jnp.concatenate([normed_here, normed_rest], axis=0), ordered(flat, query_rest)[:, cols:]
     )

time: 121 us -> 118 us (0.975)
  waiting for transfers between devices: 36.9 us -> 32.8 us
  starting transfers between devices: 19.3 us -> 23.4 us
  other arithmetic: 7.39 us -> 4.09 us
  Pallas kernels: 44.7 us -> 47.3 us
    ppermute x17, waiting for transfers between devices: 28.6 us -> 25.5 us  [swap(): return lax.ppermute(value, 'req', [(i, i ^ step) for i in range(devices)])]
    pallas_call x4 -> x5, Pallas kernels: 8.1 us -> 10.7 us  [deal(): pl.pallas_call(functools.partial(deal_kernel, counts), out_shape=[jax.Sha...]
    ppermute x3, starting transfers between devices: 3.56 us -> 5.77 us  [turn(): lax.ppermute(value, 'head', [(i, (i - step) % n_head) for i in range(n_he...]
    ppermute x17, starting transfers between devices: 15.7 us -> 17.6 us  [swap(): return lax.ppermute(value, 'req', [(i, i ^ step) for i in range(devices)])]
  transfers between devices with their start and end apart: 20 -> 20, of which waited for: 9 -> 9; matrix products, arithmetic and copies ran while one was open for 13% -> 9% of each run, Pallas kernels for 37% -> 40%
where the time goes in v3:
time: 118 us
  Pallas kernels  47.3 us (40%)
  waiting for transfers between devices  32.8 us (28%)
  starting transfers between devices  23.4 us (20%)
  matrix products  6.51 us (6%)
  other arithmetic  4.09 us (3%)
  local copies, waits for them, and re-layouts  2.21 us (2%)
  between operations  1.78 us (2%)
    pallas_call x6, Pallas kernels, cache_attention(): pl.pallas_call(functools.partial(cache_kernel, (span, heads, count, fill_...  25.9 us
    ppermute x17, waiting for transfers between devices, swap(): return lax.ppermute(value, 'req', [(i, i ^ step) for i in range(devices)])  25.5 us
    ppermute x17, starting transfers between devices, swap(): return lax.ppermute(value, 'req', [(i, i ^ step) for i in range(devices)])  17.6 us
    pallas_call x5, Pallas kernels, deal(): pl.pallas_call(functools.partial(deal_kernel, counts), out_shape=[jax.Sha...  10.7 us
    ppermute x3, waiting for transfers between devices, turn(): lax.ppermute(value, 'head', [(i, (i - step) % n_head) for i in range(n_he...  7.23 us
    dot_general x5, matrix products, dot(): lax.dot_general(left, right, (contract, ((), ())), precision=precision, p...  6.51 us
    pallas_call x1, Pallas kernels, memory_pass(): pl.pallas_call(functools.partial(memory_kernel, count), out_shape=(jax.Sh...  5.97 us
    ppermute x3, starting transfers between devices, turn(): lax.ppermute(value, 'head', [(i, (i - step) % n_head) for i in range(n_he...  5.77 us
  transfers between devices with their start and end apart: 20, of which 9 were waited for; matrix products, arithmetic and copies ran while one was open for 9% of the time, Pallas kernels for 40%

profile of v3, /device:TPU:0, one launch (start us, length us, event | category | flops | bytes accessed | tf_op | source)
XLA Modules:
  0.0 118.0 jit_solution(5691132094224565304)
XLA Ops:
  0.6 3.0 %collective-permute-start = (bf16[256,1024]{1,0:T(8,128)(2,1)}, bf16[256,1024]{1,0:T(8,128)(2,1)S(1)}, u32[]{:S(2)}, u32[]{:S(2)}) collective-permute-start(bf16[256,1024]{1,0:T(8,128)(2,1)} %bitcast.63), channel_id=1, source_target_pairs={{0,1},{1,0},{2,3},{3,2},{4,5},{5,4},{6,7},{7,6},{8,9},{9,8},{10,11... | collective-permute-start | bytes 1572872 | tf_op jit(solution)/shard_map/ppermute | solution.py:402
  4.3 3.3 %shard_map.149 = bf16[2,2048,128]{2,1,0:T(8,128)(2,1)} custom-call(s32[2]{0:T(128)} %pad_add_fusion.3.at_ref, bf16[16,2048,128]{2,1,0:T(8,128)(2,1)} %bitcast.57, bf16[1024]{0:T(1024)(128)(2,1)} %after_ref.7), custom_call_target="tpu_custom_call" | custom-call | flops 1 | bytes 1 | tf_op jit(solution)/shard_map/pallas_call | solution.py:70
  7.5 1.6 %collective-permute-start.4 = (bf16[2,2048,128]{2,1,0:T(8,128)(2,1)}, bf16[2,2048,128]{2,1,0:T(8,128)(2,1)S(1)}, u32[]{:S(2)}, u32[]{:S(2)}) collective-permute-start(bf16[2,2048,128]{2,1,0:T(8,128)(2,1)} %shard_map.149), channel_id=1, source_target_pairs={{0,4},{2,6},{4,0},{6,2},{8,12},{10,14},{12,8},{14,10},{16,20},{18,... | collective-permute-start | bytes 3145736 | tf_op jit(solution)/shard_map/ppermute | solution.py:399
  9.3 1.4 %copy.23 = bf16[128,8,4,512]{3,1,2,0:T(8,128)(2,1)S(1)} copy(bf16[128,8,4,512]{3,2,1,0:T(4,128)(2,1)S(1)} %bitcast.59) | data formatting | bytes 8388608
  12.8 2.7 %collective-permute-start.1 = (bf16[544,256]{1,0:T(8,128)(2,1)S(1)}, bf16[544,256]{1,0:T(8,128)(2,1)S(1)}, u32[]{:S(2)}, u32[]{:S(2)}) collective-permute-start(bf16[544,256]{1,0:T(8,128)(2,1)S(1)} %pad_maximum_fusion.1), channel_id=1, source_target_pairs={{0,16},{2,18},{4,20},{6,22},{8,24},{10,26},{12,28},{14,30},{16,0},... | collective-permute-start | bytes 835592 | tf_op jit(solution)/shard_map/ppermute | solution.py:399
  16.2 1.6 %collective-permute-start.9 = (bf16[528,256]{1,0:T(8,128)(2,1)}, bf16[528,256]{1,0:T(8,128)(2,1)}, u32[]{:S(2)}, u32[]{:S(2)}) collective-permute-start(bf16[528,256]{1,0:T(8,128)(2,1)} %pad_maximum_fusion.2), channel_id=1, source_target_pairs={{0,8},{2,10},{4,12},{6,14},{8,0},{10,2},{12,4},{14,6},{16,24},{18,... | collective-permute-start | bytes 811016 | tf_op jit(solution)/shard_map/ppermute | solution.py:399
  18.7 2.4 %convolution_convert_fusion.2.after_ref = bf16[512,256]{1,0:T(8,128)(2,1)} fusion(bf16[256,1024]{1,0:T(8,128)(2,1)S(1)} %fusion.14, bf16[1024,2048]{1,0:T(8,128)(2,1)} %bitcast.61), kind=kOutput, calls=%fused_computation.13 | convolution fusion | flops 268566528 | bytes 1835008 | tf_op jit(solution)/shard_map/dot_general | solution.py:30
  21.2 7.2 %shard_map.152 = (bf16[2,2048,128]{2,1,0:T(8,128)(2,1)}, bf16[2,2048,128]{2,1,0:T(8,128)(2,1)}, bf16[2,2048,128]{2,1,0:T(8,128)(2,1)}, bf16[4,2048,128]{2,1,0:T(8,128)(2,1)}, bf16[4,2048,128]{2,1,0:T(8,128)(2,1)}) custom-call(s32[14]{0:T(128)} %stack.119.at_ref, bf16[16,2048,128]{2,1,0:T(8,128)(2,1)} %bitcast.58, ...), custom_call_target="tpu_custom_call" | custom-call | flops 1 | bytes 1 | tf_op jit(solution)/shard_map/pallas_call | solution.py:70
  29.1 1.9 %fusion.38 = (bf16[1536,512]{1,0:T(8,128)(2,1)S(1)}, f32[1536,512]{1,0:T(8,128)S(1)}) fusion(bf16[256,1024]{1,0:T(8,128)(2,1)S(1)} %fusion.14, bf16[256,1024]{1,0:T(8,128)(2,1)S(1)} %fusion.11, bf16[1024,2048]{1,0:T(8,128)(2,1)S(1)} %bitcast.62), kind=kOutput, calls=%fused_computation.74 | convolution fusion | flops 1613496320 | bytes 8912896 | tf_op jit(solution)/shard_map/dot_general | solution.py:30
  31.1 1.5 %collective-permute-start.7 = (bf16[2,2048,128]{2,1,0:T(8,128)(2,1)S(1)}, bf16[2,2048,128]{2,1,0:T(8,128)(2,1)S(1)}, u32[]{:S(2)}, u32[]{:S(2)}) collective-permute-start(bf16[2,2048,128]{2,1,0:T(8,128)(2,1)S(1)} %copy-done.16), channel_id=1, source_target_pairs={{0,4},{2,6},{4,0},{6,2},{8,12},{10,14},{12,8},{14,10},{16,20},{18,... | collective-permute-start | bytes 3145736 | tf_op jit(solution)/shard_map/ppermute | solution.py:399
  32.7 3.3 %shard_map.150 = (f32[4,128,512]{2,1,0:T(8,128)S(1)}, f32[4,1,512]{2,1,0:T(1,128)S(1)}) custom-call(s32[1]{0:T(128)} %bitcast.side_ref, bf16[512,512]{1,0:T(8,128)(2,1)S(1)} %pad_maximum_fusion.q_ref, bf16[512,512]{1,0:T(8,128)(2,1)S(1)} %get-tuple-element.59.k_ref, bf16[512,512]{1,0:T(8,128)(2,1)S(1)} %get-tuple-element.58.v_ref, ...), custom_call_target="tpu_custom_call" | custom-call | flops 1 | bytes 1 | tf_op jit(solution)/shard_map/pallas_call | solution.py:231
  36.0 1.6 %collective-permute-start.10 = (bf16[512,256]{1,0:T(8,128)(2,1)S(1)}, bf16[512,256]{1,0:T(8,128)(2,1)S(1)}, u32[]{:S(2)}, u32[]{:S(2)}) collective-permute-start(bf16[512,256]{1,0:T(8,128)(2,1)S(1)} %copy-done.12), channel_id=1, source_target_pairs={{0,8},{2,10},{4,12},{6,14},{8,0},{10,2},{12,4},{14,6},{16,24},{18,... | collective-permute-start | bytes 786440 | tf_op jit(solution)/shard_map/ppermute | solution.py:399
  37.8 6.2 %collective-permute-done.2 = bf16[512,256]{1,0:T(8,128)(2,1)S(1)} collective-permute-done((bf16[512,256]{1,0:T(8,128)(2,1)S(1)}, bf16[512,256]{1,0:T(8,128)(2,1)S(1)}, u32[]{:S(2)}, u32[]{:S(2)}) %collective-permute-start.2) | collective-permute-done | bytes 262176 | tf_op jit(solution)/shard_map/ppermute | solution.py:399
  44.6 4.9 %collective-permute-done.10 = bf16[512,256]{1,0:T(8,128)(2,1)S(1)} collective-permute-done((bf16[512,256]{1,0:T(8,128)(2,1)S(1)}, bf16[512,256]{1,0:T(8,128)(2,1)S(1)}, u32[]{:S(2)}, u32[]{:S(2)}) %collective-permute-start.10) | collective-permute-done | bytes 262176 | tf_op jit(solution)/shard_map/ppermute | solution.py:399
  50.6 5.8 %shard_map.154.after_ref = bf16[528,512]{1,0:T(8,128)(2,1)S(1)} custom-call(s32[4]{0:T(128)S(1)} %pad_add_fusion.at_ref, f32[8,128]{1,0:T(8,128)S(1)} %shard_map.151.after_ref, bf16[544,512]{1,0:T(8,128)(2,1)S(1)} %fusion.20.q_ref.fill_ref, bf16[544,512]{1,0:T(8,128)(2,1)S(1)} %fusion.20.q_ref.fill_ref, bf16[4,2048,128]{2,1,0:T(8,128)(2,1)S(1)} %copy-done, ...), custom_call_target="tpu_custom_call" | custom-call | flops 1 | bytes 1 | tf_op jit(solution)/shard_map/pallas_call | solution.py:176
  56.4 2.0 %collective-permute-start.13 = (bf16[528,512]{1,0:T(8,128)(2,1)S(1)}, bf16[528,512]{1,0:T(8,128)(2,1)S(1)}, u32[]{:S(2)}, u32[]{:S(2)}) collective-permute-start(bf16[528,512]{1,0:T(8,128)(2,1)S(1)} %shard_map.154.after_ref), channel_id=1, source_target_pairs={{0,16},{2,18},{4,20},{6,22},{8,24},{10,26},{12,28},{14,30},{16,0},... | collective-permute-start | bytes 1622024 | tf_op jit(solution)/shard_map/ppermute | solution.py:399
  58.5 6.0 %shard_map.155 = (f32[512,512]{1,0:T(8,128)S(1)}, f32[2,4,128,128]{3,2,1,0:T(8,128)}) custom-call(s32[1]{0:T(128)} %bitcast.side_ref, f32[1,4]{1,0:T(1,128)S(1)} %copy-done.4, f32[1,4]{1,0:T(1,128)S(1)} %copy-done.5, f32[1,4]{1,0:T(1,128)S(1)} %copy-done.6, s32[1,8]{1,0:T(1,128)S(1)} %copy-done.7, bf16[528,512]{1,0:T(8,128)(2,1)S(1)} %shard_map.154.after_ref, ...), custom_call_target="tpu_custom_call" | custom-call | flops 1 | bytes 1 | tf_op jit(solution)/shard_map/pallas_call | solution.py:307
  64.6 1.5 %collective-permute-start.14 = (bf16[2,2048,128]{2,1,0:T(8,128)(2,1)S(1)}, bf16[2,2048,128]{2,1,0:T(8,128)(2,1)S(1)}, u32[]{:S(2)}, u32[]{:S(2)}) collective-permute-start(bf16[2,2048,128]{2,1,0:T(8,128)(2,1)S(1)} %copy-done.14), channel_id=1, source_target_pairs={{0,4},{2,6},{4,0},{6,2},{8,12},{10,14},{12,8},{14,10},{16,20},{18,... | collective-permute-start | bytes 3145736 | tf_op jit(solution)/shard_map/ppermute | solution.py:399
  66.1 1.7 %collective-permute-done.6.q_ref.fill_ref = bf16[544,512]{1,0:T(8,128)(2,1)S(1)} collective-permute-done((bf16[544,512]{1,0:T(8,128)(2,1)S(1)}, bf16[544,512]{1,0:T(8,128)(2,1)S(1)}, u32[]{:S(2)}, u32[]{:S(2)}) %collective-permute-start.6) | collective-permute-done | bytes 557088 | tf_op jit(solution)/shard_map/ppermute | solution.py:399
  67.8 5.8 %shard_map.158.refs_0_ = bf16[528,512]{1,0:T(8,128)(2,1)S(1)} custom-call(s32[4]{0:T(128)S(1)} %pad_add_fusion.1.at_ref, f32[8,128]{1,0:T(8,128)S(1)} %shard_map.156.after_ref, bf16[544,512]{1,0:T(8,128)(2,1)S(1)} %collective-permute-done.6.q_ref.fill_ref, bf16[544,512]{1,0:T(8,128)(2,1)S(1)} %collective-permute-done.6.q_ref.fill_ref, ...), custom_call_target="tpu_custom_call" | custom-call | flops 1 | bytes 1 | tf_op jit(solution)/shard_map/pallas_call | solution.py:176
  73.6 2.4 %collective-permute-start.16 = (bf16[528,512]{1,0:T(8,128)(2,1)S(1)}, bf16[528,512]{1,0:T(8,128)(2,1)S(1)}, u32[]{:S(2)}, u32[]{:S(2)}) collective-permute-start(bf16[528,512]{1,0:T(8,128)(2,1)S(1)} %shard_map.158.refs_0_), channel_id=1, source_target_pairs={{0,24},{2,26},{4,28},{6,30},{8,16},{10,18},{12,20},{14,22},{16,8},... | collective-permute-start | bytes 1622024 | tf_op jit(solution)/shard_map/ppermute | solution.py:399
  76.0 3.6 %collective-permute-done.11.from_ref.refs_2_ = bf16[2,2048,128]{2,1,0:T(8,128)(2,1)S(1)} collective-permute-done((bf16[2,2048,128]{2,1,0:T(8,128)(2,1)S(1)}, bf16[2,2048,128]{2,1,0:T(8,128)(2,1)S(1)}, u32[]{:S(2)}, u32[]{:S(2)}) %collective-permute-start.11) | collective-permute-done | bytes 1048608 | tf_op jit(solution)/shard_map/ppermute | solution.py:399
  79.8 1.5 %collective-permute-start.19 = (bf16[512,1024]{1,0:T(8,128)(2,1)S(1)}, bf16[512,1024]{1,0:T(8,128)(2,1)S(1)}, u32[]{:S(2)}, u32[]{:S(2)}) collective-permute-start(bf16[512,1024]{1,0:T(8,128)(2,1)S(1)} %copy-done.13), channel_id=1, source_target_pairs={{0,1},{1,0},{2,3},{3,2},{4,5},{5,4},{6,7},{7,6},{8,9},{9,8},{10,11... | collective-permute-start | bytes 3145736 | tf_op jit(solution)/shard_map/ppermute | solution.py:402
  81.7 5.8 %shard_map.161.after_ref = bf16[528,512]{1,0:T(8,128)(2,1)S(1)} custom-call(s32[4]{0:T(128)S(1)} %pad_add_fusion.2.at_ref, f32[8,128]{1,0:T(8,128)S(1)} %shard_map.159.after_ref, bf16[528,512]{1,0:T(8,128)(2,1)S(1)} %fusion.21.q_ref.fill_ref, bf16[528,512]{1,0:T(8,128)(2,1)S(1)} %fusion.21.q_ref.fill_ref, bf16[4,2048,128]{2,1,0:T(8,128)(2,1)S(1)} %copy-done, ...), custom_call_target="tpu_custom_call" | custom-call | flops 1 | bytes 1 | tf_op jit(solution)/shard_map/pallas_call | solution.py:176
  87.5 1.6 %collective-permute-start.17 = (bf16[528,512]{1,0:T(8,128)(2,1)S(1)}, bf16[528,512]{1,0:T(8,128)(2,1)S(1)}, u32[]{:S(2)}, u32[]{:S(2)}) collective-permute-start(bf16[528,512]{1,0:T(8,128)(2,1)S(1)} %shard_map.161.after_ref), channel_id=1, source_target_pairs={{0,8},{2,10},{4,12},{6,14},{8,0},{10,2},{12,4},{14,6},{16,24},{18,... | collective-permute-start | bytes 1622024 | tf_op jit(solution)/shard_map/ppermute | solution.py:399
  89.1 3.9 %shard_map.162 = (f32[4,128,512]{2,1,0:T(8,128)S(1)}, f32[4,1,512]{2,1,0:T(1,128)S(1)}) custom-call(s32[2]{0:T(128)S(1)} %pad_add_fusion.4.at_ref, bf16[528,512]{1,0:T(8,128)(2,1)S(1)} %shard_map.161.after_ref, bf16[512,512]{1,0:T(8,128)(2,1)S(1)} %pad_maximum_fusion.q_ref, bf16[16,128]{1,0:T(8,128)(2,1)S(1)} %pad.27.fill_ref, ...), custom_call_target="tpu_custom_call" | custom-call | flops 1 | bytes 1 | tf_op jit(solution)/shard_map/pallas_call | solution.py:176
  93.0 2.8 %collective-permute-done.13.refs_1_.refs_8_.refs_9_ = bf16[528,512]{1,0:T(8,128)(2,1)S(1)} collective-permute-done((bf16[528,512]{1,0:T(8,128)(2,1)S(1)}, bf16[528,512]{1,0:T(8,128)(2,1)S(1)}, u32[]{:S(2)}, u32[]{:S(2)}) %collective-permute-start.13) | collective-permute-done | bytes 540704 | tf_op jit(solution)/shard_map/ppermute | solution.py:399
  95.8 5.6 %collective-permute-done.14.refs_0_ = bf16[2,2048,128]{2,1,0:T(8,128)(2,1)S(1)} collective-permute-done((bf16[2,2048,128]{2,1,0:T(8,128)(2,1)S(1)}, bf16[2,2048,128]{2,1,0:T(8,128)(2,1)S(1)}, u32[]{:S(2)}, u32[]{:S(2)}) %collective-permute-start.14) | collective-permute-done | bytes 1048608 | tf_op jit(solution)/shard_map/ppermute | solution.py:399
  101.5 2.3 %shard_map.164 = (f32[4,128,512]{2,1,0:T(8,128)S(1)}, f32[4,1,512]{2,1,0:T(1,128)S(1)}) custom-call(s32[1]{0:T(128)} %bitcast.9.at_ref, f32[8,128]{1,0:T(8,128)S(1)} %shard_map.163.after_ref, bf16[512,512]{1,0:T(8,128)(2,1)S(1)} %pad_maximum_fusion.q_ref, bf16[16,128]{1,0:T(8,128)(2,1)S(1)} %pad.27.fill_ref, ...), custom_call_target="tpu_custom_call" | custom-call | flops 1 | bytes 1 | tf_op jit(solution)/shard_map/pallas_call | solution.py:176
  103.8 2.3 %shard_map.165 = (f32[4,128,512]{2,1,0:T(8,128)S(1)}, f32[4,1,512]{2,1,0:T(1,128)S(1)}) custom-call(s32[1]{0:T(128)} %constant.82.clone.1.at_ref, f32[4,1,512]{2,1,0:T(1,128)S(1)} %get-tuple-element.48.after_ref.refs_5_, bf16[512,512]{1,0:T(8,128)(2,1)S(1)} %pad_maximum_fusion.q_ref, bf16[16,128]{1,0:T(8,128)(2,1)S(1)} %pad.27.fill_ref, ...), custom_call_target="tpu_custom_call" | custom-call | flops 1 | bytes 1 | tf_op jit(solution)/shard_map/pallas_call | solution.py:176
  106.4 1.4 %shard_map.166 = bf16[512,512]{1,0:T(8,128)(2,1)S(1)} custom-call(f32[4,128,512]{2,1,0:T(8,128)S(1)} %get-tuple-element.31.refs_0_, f32[4,1,512]{2,1,0:T(1,128)S(1)} %get-tuple-element.32.refs_0_.refs_1_, f32[4,128,512]{2,1,0:T(8,128)S(1)} %get-tuple-element.43.refs_2_, f32[4,1,512]{2,1,0:T(1,128)S(1)} %get-tuple-element.44.refs_0_.refs_3_, ...), custom_call_target="tpu_custom_call" | custom-call | flops 18350080 | bytes 8388608 | tf_op jit(solution)/shard_map/pallas_call | solution.py:352
  109.0 7.2 %collective-permute-done.18 = bf16[512,256]{1,0:T(8,128)(2,1)S(1)} collective-permute-done((bf16[512,256]{1,0:T(8,128)(2,1)S(1)}, bf16[512,256]{1,0:T(8,128)(2,1)S(1)}, u32[]{:S(2)}, u32[]{:S(2)}) %collective-permute-start.18) | collective-permute-done | bytes 262176 | tf_op jit(solution)/shard_map/ppermute | solution.py:402
  (103 shorter events, 10.6 us)
Async XLA Ops:
  0.6 17.7 %collective-permute-start = (bf16[256,1024]{1,0:T(8,128)(2,1)}, bf16[256,1024]{1,0:T(8,128)(2,1)S(1)}, u32[]{:S(2)}, u32[]{:S(2)}) collective-permute-start(bf16[256,1024]{1,0:T(8,128)(2,1)} %bitcast.63), channel_id=1, source_target_pairs={{0,1},{1,0},{2,3},{3,2},{4,5},{5,4},{6,7},{7,6},{8,9},{9,8},{10,11... | collective-permute-start | bytes 1572872 | tf_op jit(solution)/shard_map/ppermute | solution.py:402
  7.5 28.4 %collective-permute-start.4 = (bf16[2,2048,128]{2,1,0:T(8,128)(2,1)}, bf16[2,2048,128]{2,1,0:T(8,128)(2,1)S(1)}, u32[]{:S(2)}, u32[]{:S(2)}) collective-permute-start(bf16[2,2048,128]{2,1,0:T(8,128)(2,1)} %shard_map.149), channel_id=1, source_target_pairs={{0,4},{2,6},{4,0},{6,2},{8,12},{10,14},{12,8},{14,10},{16,20},{18,... | collective-permute-start | bytes 3145736 | tf_op jit(solution)/shard_map/ppermute | solution.py:399
  10.7 5.4 %copy-start.9 = (bf16[128,8,4,512]{3,1,2,0:T(8,128)(2,1)}, bf16[128,8,4,512]{3,1,2,0:T(8,128)(2,1)S(1)}, u32[]{:S(2)}) copy-start(bf16[128,8,4,512]{3,1,2,0:T(8,128)(2,1)S(1)} %copy.23) | copy-start | bytes 12582916
  12.8 24.9 %collective-permute-start.1 = (bf16[544,256]{1,0:T(8,128)(2,1)S(1)}, bf16[544,256]{1,0:T(8,128)(2,1)S(1)}, u32[]{:S(2)}, u32[]{:S(2)}) collective-permute-start(bf16[544,256]{1,0:T(8,128)(2,1)S(1)} %pad_maximum_fusion.1), channel_id=1, source_target_pairs={{0,16},{2,18},{4,20},{6,22},{8,24},{10,26},{12,28},{14,30},{16,0},... | collective-permute-start | bytes 835592 | tf_op jit(solution)/shard_map/ppermute | solution.py:399
  16.2 14.9 %collective-permute-start.9 = (bf16[528,256]{1,0:T(8,128)(2,1)}, bf16[528,256]{1,0:T(8,128)(2,1)}, u32[]{:S(2)}, u32[]{:S(2)}) collective-permute-start(bf16[528,256]{1,0:T(8,128)(2,1)} %pad_maximum_fusion.2), channel_id=1, source_target_pairs={{0,8},{2,10},{4,12},{6,14},{8,0},{10,2},{12,4},{14,6},{16,24},{18,... | collective-permute-start | bytes 811016 | tf_op jit(solution)/shard_map/ppermute | solution.py:399
  21.2 7.6 %copy-start.12 = (bf16[512,256]{1,0:T(8,128)(2,1)S(1)}, bf16[512,256]{1,0:T(8,128)(2,1)}, u32[]{:S(2)}) copy-start(bf16[512,256]{1,0:T(8,128)(2,1)} %convolution_convert_fusion.2.after_ref) | copy-start | bytes 786436
  21.2 8.0 %copy-start.10 = (bf16[128,8,4,512]{3,1,2,0:T(8,128)(2,1)S(1)}, bf16[128,8,4,512]{3,1,2,0:T(8,128)(2,1)}, u32[]{:S(2)}) copy-start(bf16[128,8,4,512]{3,1,2,0:T(8,128)(2,1)} %copy-done.9) | copy-start | bytes 12582916
  28.4 22.2 %collective-permute-start.3 = (bf16[4,2048,128]{2,1,0:T(8,128)(2,1)}, bf16[4,2048,128]{2,1,0:T(8,128)(2,1)S(1)}, u32[]{:S(2)}, u32[]{:S(2)}) collective-permute-start(bf16[4,2048,128]{2,1,0:T(8,128)(2,1)} %get-tuple-element.34), channel_id=1, source_target_pairs={{0,2},{2,0},{4,6},{6,4},{8,10},{10,8},{12,14},{14,12},{16,18},{18,... | collective-permute-start | bytes 6291464 | tf_op jit(solution)/shard_map/ppermute | solution.py:399
  28.8 15.2 %collective-permute-start.2 = (bf16[512,256]{1,0:T(8,128)(2,1)S(1)}, bf16[512,256]{1,0:T(8,128)(2,1)S(1)}, u32[]{:S(2)}, u32[]{:S(2)}) collective-permute-start(bf16[512,256]{1,0:T(8,128)(2,1)S(1)} %copy-done.12), channel_id=1, source_target_pairs={{0,16},{2,18},{4,20},{6,22},{8,24},{10,26},{12,28},{14,30},{16,0},... | collective-permute-start | bytes 786440 | tf_op jit(solution)/shard_map/ppermute | solution.py:399
  31.1 33.3 %collective-permute-start.7 = (bf16[2,2048,128]{2,1,0:T(8,128)(2,1)S(1)}, bf16[2,2048,128]{2,1,0:T(8,128)(2,1)S(1)}, u32[]{:S(2)}, u32[]{:S(2)}) collective-permute-start(bf16[2,2048,128]{2,1,0:T(8,128)(2,1)S(1)} %copy-done.16), channel_id=1, source_target_pairs={{0,4},{2,6},{4,0},{6,2},{8,12},{10,14},{12,8},{14,10},{16,20},{18,... | collective-permute-start | bytes 3145736 | tf_op jit(solution)/shard_map/ppermute | solution.py:399
  32.6 11.4 %copy-start.15 = (bf16[2,2048,128]{2,1,0:T(8,128)(2,1)S(1)}, bf16[2,2048,128]{2,1,0:T(8,128)(2,1)}, u32[]{:S(2)}) copy-start(bf16[2,2048,128]{2,1,0:T(8,128)(2,1)} %get-tuple-element.41) | copy-start | bytes 3145732
  36.0 13.6 %collective-permute-start.10 = (bf16[512,256]{1,0:T(8,128)(2,1)S(1)}, bf16[512,256]{1,0:T(8,128)(2,1)S(1)}, u32[]{:S(2)}, u32[]{:S(2)}) collective-permute-start(bf16[512,256]{1,0:T(8,128)(2,1)S(1)} %copy-done.12), channel_id=1, source_target_pairs={{0,8},{2,10},{4,12},{6,14},{8,0},{10,2},{12,4},{14,6},{16,24},{18,... | collective-permute-start | bytes 786440 | tf_op jit(solution)/shard_map/ppermute | solution.py:399
  37.7 12.8 %collective-permute-start.5 = (bf16[1,2048,128]{2,1,0:T(8,128)(2,1)S(1)}, bf16[1,2048,128]{2,1,0:T(8,128)(2,1)S(1)}, u32[]{:S(2)}, u32[]{:S(2)}) collective-permute-start(bf16[1,2048,128]{2,1,0:T(8,128)(2,1)S(1)} %shard_map.153), channel_id=1, source_target_pairs={{0,2},{2,0},{4,6},{6,4},{8,10},{10,8},{12,14},{14,12},{16,18},{18,... | collective-permute-start | bytes 1572872 | tf_op jit(solution)/shard_map/ppermute | solution.py:399
  44.0 35.6 %collective-permute-start.11 = (bf16[2,2048,128]{2,1,0:T(8,128)(2,1)S(1)}, bf16[2,2048,128]{2,1,0:T(8,128)(2,1)S(1)}, u32[]{:S(2)}, u32[]{:S(2)}) collective-permute-start(bf16[2,2048,128]{2,1,0:T(8,128)(2,1)S(1)} %copy-done.15), channel_id=1, source_target_pairs={{0,4},{2,6},{4,0},{6,2},{8,12},{10,14},{12,8},{14,10},{16,20},{18,... | collective-permute-start | bytes 3145736 | tf_op jit(solution)/shard_map/ppermute | solution.py:399
  44.5 6.0 %copy-start = (bf16[4,2048,128]{2,1,0:T(8,128)(2,1)S(1)}, bf16[4,2048,128]{2,1,0:T(8,128)(2,1)}, u32[]{:S(2)}) copy-start(bf16[4,2048,128]{2,1,0:T(8,128)(2,1)} %get-tuple-element.33.refs_0_) | copy-start | bytes 6291460
  49.5 18.3 %collective-permute-start.6 = (bf16[544,512]{1,0:T(8,128)(2,1)S(1)}, bf16[544,512]{1,0:T(8,128)(2,1)S(1)}, u32[]{:S(2)}, u32[]{:S(2)}) collective-permute-start(bf16[544,512]{1,0:T(8,128)(2,1)S(1)} %fusion.20.q_ref.fill_ref), channel_id=1, source_target_pairs={{0,8},{2,10},{4,12},{6,14},{8,0},{10,2},{12,4},{14,6},{16,24},{18,... | collective-permute-start | bytes 1671176 | tf_op jit(solution)/shard_map/ppermute | solution.py:399
  50.5 7.9 %copy-start.1 = (f32[2,1,4,128,128]{4,3,2,1,0:T(8,128)S(1)}, f32[2,1,4,128,128]{4,3,2,1,0:T(8,128)}, u32[]{:S(2)}) copy-start(f32[2,1,4,128,128]{4,3,2,1,0:T(8,128)} %param.23) | copy-start | bytes 1572868
  50.6 7.9 %copy-start.4 = (f32[1,4]{1,0:T(1,128)S(1)}, f32[1,4]{1,0:T(1,128)}, u32[]{:S(2)}) copy-start(f32[1,4]{1,0:T(1,128)} %retention_ref.1) | copy-start | bytes 52
  50.6 7.9 %copy-start.5 = (f32[1,4]{1,0:T(1,128)S(1)}, f32[1,4]{1,0:T(1,128)}, u32[]{:S(2)}) copy-start(f32[1,4]{1,0:T(1,128)} %momentum_ref.1) | copy-start | bytes 52
  50.6 7.8 %copy-start.6 = (f32[1,4]{1,0:T(1,128)S(1)}, f32[1,4]{1,0:T(1,128)}, u32[]{:S(2)}) copy-start(f32[1,4]{1,0:T(1,128)} %step_ref.1) | copy-start | bytes 52
  50.6 7.8 %copy-start.7 = (s32[1,8]{1,0:T(1,128)S(1)}, s32[1,8]{1,0:T(1,128)}, u32[]{:S(2)}) copy-start(s32[1,8]{1,0:T(1,128)} %halving_ref.1) | copy-start | bytes 100
  56.4 39.4 %collective-permute-start.13 = (bf16[528,512]{1,0:T(8,128)(2,1)S(1)}, bf16[528,512]{1,0:T(8,128)(2,1)S(1)}, u32[]{:S(2)}, u32[]{:S(2)}) collective-permute-start(bf16[528,512]{1,0:T(8,128)(2,1)S(1)} %shard_map.154.after_ref), channel_id=1, source_target_pairs={{0,16},{2,18},{4,20},{6,22},{8,24},{10,26},{12,28},{14,30},{16,0},... | collective-permute-start | bytes 1622024 | tf_op jit(solution)/shard_map/ppermute | solution.py:399
  58.4 6.2 %copy-start.14 = (bf16[2,2048,128]{2,1,0:T(8,128)(2,1)S(1)}, bf16[2,2048,128]{2,1,0:T(8,128)(2,1)}, u32[]{:S(2)}) copy-start(bf16[2,2048,128]{2,1,0:T(8,128)(2,1)} %get-tuple-element.46) | copy-start | bytes 3145732
  64.5 3.3 %collective-permute-start.8 = (bf16[1,2048,128]{2,1,0:T(8,128)(2,1)S(1)}, bf16[1,2048,128]{2,1,0:T(8,128)(2,1)S(1)}, u32[]{:S(2)}, u32[]{:S(2)}) collective-permute-start(bf16[1,2048,128]{2,1,0:T(8,128)(2,1)S(1)} %shard_map.157), channel_id=1, source_target_pairs={{0,2},{2,0},{4,6},{6,4},{8,10},{10,8},{12,14},{14,12},{16,18},{18,... | collective-permute-start | bytes 1572872 | tf_op jit(solution)/shard_map/ppermute | solution.py:399
  64.6 36.8 %collective-permute-start.14 = (bf16[2,2048,128]{2,1,0:T(8,128)(2,1)S(1)}, bf16[2,2048,128]{2,1,0:T(8,128)(2,1)S(1)}, u32[]{:S(2)}, u32[]{:S(2)}) collective-permute-start(bf16[2,2048,128]{2,1,0:T(8,128)(2,1)S(1)} %copy-done.14), channel_id=1, source_target_pairs={{0,4},{2,6},{4,0},{6,2},{8,12},{10,14},{12,8},{14,10},{16,20},{18,... | collective-permute-start | bytes 3145736 | tf_op jit(solution)/shard_map/ppermute | solution.py:399
  66.1 13.7 %copy-start.13 = (bf16[512,1024]{1,0:T(8,128)(2,1)S(1)}, bf16[512,1024]{1,0:T(8,128)(2,1)}, u32[]{:S(2)}) copy-start(bf16[512,1024]{1,0:T(8,128)(2,1)} %param.17) | copy-start | bytes 3145732
  73.6 32.5 %collective-permute-start.16 = (bf16[528,512]{1,0:T(8,128)(2,1)S(1)}, bf16[528,512]{1,0:T(8,128)(2,1)S(1)}, u32[]{:S(2)}, u32[]{:S(2)}) collective-permute-start(bf16[528,512]{1,0:T(8,128)(2,1)S(1)} %shard_map.158.refs_0_), channel_id=1, source_target_pairs={{0,24},{2,26},{4,28},{6,30},{8,16},{10,18},{12,20},{14,22},{16,8},... | collective-permute-start | bytes 1622024 | tf_op jit(solution)/shard_map/ppermute | solution.py:399
  79.7 2.0 %collective-permute-start.12 = (bf16[1,2048,128]{2,1,0:T(8,128)(2,1)S(1)}, bf16[1,2048,128]{2,1,0:T(8,128)(2,1)S(1)}, u32[]{:S(2)}, u32[]{:S(2)}) collective-permute-start(bf16[1,2048,128]{2,1,0:T(8,128)(2,1)S(1)} %shard_map.160), channel_id=1, source_target_pairs={{0,2},{2,0},{4,6},{6,4},{8,10},{10,8},{12,14},{14,12},{16,18},{18,... | collective-permute-start | bytes 1572872 | tf_op jit(solution)/shard_map/ppermute | solution.py:399
  79.8 29.2 %collective-permute-start.19 = (bf16[512,1024]{1,0:T(8,128)(2,1)S(1)}, bf16[512,1024]{1,0:T(8,128)(2,1)S(1)}, u32[]{:S(2)}, u32[]{:S(2)}) collective-permute-start(bf16[512,1024]{1,0:T(8,128)(2,1)S(1)} %copy-done.13), channel_id=1, source_target_pairs={{0,1},{1,0},{2,3},{3,2},{4,5},{5,4},{6,7},{7,6},{8,9},{9,8},{10,11... | collective-permute-start | bytes 3145736 | tf_op jit(solution)/shard_map/ppermute | solution.py:402
  87.5 18.9 %collective-permute-start.17 = (bf16[528,512]{1,0:T(8,128)(2,1)S(1)}, bf16[528,512]{1,0:T(8,128)(2,1)S(1)}, u32[]{:S(2)}, u32[]{:S(2)}) collective-permute-start(bf16[528,512]{1,0:T(8,128)(2,1)S(1)} %shard_map.161.after_ref), channel_id=1, source_target_pairs={{0,8},{2,10},{4,12},{6,14},{8,0},{10,2},{12,4},{14,6},{16,24},{18,... | collective-permute-start | bytes 1622024 | tf_op jit(solution)/shard_map/ppermute | solution.py:399
  101.4 2.4 %collective-permute-start.15 = (bf16[1,2048,128]{2,1,0:T(8,128)(2,1)S(1)}, bf16[1,2048,128]{2,1,0:T(8,128)(2,1)S(1)}, u32[]{:S(2)}, u32[]{:S(2)}) collective-permute-start(bf16[1,2048,128]{2,1,0:T(8,128)(2,1)S(1)} %constant_dynamic-slice_fusion), channel_id=1, source_target_pairs={{0,2},{2,0},{4,6},{6,4},{8,10},{10,8},{12,14},{14,12},{16,18},{18,... | collective-permute-start | bytes 1572872 | tf_op jit(solution)/shard_map/ppermute | solution.py:399
  107.8 8.5 %collective-permute-start.18 = (bf16[512,256]{1,0:T(8,128)(2,1)S(1)}, bf16[512,256]{1,0:T(8,128)(2,1)S(1)}, u32[]{:S(2)}, u32[]{:S(2)}) collective-permute-start(bf16[512,256]{1,0:T(8,128)(2,1)S(1)} %slice.55), channel_id=1, source_target_pairs={{0,1},{1,0},{2,3},{3,2},{4,5},{5,4},{6,7},{7,6},{8,9},{9,8},{10,11... | collective-permute-start | bytes 786440 | tf_op jit(solution)/shard_map/ppermute | solution.py:402
  (7 other events, 23.2 us)

commit v4 on v3

--- a/solution.py
+++ b/solution.py
@@ -114,7 +114,7 @@
             column = filled[:, fill_row + g : fill_row + g + 1]
             bias_ref[pl.ds(g * span, span), :] = jnp.where(row_f < column, 0.0, MASKED)
             copies[g].wait()
-            wide_ref[g] = kept_ref[g].astype(f32)
+            wide_ref[g, pl.ds(0, 2 * heads * span), :] = kept_ref[g].astype(f32)
 
     def part_of(g, which):
         rows = pl.ds(2 * head + which, span, stride=2 * heads)
@@ -188,7 +188,7 @@
             out_specs=out_specs,
             scratch_shapes=[
                 pltpu.VMEM((count,) + kvs[0].shape[1:], bf16),
-                pltpu.VMEM((count,) + kvs[0].shape[1:], f32),
+                pltpu.VMEM((count, 2 * heads * (span + 1), HD), f32),
                 pltpu.VMEM((count * span, HD), f32),
                 pltpu.VMEM((count * span, tokens), f32),
                 pltpu.VMEM((TAIL, tokens), f32),

time: 118 us -> 118 us (level)
  no operation moved by 1% of the time
where the time goes in v4:
time: 118 us
  Pallas kernels  47.3 us (40%)
  waiting for transfers between devices  32.8 us (28%)
  starting transfers between devices  23.4 us (20%)
  matrix products  6.51 us (6%)
  other arithmetic  4.09 us (3%)
  local copies, waits for them, and re-layouts  2.21 us (2%)
  between operations  1.78 us (2%)
    pallas_call x6, Pallas kernels, cache_attention(): pl.pallas_call(functools.partial(cache_kernel, (span, heads, count, fill_...  25.9 us
    ppermute x17, waiting for transfers between devices, swap(): return lax.ppermute(value, 'req', [(i, i ^ step) for i in range(devices)])  25.5 us
    ppermute x17, starting transfers between devices, swap(): return lax.ppermute(value, 'req', [(i, i ^ step) for i in range(devices)])  17.6 us
    pallas_call x5, Pallas kernels, deal(): pl.pallas_call(functools.partial(deal_kernel, counts), out_shape=[jax.Sha...  10.7 us
    ppermute x3, waiting for transfers between devices, turn(): lax.ppermute(value, 'head', [(i, (i - step) % n_head) for i in range(n_he...  7.23 us
    dot_general x5, matrix products, dot(): lax.dot_general(left, right, (contract, ((), ())), precision=precision, p...  6.51 us
    pallas_call x1, Pallas kernels, memory_pass(): pl.pallas_call(functools.partial(memory_kernel, count), out_shape=(jax.Sh...  5.97 us
    ppermute x3, starting transfers between devices, turn(): lax.ppermute(value, 'head', [(i, (i - step) % n_head) for i in range(n_he...  5.77 us
  transfers between devices with their start and end apart: 20, of which 9 were waited for; matrix products, arithmetic and copies ran while one was open for 9% of the time, Pallas kernels for 40%

profile of v4, /device:TPU:0, one launch (start us, length us, event | category | flops | bytes accessed | tf_op | source)
XLA Modules:
  0.0 118.0 jit_solution(46491567322559852)
XLA Ops:
  0.6 3.0 %collective-permute-start = (bf16[256,1024]{1,0:T(8,128)(2,1)}, bf16[256,1024]{1,0:T(8,128)(2,1)S(1)}, u32[]{:S(2)}, u32[]{:S(2)}) collective-permute-start(bf16[256,1024]{1,0:T(8,128)(2,1)} %bitcast.63), channel_id=1, source_target_pairs={{0,1},{1,0},{2,3},{3,2},{4,5},{5,4},{6,7},{7,6},{8,9},{9,8},{10,11... | collective-permute-start | bytes 1572872 | tf_op jit(solution)/shard_map/ppermute | solution.py:402
  4.3 3.3 %shard_map.149 = bf16[2,2048,128]{2,1,0:T(8,128)(2,1)} custom-call(s32[2]{0:T(128)} %pad_add_fusion.3.at_ref, bf16[16,2048,128]{2,1,0:T(8,128)(2,1)} %bitcast.57, bf16[1024]{0:T(1024)(128)(2,1)} %after_ref.7), custom_call_target="tpu_custom_call" | custom-call | flops 1 | bytes 1 | tf_op jit(solution)/shard_map/pallas_call | solution.py:70
  7.5 1.6 %collective-permute-start.4 = (bf16[2,2048,128]{2,1,0:T(8,128)(2,1)}, bf16[2,2048,128]{2,1,0:T(8,128)(2,1)S(1)}, u32[]{:S(2)}, u32[]{:S(2)}) collective-permute-start(bf16[2,2048,128]{2,1,0:T(8,128)(2,1)} %shard_map.149), channel_id=1, source_target_pairs={{0,4},{2,6},{4,0},{6,2},{8,12},{10,14},{12,8},{14,10},{16,20},{18,... | collective-permute-start | bytes 3145736 | tf_op jit(solution)/shard_map/ppermute | solution.py:399
  9.3 1.4 %copy.23 = bf16[128,8,4,512]{3,1,2,0:T(8,128)(2,1)S(1)} copy(bf16[128,8,4,512]{3,2,1,0:T(4,128)(2,1)S(1)} %bitcast.59) | data formatting | bytes 8388608
  12.8 2.7 %collective-permute-start.1 = (bf16[544,256]{1,0:T(8,128)(2,1)S(1)}, bf16[544,256]{1,0:T(8,128)(2,1)S(1)}, u32[]{:S(2)}, u32[]{:S(2)}) collective-permute-start(bf16[544,256]{1,0:T(8,128)(2,1)S(1)} %pad_maximum_fusion.1), channel_id=1, source_target_pairs={{0,16},{2,18},{4,20},{6,22},{8,24},{10,26},{12,28},{14,30},{16,0},... | collective-permute-start | bytes 835592 | tf_op jit(solution)/shard_map/ppermute | solution.py:399
  16.2 1.6 %collective-permute-start.9 = (bf16[528,256]{1,0:T(8,128)(2,1)}, bf16[528,256]{1,0:T(8,128)(2,1)}, u32[]{:S(2)}, u32[]{:S(2)}) collective-permute-start(bf16[528,256]{1,0:T(8,128)(2,1)} %pad_maximum_fusion.2), channel_id=1, source_target_pairs={{0,8},{2,10},{4,12},{6,14},{8,0},{10,2},{12,4},{14,6},{16,24},{18,... | collective-permute-start | bytes 811016 | tf_op jit(solution)/shard_map/ppermute | solution.py:399
  18.7 2.4 %convolution_convert_fusion.2.after_ref = bf16[512,256]{1,0:T(8,128)(2,1)} fusion(bf16[256,1024]{1,0:T(8,128)(2,1)S(1)} %fusion.14, bf16[1024,2048]{1,0:T(8,128)(2,1)} %bitcast.61), kind=kOutput, calls=%fused_computation.13 | convolution fusion | flops 268566528 | bytes 1835008 | tf_op jit(solution)/shard_map/dot_general | solution.py:30
  21.2 7.2 %shard_map.152 = (bf16[2,2048,128]{2,1,0:T(8,128)(2,1)}, bf16[2,2048,128]{2,1,0:T(8,128)(2,1)}, bf16[2,2048,128]{2,1,0:T(8,128)(2,1)}, bf16[4,2048,128]{2,1,0:T(8,128)(2,1)}, bf16[4,2048,128]{2,1,0:T(8,128)(2,1)}) custom-call(s32[14]{0:T(128)} %stack.119.at_ref, bf16[16,2048,128]{2,1,0:T(8,128)(2,1)} %bitcast.58, ...), custom_call_target="tpu_custom_call" | custom-call | flops 1 | bytes 1 | tf_op jit(solution)/shard_map/pallas_call | solution.py:70
  29.1 1.9 %fusion.38 = (bf16[1536,512]{1,0:T(8,128)(2,1)S(1)}, f32[1536,512]{1,0:T(8,128)S(1)}) fusion(bf16[256,1024]{1,0:T(8,128)(2,1)S(1)} %fusion.14, bf16[256,1024]{1,0:T(8,128)(2,1)S(1)} %fusion.11, bf16[1024,2048]{1,0:T(8,128)(2,1)S(1)} %bitcast.62), kind=kOutput, calls=%fused_computation.74 | convolution fusion | flops 1613496320 | bytes 8912896 | tf_op jit(solution)/shard_map/dot_general | solution.py:30
  31.1 1.5 %collective-permute-start.7 = (bf16[2,2048,128]{2,1,0:T(8,128)(2,1)S(1)}, bf16[2,2048,128]{2,1,0:T(8,128)(2,1)S(1)}, u32[]{:S(2)}, u32[]{:S(2)}) collective-permute-start(bf16[2,2048,128]{2,1,0:T(8,128)(2,1)S(1)} %copy-done.16), channel_id=1, source_target_pairs={{0,4},{2,6},{4,0},{6,2},{8,12},{10,14},{12,8},{14,10},{16,20},{18,... | collective-permute-start | bytes 3145736 | tf_op jit(solution)/shard_map/ppermute | solution.py:399
  32.7 3.3 %shard_map.150 = (f32[4,128,512]{2,1,0:T(8,128)S(1)}, f32[4,1,512]{2,1,0:T(1,128)S(1)}) custom-call(s32[1]{0:T(128)} %bitcast.side_ref, bf16[512,512]{1,0:T(8,128)(2,1)S(1)} %pad_maximum_fusion.q_ref, bf16[512,512]{1,0:T(8,128)(2,1)S(1)} %get-tuple-element.59.k_ref, bf16[512,512]{1,0:T(8,128)(2,1)S(1)} %get-tuple-element.58.v_ref, ...), custom_call_target="tpu_custom_call" | custom-call | flops 1 | bytes 1 | tf_op jit(solution)/shard_map/pallas_call | solution.py:231
  36.0 1.6 %collective-permute-start.10 = (bf16[512,256]{1,0:T(8,128)(2,1)S(1)}, bf16[512,256]{1,0:T(8,128)(2,1)S(1)}, u32[]{:S(2)}, u32[]{:S(2)}) collective-permute-start(bf16[512,256]{1,0:T(8,128)(2,1)S(1)} %copy-done.12), channel_id=1, source_target_pairs={{0,8},{2,10},{4,12},{6,14},{8,0},{10,2},{12,4},{14,6},{16,24},{18,... | collective-permute-start | bytes 786440 | tf_op jit(solution)/shard_map/ppermute | solution.py:399
  37.8 6.2 %collective-permute-done.2 = bf16[512,256]{1,0:T(8,128)(2,1)S(1)} collective-permute-done((bf16[512,256]{1,0:T(8,128)(2,1)S(1)}, bf16[512,256]{1,0:T(8,128)(2,1)S(1)}, u32[]{:S(2)}, u32[]{:S(2)}) %collective-permute-start.2) | collective-permute-done | bytes 262176 | tf_op jit(solution)/shard_map/ppermute | solution.py:399
  44.6 4.9 %collective-permute-done.10 = bf16[512,256]{1,0:T(8,128)(2,1)S(1)} collective-permute-done((bf16[512,256]{1,0:T(8,128)(2,1)S(1)}, bf16[512,256]{1,0:T(8,128)(2,1)S(1)}, u32[]{:S(2)}, u32[]{:S(2)}) %collective-permute-start.10) | collective-permute-done | bytes 262176 | tf_op jit(solution)/shard_map/ppermute | solution.py:399
  50.6 5.8 %shard_map.154.after_ref = bf16[528,512]{1,0:T(8,128)(2,1)S(1)} custom-call(s32[4]{0:T(128)S(1)} %pad_add_fusion.at_ref, f32[8,128]{1,0:T(8,128)S(1)} %shard_map.151.after_ref, bf16[544,512]{1,0:T(8,128)(2,1)S(1)} %fusion.20.q_ref.fill_ref, bf16[544,512]{1,0:T(8,128)(2,1)S(1)} %fusion.20.q_ref.fill_ref, bf16[4,2048,128]{2,1,0:T(8,128)(2,1)S(1)} %copy-done, ...), custom_call_target="tpu_custom_call" | custom-call | flops 1 | bytes 1 | tf_op jit(solution)/shard_map/pallas_call | solution.py:176
  56.4 2.0 %collective-permute-start.13 = (bf16[528,512]{1,0:T(8,128)(2,1)S(1)}, bf16[528,512]{1,0:T(8,128)(2,1)S(1)}, u32[]{:S(2)}, u32[]{:S(2)}) collective-permute-start(bf16[528,512]{1,0:T(8,128)(2,1)S(1)} %shard_map.154.after_ref), channel_id=1, source_target_pairs={{0,16},{2,18},{4,20},{6,22},{8,24},{10,26},{12,28},{14,30},{16,0},... | collective-permute-start | bytes 1622024 | tf_op jit(solution)/shard_map/ppermute | solution.py:399
  58.5 6.0 %shard_map.155 = (f32[512,512]{1,0:T(8,128)S(1)}, f32[2,4,128,128]{3,2,1,0:T(8,128)}) custom-call(s32[1]{0:T(128)} %bitcast.side_ref, f32[1,4]{1,0:T(1,128)S(1)} %copy-done.4, f32[1,4]{1,0:T(1,128)S(1)} %copy-done.5, f32[1,4]{1,0:T(1,128)S(1)} %copy-done.6, s32[1,8]{1,0:T(1,128)S(1)} %copy-done.7, bf16[528,512]{1,0:T(8,128)(2,1)S(1)} %shard_map.154.after_ref, ...), custom_call_target="tpu_custom_call" | custom-call | flops 1 | bytes 1 | tf_op jit(solution)/shard_map/pallas_call | solution.py:307
  64.6 1.5 %collective-permute-start.14 = (bf16[2,2048,128]{2,1,0:T(8,128)(2,1)S(1)}, bf16[2,2048,128]{2,1,0:T(8,128)(2,1)S(1)}, u32[]{:S(2)}, u32[]{:S(2)}) collective-permute-start(bf16[2,2048,128]{2,1,0:T(8,128)(2,1)S(1)} %copy-done.14), channel_id=1, source_target_pairs={{0,4},{2,6},{4,0},{6,2},{8,12},{10,14},{12,8},{14,10},{16,20},{18,... | collective-permute-start | bytes 3145736 | tf_op jit(solution)/shard_map/ppermute | solution.py:399
  66.1 1.7 %collective-permute-done.6.q_ref.fill_ref = bf16[544,512]{1,0:T(8,128)(2,1)S(1)} collective-permute-done((bf16[544,512]{1,0:T(8,128)(2,1)S(1)}, bf16[544,512]{1,0:T(8,128)(2,1)S(1)}, u32[]{:S(2)}, u32[]{:S(2)}) %collective-permute-start.6) | collective-permute-done | bytes 557088 | tf_op jit(solution)/shard_map/ppermute | solution.py:399
  67.8 5.8 %shard_map.158.refs_0_ = bf16[528,512]{1,0:T(8,128)(2,1)S(1)} custom-call(s32[4]{0:T(128)S(1)} %pad_add_fusion.1.at_ref, f32[8,128]{1,0:T(8,128)S(1)} %shard_map.156.after_ref, bf16[544,512]{1,0:T(8,128)(2,1)S(1)} %collective-permute-done.6.q_ref.fill_ref, bf16[544,512]{1,0:T(8,128)(2,1)S(1)} %collective-permute-done.6.q_ref.fill_ref, ...), custom_call_target="tpu_custom_call" | custom-call | flops 1 | bytes 1 | tf_op jit(solution)/shard_map/pallas_call | solution.py:176
  73.6 2.4 %collective-permute-start.16 = (bf16[528,512]{1,0:T(8,128)(2,1)S(1)}, bf16[528,512]{1,0:T(8,128)(2,1)S(1)}, u32[]{:S(2)}, u32[]{:S(2)}) collective-permute-start(bf16[528,512]{1,0:T(8,128)(2,1)S(1)} %shard_map.158.refs_0_), channel_id=1, source_target_pairs={{0,24},{2,26},{4,28},{6,30},{8,16},{10,18},{12,20},{14,22},{16,8},... | collective-permute-start | bytes 1622024 | tf_op jit(solution)/shard_map/ppermute | solution.py:399
  76.0 3.6 %collective-permute-done.11.from_ref.refs_2_ = bf16[2,2048,128]{2,1,0:T(8,128)(2,1)S(1)} collective-permute-done((bf16[2,2048,128]{2,1,0:T(8,128)(2,1)S(1)}, bf16[2,2048,128]{2,1,0:T(8,128)(2,1)S(1)}, u32[]{:S(2)}, u32[]{:S(2)}) %collective-permute-start.11) | collective-permute-done | bytes 1048608 | tf_op jit(solution)/shard_map/ppermute | solution.py:399
  79.8 1.5 %collective-permute-start.19 = (bf16[512,1024]{1,0:T(8,128)(2,1)S(1)}, bf16[512,1024]{1,0:T(8,128)(2,1)S(1)}, u32[]{:S(2)}, u32[]{:S(2)}) collective-permute-start(bf16[512,1024]{1,0:T(8,128)(2,1)S(1)} %copy-done.13), channel_id=1, source_target_pairs={{0,1},{1,0},{2,3},{3,2},{4,5},{5,4},{6,7},{7,6},{8,9},{9,8},{10,11... | collective-permute-start | bytes 3145736 | tf_op jit(solution)/shard_map/ppermute | solution.py:402
  81.7 5.8 %shard_map.161.after_ref = bf16[528,512]{1,0:T(8,128)(2,1)S(1)} custom-call(s32[4]{0:T(128)S(1)} %pad_add_fusion.2.at_ref, f32[8,128]{1,0:T(8,128)S(1)} %shard_map.159.after_ref, bf16[528,512]{1,0:T(8,128)(2,1)S(1)} %fusion.21.q_ref.fill_ref, bf16[528,512]{1,0:T(8,128)(2,1)S(1)} %fusion.21.q_ref.fill_ref, bf16[4,2048,128]{2,1,0:T(8,128)(2,1)S(1)} %copy-done, ...), custom_call_target="tpu_custom_call" | custom-call | flops 1 | bytes 1 | tf_op jit(solution)/shard_map/pallas_call | solution.py:176
  87.5 1.6 %collective-permute-start.17 = (bf16[528,512]{1,0:T(8,128)(2,1)S(1)}, bf16[528,512]{1,0:T(8,128)(2,1)S(1)}, u32[]{:S(2)}, u32[]{:S(2)}) collective-permute-start(bf16[528,512]{1,0:T(8,128)(2,1)S(1)} %shard_map.161.after_ref), channel_id=1, source_target_pairs={{0,8},{2,10},{4,12},{6,14},{8,0},{10,2},{12,4},{14,6},{16,24},{18,... | collective-permute-start | bytes 1622024 | tf_op jit(solution)/shard_map/ppermute | solution.py:399
  89.1 3.9 %shard_map.162 = (f32[4,128,512]{2,1,0:T(8,128)S(1)}, f32[4,1,512]{2,1,0:T(1,128)S(1)}) custom-call(s32[2]{0:T(128)S(1)} %pad_add_fusion.4.at_ref, bf16[528,512]{1,0:T(8,128)(2,1)S(1)} %shard_map.161.after_ref, bf16[512,512]{1,0:T(8,128)(2,1)S(1)} %pad_maximum_fusion.q_ref, bf16[16,128]{1,0:T(8,128)(2,1)S(1)} %pad.27.fill_ref, ...), custom_call_target="tpu_custom_call" | custom-call | flops 1 | bytes 1 | tf_op jit(solution)/shard_map/pallas_call | solution.py:176
  93.0 2.8 %collective-permute-done.13.refs_1_.refs_8_.refs_9_ = bf16[528,512]{1,0:T(8,128)(2,1)S(1)} collective-permute-done((bf16[528,512]{1,0:T(8,128)(2,1)S(1)}, bf16[528,512]{1,0:T(8,128)(2,1)S(1)}, u32[]{:S(2)}, u32[]{:S(2)}) %collective-permute-start.13) | collective-permute-done | bytes 540704 | tf_op jit(solution)/shard_map/ppermute | solution.py:399
  95.8 5.6 %collective-permute-done.14.refs_0_ = bf16[2,2048,128]{2,1,0:T(8,128)(2,1)S(1)} collective-permute-done((bf16[2,2048,128]{2,1,0:T(8,128)(2,1)S(1)}, bf16[2,2048,128]{2,1,0:T(8,128)(2,1)S(1)}, u32[]{:S(2)}, u32[]{:S(2)}) %collective-permute-start.14) | collective-permute-done | bytes 1048608 | tf_op jit(solution)/shard_map/ppermute | solution.py:399
  101.5 2.3 %shard_map.164 = (f32[4,128,512]{2,1,0:T(8,128)S(1)}, f32[4,1,512]{2,1,0:T(1,128)S(1)}) custom-call(s32[1]{0:T(128)} %bitcast.9.at_ref, f32[8,128]{1,0:T(8,128)S(1)} %shard_map.163.after_ref, bf16[512,512]{1,0:T(8,128)(2,1)S(1)} %pad_maximum_fusion.q_ref, bf16[16,128]{1,0:T(8,128)(2,1)S(1)} %pad.27.fill_ref, ...), custom_call_target="tpu_custom_call" | custom-call | flops 1 | bytes 1 | tf_op jit(solution)/shard_map/pallas_call | solution.py:176
  103.8 2.3 %shard_map.165 = (f32[4,128,512]{2,1,0:T(8,128)S(1)}, f32[4,1,512]{2,1,0:T(1,128)S(1)}) custom-call(s32[1]{0:T(128)} %constant.82.clone.1.at_ref, f32[4,1,512]{2,1,0:T(1,128)S(1)} %get-tuple-element.48.after_ref.refs_5_, bf16[512,512]{1,0:T(8,128)(2,1)S(1)} %pad_maximum_fusion.q_ref, bf16[16,128]{1,0:T(8,128)(2,1)S(1)} %pad.27.fill_ref, ...), custom_call_target="tpu_custom_call" | custom-call | flops 1 | bytes 1 | tf_op jit(solution)/shard_map/pallas_call | solution.py:176
  106.4 1.4 %shard_map.166 = bf16[512,512]{1,0:T(8,128)(2,1)S(1)} custom-call(f32[4,128,512]{2,1,0:T(8,128)S(1)} %get-tuple-element.31.refs_0_, f32[4,1,512]{2,1,0:T(1,128)S(1)} %get-tuple-element.32.refs_0_.refs_1_, f32[4,128,512]{2,1,0:T(8,128)S(1)} %get-tuple-element.43.refs_2_, f32[4,1,512]{2,1,0:T(1,128)S(1)} %get-tuple-element.44.refs_0_.refs_3_, ...), custom_call_target="tpu_custom_call" | custom-call | flops 18350080 | bytes 8388608 | tf_op jit(solution)/shard_map/pallas_call | solution.py:352
  109.0 7.2 %collective-permute-done.18 = bf16[512,256]{1,0:T(8,128)(2,1)S(1)} collective-permute-done((bf16[512,256]{1,0:T(8,128)(2,1)S(1)}, bf16[512,256]{1,0:T(8,128)(2,1)S(1)}, u32[]{:S(2)}, u32[]{:S(2)}) %collective-permute-start.18) | collective-permute-done | bytes 262176 | tf_op jit(solution)/shard_map/ppermute | solution.py:402
  (103 shorter events, 10.6 us)
Async XLA Ops:
  0.6 17.7 %collective-permute-start = (bf16[256,1024]{1,0:T(8,128)(2,1)}, bf16[256,1024]{1,0:T(8,128)(2,1)S(1)}, u32[]{:S(2)}, u32[]{:S(2)}) collective-permute-start(bf16[256,1024]{1,0:T(8,128)(2,1)} %bitcast.63), channel_id=1, source_target_pairs={{0,1},{1,0},{2,3},{3,2},{4,5},{5,4},{6,7},{7,6},{8,9},{9,8},{10,11... | collective-permute-start | bytes 1572872 | tf_op jit(solution)/shard_map/ppermute | solution.py:402
  7.5 28.4 %collective-permute-start.4 = (bf16[2,2048,128]{2,1,0:T(8,128)(2,1)}, bf16[2,2048,128]{2,1,0:T(8,128)(2,1)S(1)}, u32[]{:S(2)}, u32[]{:S(2)}) collective-permute-start(bf16[2,2048,128]{2,1,0:T(8,128)(2,1)} %shard_map.149), channel_id=1, source_target_pairs={{0,4},{2,6},{4,0},{6,2},{8,12},{10,14},{12,8},{14,10},{16,20},{18,... | collective-permute-start | bytes 3145736 | tf_op jit(solution)/shard_map/ppermute | solution.py:399
  10.7 5.4 %copy-start.9 = (bf16[128,8,4,512]{3,1,2,0:T(8,128)(2,1)}, bf16[128,8,4,512]{3,1,2,0:T(8,128)(2,1)S(1)}, u32[]{:S(2)}) copy-start(bf16[128,8,4,512]{3,1,2,0:T(8,128)(2,1)S(1)} %copy.23) | copy-start | bytes 12582916
  12.8 24.9 %collective-permute-start.1 = (bf16[544,256]{1,0:T(8,128)(2,1)S(1)}, bf16[544,256]{1,0:T(8,128)(2,1)S(1)}, u32[]{:S(2)}, u32[]{:S(2)}) collective-permute-start(bf16[544,256]{1,0:T(8,128)(2,1)S(1)} %pad_maximum_fusion.1), channel_id=1, source_target_pairs={{0,16},{2,18},{4,20},{6,22},{8,24},{10,26},{12,28},{14,30},{16,0},... | collective-permute-start | bytes 835592 | tf_op jit(solution)/shard_map/ppermute | solution.py:399
  16.2 14.9 %collective-permute-start.9 = (bf16[528,256]{1,0:T(8,128)(2,1)}, bf16[528,256]{1,0:T(8,128)(2,1)}, u32[]{:S(2)}, u32[]{:S(2)}) collective-permute-start(bf16[528,256]{1,0:T(8,128)(2,1)} %pad_maximum_fusion.2), channel_id=1, source_target_pairs={{0,8},{2,10},{4,12},{6,14},{8,0},{10,2},{12,4},{14,6},{16,24},{18,... | collective-permute-start | bytes 811016 | tf_op jit(solution)/shard_map/ppermute | solution.py:399
  21.2 7.6 %copy-start.12 = (bf16[512,256]{1,0:T(8,128)(2,1)S(1)}, bf16[512,256]{1,0:T(8,128)(2,1)}, u32[]{:S(2)}) copy-start(bf16[512,256]{1,0:T(8,128)(2,1)} %convolution_convert_fusion.2.after_ref) | copy-start | bytes 786436
  21.2 8.0 %copy-start.10 = (bf16[128,8,4,512]{3,1,2,0:T(8,128)(2,1)S(1)}, bf16[128,8,4,512]{3,1,2,0:T(8,128)(2,1)}, u32[]{:S(2)}) copy-start(bf16[128,8,4,512]{3,1,2,0:T(8,128)(2,1)} %copy-done.9) | copy-start | bytes 12582916
  28.4 22.2 %collective-permute-start.3 = (bf16[4,2048,128]{2,1,0:T(8,128)(2,1)}, bf16[4,2048,128]{2,1,0:T(8,128)(2,1)S(1)}, u32[]{:S(2)}, u32[]{:S(2)}) collective-permute-start(bf16[4,2048,128]{2,1,0:T(8,128)(2,1)} %get-tuple-element.34), channel_id=1, source_target_pairs={{0,2},{2,0},{4,6},{6,4},{8,10},{10,8},{12,14},{14,12},{16,18},{18,... | collective-permute-start | bytes 6291464 | tf_op jit(solution)/shard_map/ppermute | solution.py:399
  28.8 15.2 %collective-permute-start.2 = (bf16[512,256]{1,0:T(8,128)(2,1)S(1)}, bf16[512,256]{1,0:T(8,128)(2,1)S(1)}, u32[]{:S(2)}, u32[]{:S(2)}) collective-permute-start(bf16[512,256]{1,0:T(8,128)(2,1)S(1)} %copy-done.12), channel_id=1, source_target_pairs={{0,16},{2,18},{4,20},{6,22},{8,24},{10,26},{12,28},{14,30},{16,0},... | collective-permute-start | bytes 786440 | tf_op jit(solution)/shard_map/ppermute | solution.py:399
  31.1 33.3 %collective-permute-start.7 = (bf16[2,2048,128]{2,1,0:T(8,128)(2,1)S(1)}, bf16[2,2048,128]{2,1,0:T(8,128)(2,1)S(1)}, u32[]{:S(2)}, u32[]{:S(2)}) collective-permute-start(bf16[2,2048,128]{2,1,0:T(8,128)(2,1)S(1)} %copy-done.16), channel_id=1, source_target_pairs={{0,4},{2,6},{4,0},{6,2},{8,12},{10,14},{12,8},{14,10},{16,20},{18,... | collective-permute-start | bytes 3145736 | tf_op jit(solution)/shard_map/ppermute | solution.py:399
  32.6 11.4 %copy-start.15 = (bf16[2,2048,128]{2,1,0:T(8,128)(2,1)S(1)}, bf16[2,2048,128]{2,1,0:T(8,128)(2,1)}, u32[]{:S(2)}) copy-start(bf16[2,2048,128]{2,1,0:T(8,128)(2,1)} %get-tuple-element.41) | copy-start | bytes 3145732
  36.0 13.6 %collective-permute-start.10 = (bf16[512,256]{1,0:T(8,128)(2,1)S(1)}, bf16[512,256]{1,0:T(8,128)(2,1)S(1)}, u32[]{:S(2)}, u32[]{:S(2)}) collective-permute-start(bf16[512,256]{1,0:T(8,128)(2,1)S(1)} %copy-done.12), channel_id=1, source_target_pairs={{0,8},{2,10},{4,12},{6,14},{8,0},{10,2},{12,4},{14,6},{16,24},{18,... | collective-permute-start | bytes 786440 | tf_op jit(solution)/shard_map/ppermute | solution.py:399
  37.7 12.8 %collective-permute-start.5 = (bf16[1,2048,128]{2,1,0:T(8,128)(2,1)S(1)}, bf16[1,2048,128]{2,1,0:T(8,128)(2,1)S(1)}, u32[]{:S(2)}, u32[]{:S(2)}) collective-permute-start(bf16[1,2048,128]{2,1,0:T(8,128)(2,1)S(1)} %shard_map.153), channel_id=1, source_target_pairs={{0,2},{2,0},{4,6},{6,4},{8,10},{10,8},{12,14},{14,12},{16,18},{18,... | collective-permute-start | bytes 1572872 | tf_op jit(solution)/shard_map/ppermute | solution.py:399
  44.0 35.6 %collective-permute-start.11 = (bf16[2,2048,128]{2,1,0:T(8,128)(2,1)S(1)}, bf16[2,2048,128]{2,1,0:T(8,128)(2,1)S(1)}, u32[]{:S(2)}, u32[]{:S(2)}) collective-permute-start(bf16[2,2048,128]{2,1,0:T(8,128)(2,1)S(1)} %copy-done.15), channel_id=1, source_target_pairs={{0,4},{2,6},{4,0},{6,2},{8,12},{10,14},{12,8},{14,10},{16,20},{18,... | collective-permute-start | bytes 3145736 | tf_op jit(solution)/shard_map/ppermute | solution.py:399
  44.5 6.0 %copy-start = (bf16[4,2048,128]{2,1,0:T(8,128)(2,1)S(1)}, bf16[4,2048,128]{2,1,0:T(8,128)(2,1)}, u32[]{:S(2)}) copy-start(bf16[4,2048,128]{2,1,0:T(8,128)(2,1)} %get-tuple-element.33.refs_0_) | copy-start | bytes 6291460
  49.5 18.3 %collective-permute-start.6 = (bf16[544,512]{1,0:T(8,128)(2,1)S(1)}, bf16[544,512]{1,0:T(8,128)(2,1)S(1)}, u32[]{:S(2)}, u32[]{:S(2)}) collective-permute-start(bf16[544,512]{1,0:T(8,128)(2,1)S(1)} %fusion.20.q_ref.fill_ref), channel_id=1, source_target_pairs={{0,8},{2,10},{4,12},{6,14},{8,0},{10,2},{12,4},{14,6},{16,24},{18,... | collective-permute-start | bytes 1671176 | tf_op jit(solution)/shard_map/ppermute | solution.py:399
  50.5 7.9 %copy-start.1 = (f32[2,1,4,128,128]{4,3,2,1,0:T(8,128)S(1)}, f32[2,1,4,128,128]{4,3,2,1,0:T(8,128)}, u32[]{:S(2)}) copy-start(f32[2,1,4,128,128]{4,3,2,1,0:T(8,128)} %param.23) | copy-start | bytes 1572868
  50.6 7.9 %copy-start.4 = (f32[1,4]{1,0:T(1,128)S(1)}, f32[1,4]{1,0:T(1,128)}, u32[]{:S(2)}) copy-start(f32[1,4]{1,0:T(1,128)} %retention_ref.1) | copy-start | bytes 52
  50.6 7.9 %copy-start.5 = (f32[1,4]{1,0:T(1,128)S(1)}, f32[1,4]{1,0:T(1,128)}, u32[]{:S(2)}) copy-start(f32[1,4]{1,0:T(1,128)} %momentum_ref.1) | copy-start | bytes 52
  50.6 7.8 %copy-start.6 = (f32[1,4]{1,0:T(1,128)S(1)}, f32[1,4]{1,0:T(1,128)}, u32[]{:S(2)}) copy-start(f32[1,4]{1,0:T(1,128)} %step_ref.1) | copy-start | bytes 52
  50.6 7.8 %copy-start.7 = (s32[1,8]{1,0:T(1,128)S(1)}, s32[1,8]{1,0:T(1,128)}, u32[]{:S(2)}) copy-start(s32[1,8]{1,0:T(1,128)} %halving_ref.1) | copy-start | bytes 100
  56.4 39.4 %collective-permute-start.13 = (bf16[528,512]{1,0:T(8,128)(2,1)S(1)}, bf16[528,512]{1,0:T(8,128)(2,1)S(1)}, u32[]{:S(2)}, u32[]{:S(2)}) collective-permute-start(bf16[528,512]{1,0:T(8,128)(2,1)S(1)} %shard_map.154.after_ref), channel_id=1, source_target_pairs={{0,16},{2,18},{4,20},{6,22},{8,24},{10,26},{12,28},{14,30},{16,0},... | collective-permute-start | bytes 1622024 | tf_op jit(solution)/shard_map/ppermute | solution.py:399
  58.4 6.2 %copy-start.14 = (bf16[2,2048,128]{2,1,0:T(8,128)(2,1)S(1)}, bf16[2,2048,128]{2,1,0:T(8,128)(2,1)}, u32[]{:S(2)}) copy-start(bf16[2,2048,128]{2,1,0:T(8,128)(2,1)} %get-tuple-element.46) | copy-start | bytes 3145732
  64.5 3.3 %collective-permute-start.8 = (bf16[1,2048,128]{2,1,0:T(8,128)(2,1)S(1)}, bf16[1,2048,128]{2,1,0:T(8,128)(2,1)S(1)}, u32[]{:S(2)}, u32[]{:S(2)}) collective-permute-start(bf16[1,2048,128]{2,1,0:T(8,128)(2,1)S(1)} %shard_map.157), channel_id=1, source_target_pairs={{0,2},{2,0},{4,6},{6,4},{8,10},{10,8},{12,14},{14,12},{16,18},{18,... | collective-permute-start | bytes 1572872 | tf_op jit(solution)/shard_map/ppermute | solution.py:399
  64.6 36.8 %collective-permute-start.14 = (bf16[2,2048,128]{2,1,0:T(8,128)(2,1)S(1)}, bf16[2,2048,128]{2,1,0:T(8,128)(2,1)S(1)}, u32[]{:S(2)}, u32[]{:S(2)}) collective-permute-start(bf16[2,2048,128]{2,1,0:T(8,128)(2,1)S(1)} %copy-done.14), channel_id=1, source_target_pairs={{0,4},{2,6},{4,0},{6,2},{8,12},{10,14},{12,8},{14,10},{16,20},{18,... | collective-permute-start | bytes 3145736 | tf_op jit(solution)/shard_map/ppermute | solution.py:399
  66.1 13.7 %copy-start.13 = (bf16[512,1024]{1,0:T(8,128)(2,1)S(1)}, bf16[512,1024]{1,0:T(8,128)(2,1)}, u32[]{:S(2)}) copy-start(bf16[512,1024]{1,0:T(8,128)(2,1)} %param.17) | copy-start | bytes 3145732
  73.6 32.5 %collective-permute-start.16 = (bf16[528,512]{1,0:T(8,128)(2,1)S(1)}, bf16[528,512]{1,0:T(8,128)(2,1)S(1)}, u32[]{:S(2)}, u32[]{:S(2)}) collective-permute-start(bf16[528,512]{1,0:T(8,128)(2,1)S(1)} %shard_map.158.refs_0_), channel_id=1, source_target_pairs={{0,24},{2,26},{4,28},{6,30},{8,16},{10,18},{12,20},{14,22},{16,8},... | collective-permute-start | bytes 1622024 | tf_op jit(solution)/shard_map/ppermute | solution.py:399
  79.7 2.0 %collective-permute-start.12 = (bf16[1,2048,128]{2,1,0:T(8,128)(2,1)S(1)}, bf16[1,2048,128]{2,1,0:T(8,128)(2,1)S(1)}, u32[]{:S(2)}, u32[]{:S(2)}) collective-permute-start(bf16[1,2048,128]{2,1,0:T(8,128)(2,1)S(1)} %shard_map.160), channel_id=1, source_target_pairs={{0,2},{2,0},{4,6},{6,4},{8,10},{10,8},{12,14},{14,12},{16,18},{18,... | collective-permute-start | bytes 1572872 | tf_op jit(solution)/shard_map/ppermute | solution.py:399
  79.8 29.2 %collective-permute-start.19 = (bf16[512,1024]{1,0:T(8,128)(2,1)S(1)}, bf16[512,1024]{1,0:T(8,128)(2,1)S(1)}, u32[]{:S(2)}, u32[]{:S(2)}) collective-permute-start(bf16[512,1024]{1,0:T(8,128)(2,1)S(1)} %copy-done.13), channel_id=1, source_target_pairs={{0,1},{1,0},{2,3},{3,2},{4,5},{5,4},{6,7},{7,6},{8,9},{9,8},{10,11... | collective-permute-start | bytes 3145736 | tf_op jit(solution)/shard_map/ppermute | solution.py:402
  87.5 18.9 %collective-permute-start.17 = (bf16[528,512]{1,0:T(8,128)(2,1)S(1)}, bf16[528,512]{1,0:T(8,128)(2,1)S(1)}, u32[]{:S(2)}, u32[]{:S(2)}) collective-permute-start(bf16[528,512]{1,0:T(8,128)(2,1)S(1)} %shard_map.161.after_ref), channel_id=1, source_target_pairs={{0,8},{2,10},{4,12},{6,14},{8,0},{10,2},{12,4},{14,6},{16,24},{18,... | collective-permute-start | bytes 1622024 | tf_op jit(solution)/shard_map/ppermute | solution.py:399
  101.4 2.4 %collective-permute-start.15 = (bf16[1,2048,128]{2,1,0:T(8,128)(2,1)S(1)}, bf16[1,2048,128]{2,1,0:T(8,128)(2,1)S(1)}, u32[]{:S(2)}, u32[]{:S(2)}) collective-permute-start(bf16[1,2048,128]{2,1,0:T(8,128)(2,1)S(1)} %constant_dynamic-slice_fusion), channel_id=1, source_target_pairs={{0,2},{2,0},{4,6},{6,4},{8,10},{10,8},{12,14},{14,12},{16,18},{18,... | collective-permute-start | bytes 1572872 | tf_op jit(solution)/shard_map/ppermute | solution.py:399
  107.8 8.5 %collective-permute-start.18 = (bf16[512,256]{1,0:T(8,128)(2,1)S(1)}, bf16[512,256]{1,0:T(8,128)(2,1)S(1)}, u32[]{:S(2)}, u32[]{:S(2)}) collective-permute-start(bf16[512,256]{1,0:T(8,128)(2,1)S(1)} %slice.55), channel_id=1, source_target_pairs={{0,1},{1,0},{2,3},{3,2},{4,5},{5,4},{6,7},{7,6},{8,9},{9,8},{10,11... | collective-permute-start | bytes 786440 | tf_op jit(solution)/shard_map/ppermute | solution.py:402
  (7 other events, 23.2 us)

commit v5 on v4

--- a/solution.py
+++ b/solution.py
@@ -46,13 +46,14 @@
     )(*earlier)
 
 
-def deal_kernel(counts, at_ref, from_ref, after_ref, *refs):
+def deal_kernel(choose, from_ref, after_ref, *refs):
     del after_ref
-    outs, (held, into, out_of) = refs[: len(counts)], refs[len(counts) :]
-    places = [(out, i) for count, out in zip(counts, outs) for i in range(count)]
+    hands = choose(lax.axis_index("req"))
+    outs, (held, into, out_of) = refs[: len(hands)], refs[len(hands) :]
+    places = [(out, i, row) for hand, out in zip(hands, outs) for i, row in enumerate(hand)]
     reads, writes = [], []
-    for at, (out, i) in enumerate(places):
-        reads.append(pltpu.make_async_copy(from_ref.at[at_ref[at]], held.at[at], into.at[at]))
+    for at, (out, i, row) in enumerate(places):
+        reads.append(pltpu.make_async_copy(from_ref.at[row], held.at[at], into.at[at]))
         writes.append(pltpu.make_async_copy(held.at[at], out.at[i], out_of.at[at]))
     for copy in reads:
         copy.start()
@@ -63,28 +64,25 @@
         copy.wait()
 
 
-def deal(source, hands, after, vmem_limit):
-    counts = [len(rows) for rows in hands]
+def deal(source, choose, after, vmem_limit):
+    counts = [len(hand) for hand in choose(0)]
     total = sum(counts)
     anywhere = pl.BlockSpec(memory_space=pl.ANY)
     return pl.pallas_call(
-        functools.partial(deal_kernel, counts),
+        functools.partial(deal_kernel, choose),
         out_shape=[
             jax.ShapeDtypeStruct((count,) + source.shape[1:], source.dtype) for count in counts
         ],
-        grid_spec=pltpu.PrefetchScalarGridSpec(
-            num_scalar_prefetch=1,
-            in_specs=[anywhere] * 2,
-            out_specs=[anywhere] * len(counts),
-            scratch_shapes=[
-                pltpu.VMEM((total,) + source.shape[1:], source.dtype),
-                pltpu.SemaphoreType.DMA((total,)),
-                pltpu.SemaphoreType.DMA((total,)),
-            ],
-        ),
+        in_specs=[anywhere] * 2,
+        out_specs=[anywhere] * len(counts),
+        scratch_shapes=[
+            pltpu.VMEM((total,) + source.shape[1:], source.dtype),
+            pltpu.SemaphoreType.DMA((total,)),
+            pltpu.SemaphoreType.DMA((total,)),
+        ],
         compiler_params=pltpu.CompilerParams(vmem_limit_bytes=vmem_limit),
         cost_estimate=COST,
-    )(jnp.stack([row for rows in hands for row in rows]), source, after)
+    )(source, after)
 
 
 def cache_kernel(shape, sent, at_ref, after_ref, q_ref, fill_ref, *refs):
@@ -435,13 +433,17 @@
     cache = cache.reshape(devices, span, 2, heads, HD).transpose(0, 1, 3, 2, 4)
     cache = cache.reshape(devices, span * heads * 2, HD)
 
-    hands = []
-    for d in offsets:
-        start = (plane ^ d) * GROUP + ((place // 2) ^ 1) * 2
-        hands.append([start, start + 1])
-    for k in (1, 0):
-        hands.append([z * GROUP + (place ^ k) for z in range(planes)])
-    pieces = dict(zip(offsets, deal(cache, hands[:1], gain, 56 * 2**20)))
+    def hands(here):
+        plane, place = here // GROUP, here % GROUP
+        rows = []
+        for d in offsets:
+            start = (plane ^ d) * GROUP + ((place // 2) ^ 1) * 2
+            rows.append([start, start + 1])
+        for k in (1, 0):
+            rows.append([z * GROUP + (place ^ k) for z in range(planes)])
+        return rows
+
+    pieces = dict(zip(offsets, deal(cache, lambda here: hands(here)[:1], gain, 56 * 2**20)))
 
     def with_fill(value, d):
         rows = jnp.concatenate([slot_fill[d], slot_fill[d ^ 1]], axis=0)
@@ -454,7 +456,7 @@
     def pass_on(d, *earlier):
         piece = ordered(across[d], *earlier)
         if d:
-            (piece,) = deal(piece, [[1 - core]], gain, 2 * 2**20)
+            (piece,) = deal(piece, lambda here: [[1 - here % 2]], gain, 2 * 2**20)
         else:
             piece = lax.dynamic_index_in_dim(piece, 1 - core, 0)
         sibling[d] = swap(piece, 1)
@@ -469,7 +471,7 @@
     normed_rest = norm(ordered(jnp.concatenate(others, axis=0), query_here))
     query_rest = projection(normed_rest, flat[:, :cols]).astype(bf16)
     far_rest[first] = swap(query_rest, first * GROUP)
-    *rest, column, own = deal(cache, hands[1:], query_rest, 56 * 2**20)
+    *rest, column, own = deal(cache, lambda here: hands(here)[1:], query_rest, 56 * 2**20)
     pieces |= zip(offsets[1:], rest)
     across[second] = swap(pieces[second], 2)
     beside = swap(column, 1)

time: 118 us -> 118 us (level)
  starting transfers between devices: 23.4 us -> 19.6 us
  waiting for transfers between devices: 32.8 us -> 36.4 us
  Pallas kernels: 47.3 us -> 45.1 us
  local copies, waits for them, and re-layouts: 2.21 us -> 3.88 us
    ppermute x17, waiting for transfers between devices: 25.5 us -> 28.5 us  [swap(): return lax.ppermute(value, 'req', [(i, i ^ step) for i in range(devices)])]
    ppermute x17, starting transfers between devices: 17.6 us -> 15.1 us  [swap(): return lax.ppermute(value, 'req', [(i, i ^ step) for i in range(devices)])]
    unnamed x39 -> x37, local copies, waits for them, and re-layouts: 1.49 us -> 3.74 us
    pallas_call x5, Pallas kernels: 10.7 us -> 8.58 us  [deal(): pl.pallas_call(functools.partial(deal_kernel, choose), out_shape=[jax.Sha...]
    ppermute x3, starting transfers between devices: 5.77 us -> 4.43 us  [turn(): lax.ppermute(value, 'head', [(i, (i - step) % n_head) for i in range(n_he...]
    concatenate x2, other arithmetic: 0.74 us -> 1.93 us  [with_fill(): return jnp.concatenate([value, rows.astype(bf16)], axis=0)]
  transfers between devices with their start and end apart: 20 -> 20, of which waited for: 9 -> 9; matrix products, arithmetic and copies ran while one was open for 9% -> 11% of each run, Pallas kernels for 40% -> 38%
where the time goes in v5:
time: 118 us
  Pallas kernels  45.1 us (38%)
  waiting for transfers between devices  36.4 us (31%)
  starting transfers between devices  19.6 us (17%)
  matrix products  6.57 us (6%)
  other arithmetic  4.69 us (4%)
  local copies, waits for them, and re-layouts  3.88 us (3%)
  between operations  1.81 us (2%)
    ppermute x17, waiting for transfers between devices, swap(): return lax.ppermute(value, 'req', [(i, i ^ step) for i in range(devices)])  28.5 us
    pallas_call x6, Pallas kernels, cache_attention(): pl.pallas_call(functools.partial(cache_kernel, (span, heads, count, fill_...  25.9 us
    ppermute x17, starting transfers between devices, swap(): return lax.ppermute(value, 'req', [(i, i ^ step) for i in range(devices)])  15.1 us
    pallas_call x5, Pallas kernels, deal(): pl.pallas_call(functools.partial(deal_kernel, choose), out_shape=[jax.Sha...  8.58 us
    ppermute x3, waiting for transfers between devices, turn(): lax.ppermute(value, 'head', [(i, (i - step) % n_head) for i in range(n_he...  7.92 us
    dot_general x5, matrix products, dot(): lax.dot_general(left, right, (contract, ((), ())), precision=precision, p...  6.57 us
    pallas_call x1, Pallas kernels, memory_pass(): pl.pallas_call(functools.partial(memory_kernel, count), out_shape=(jax.Sh...  5.97 us
    ppermute x3, starting transfers between devices, turn(): lax.ppermute(value, 'head', [(i, (i - step) % n_head) for i in range(n_he...  4.43 us
  transfers between devices with their start and end apart: 20, of which 9 were waited for; matrix products, arithmetic and copies ran while one was open for 11% of the time, Pallas kernels for 38%

profile of v5, /device:TPU:0, one launch (start us, length us, event | category | flops | bytes accessed | tf_op | source)
XLA Modules:
  0.0 118.0 jit_solution(9748381670692099169)
XLA Ops:
  0.6 3.0 %collective-permute-start = (bf16[256,1024]{1,0:T(8,128)(2,1)}, bf16[256,1024]{1,0:T(8,128)(2,1)S(1)}, u32[]{:S(2)}, u32[]{:S(2)}) collective-permute-start(bf16[256,1024]{1,0:T(8,128)(2,1)} %bitcast.46), channel_id=1, source_target_pairs={{0,1},{1,0},{2,3},{3,2},{4,5},{5,4},{6,7},{7,6},{8,9},{9,8},{10,11... | collective-permute-start | bytes 1572872 | tf_op jit(solution)/shard_map/ppermute | solution.py:400
  3.7 2.1 %shard_map.149 = bf16[2,2048,128]{2,1,0:T(8,128)(2,1)} custom-call(bf16[16,2048,128]{2,1,0:T(8,128)(2,1)} %bitcast.40, bf16[1024]{0:T(1024)(128)(2,1)} %after_ref.7), custom_call_target="tpu_custom_call" | custom-call | flops 1 | bytes 1 | tf_op jit(solution)/shard_map/pallas_call | solution.py:71
  5.8 1.6 %collective-permute-start.4 = (bf16[2,2048,128]{2,1,0:T(8,128)(2,1)}, bf16[2,2048,128]{2,1,0:T(8,128)(2,1)S(1)}, u32[]{:S(2)}, u32[]{:S(2)}) collective-permute-start(bf16[2,2048,128]{2,1,0:T(8,128)(2,1)} %shard_map.149), channel_id=1, source_target_pairs={{0,4},{2,6},{4,0},{6,2},{8,12},{10,14},{12,8},{14,10},{16,20},{18,... | collective-permute-start | bytes 3145736 | tf_op jit(solution)/shard_map/ppermute | solution.py:397
  8.9 3.6 %copy.23 = bf16[128,8,4,512]{3,1,2,0:T(8,128)(2,1)S(1)} copy(bf16[128,8,4,512]{3,2,1,0:T(4,128)(2,1)} %bitcast.42) | data formatting | bytes 8388608
  13.2 1.2 %pad_maximum_fusion.1 = bf16[544,256]{1,0:T(8,128)(2,1)} fusion(bf16[32,256]{1,0:T(8,128)(2,1)S(1)} %fusion.28, bf16[512,256]{1,0:T(8,128)(2,1)S(1)} %convolution_convert_fusion.3), kind=kLoop, calls=%fused_computation.33 | loop fusion | flops 557056 | bytes 557056 | tf_op jit(solution)/shard_map/concatenate | solution.py:452
  14.4 2.6 %collective-permute-start.1 = (bf16[544,256]{1,0:T(8,128)(2,1)}, bf16[544,256]{1,0:T(8,128)(2,1)S(1)}, u32[]{:S(2)}, u32[]{:S(2)}) collective-permute-start(bf16[544,256]{1,0:T(8,128)(2,1)} %pad_maximum_fusion.1), channel_id=1, source_target_pairs={{0,16},{2,18},{4,20},{6,22},{8,24},{10,26},{12,28},{14,30},{16,0},... | collective-permute-start | bytes 835592 | tf_op jit(solution)/shard_map/ppermute | solution.py:397
  17.8 1.6 %collective-permute-start.9 = (bf16[528,256]{1,0:T(8,128)(2,1)}, bf16[528,256]{1,0:T(8,128)(2,1)}, u32[]{:S(2)}, u32[]{:S(2)}) collective-permute-start(bf16[528,256]{1,0:T(8,128)(2,1)} %pad_maximum_fusion.2), channel_id=1, source_target_pairs={{0,8},{2,10},{4,12},{6,14},{8,0},{10,2},{12,4},{14,6},{16,24},{18,... | collective-permute-start | bytes 811016 | tf_op jit(solution)/shard_map/ppermute | solution.py:397
  19.7 2.4 %convolution_convert_fusion.2.after_ref = bf16[512,256]{1,0:T(8,128)(2,1)} fusion(bf16[256,1024]{1,0:T(8,128)(2,1)S(1)} %fusion.14, bf16[1024,2048]{1,0:T(8,128)(2,1)} %bitcast.44), kind=kOutput, calls=%fused_computation.13 | convolution fusion | flops 268566528 | bytes 1835008 | tf_op jit(solution)/shard_map/dot_general | solution.py:30
  22.2 6.2 %shard_map.152 = (bf16[2,2048,128]{2,1,0:T(8,128)(2,1)}, bf16[2,2048,128]{2,1,0:T(8,128)(2,1)}, bf16[2,2048,128]{2,1,0:T(8,128)(2,1)}, bf16[4,2048,128]{2,1,0:T(8,128)(2,1)}, bf16[4,2048,128]{2,1,0:T(8,128)(2,1)}) custom-call(bf16[16,2048,128]{2,1,0:T(8,128)(2,1)} %bitcast.41, bf16[512,256]{1,0:T(8,128)(2,1)} %convolution_convert_fusion.2.after_ref), custom_call_target="tpu_custom_call" | custom-call | flops 1 | bytes 1 | tf_op jit(solution)/shard_map/pallas_call | solution.py:71
  29.2 1.9 %fusion.38 = (bf16[1536,512]{1,0:T(8,128)(2,1)S(1)}, f32[1536,512]{1,0:T(8,128)S(1)}) fusion(bf16[256,1024]{1,0:T(8,128)(2,1)S(1)} %fusion.14, bf16[256,1024]{1,0:T(8,128)(2,1)S(1)} %fusion.11, bf16[1024,2048]{1,0:T(8,128)(2,1)S(1)} %bitcast.45), kind=kOutput, calls=%fused_computation.73 | convolution fusion | flops 1613496320 | bytes 8912896 | tf_op jit(solution)/shard_map/dot_general | solution.py:30
  31.9 3.3 %shard_map.150 = (f32[4,128,512]{2,1,0:T(8,128)S(1)}, f32[4,1,512]{2,1,0:T(1,128)S(1)}) custom-call(s32[1]{0:T(128)} %bitcast.side_ref, bf16[512,512]{1,0:T(8,128)(2,1)S(1)} %pad_maximum_fusion.q_ref, bf16[512,512]{1,0:T(8,128)(2,1)S(1)} %get-tuple-element.59.k_ref, bf16[512,512]{1,0:T(8,128)(2,1)S(1)} %get-tuple-element.58.v_ref, ...), custom_call_target="tpu_custom_call" | custom-call | flops 1 | bytes 1 | tf_op jit(solution)/shard_map/pallas_call | solution.py:229
  35.2 1.4 %collective-permute-start.10 = (bf16[512,256]{1,0:T(8,128)(2,1)S(1)}, bf16[512,256]{1,0:T(8,128)(2,1)S(1)}, u32[]{:S(2)}, u32[]{:S(2)}) collective-permute-start(bf16[512,256]{1,0:T(8,128)(2,1)S(1)} %copy-done.11), channel_id=1, source_target_pairs={{0,8},{2,10},{4,12},{6,14},{8,0},{10,2},{12,4},{14,6},{16,24},{18,... | collective-permute-start | bytes 786440 | tf_op jit(solution)/shard_map/ppermute | solution.py:397
  36.8 7.2 %collective-permute-done.2 = bf16[512,256]{1,0:T(8,128)(2,1)S(1)} collective-permute-done((bf16[512,256]{1,0:T(8,128)(2,1)S(1)}, bf16[512,256]{1,0:T(8,128)(2,1)S(1)}, u32[]{:S(2)}, u32[]{:S(2)}) %collective-permute-start.2) | collective-permute-done | bytes 262176 | tf_op jit(solution)/shard_map/ppermute | solution.py:397
  44.6 4.4 %collective-permute-done.10 = bf16[512,256]{1,0:T(8,128)(2,1)S(1)} collective-permute-done((bf16[512,256]{1,0:T(8,128)(2,1)S(1)}, bf16[512,256]{1,0:T(8,128)(2,1)S(1)}, u32[]{:S(2)}, u32[]{:S(2)}) %collective-permute-start.10) | collective-permute-done | bytes 262176 | tf_op jit(solution)/shard_map/ppermute | solution.py:397
  50.0 5.8 %shard_map.154.after_ref = bf16[528,512]{1,0:T(8,128)(2,1)S(1)} custom-call(s32[4]{0:T(128)S(1)} %pad_add_fusion.at_ref, f32[8,128]{1,0:T(8,128)S(1)} %shard_map.151.after_ref, bf16[544,512]{1,0:T(8,128)(2,1)S(1)} %fusion.20.q_ref.fill_ref, bf16[544,512]{1,0:T(8,128)(2,1)S(1)} %fusion.20.q_ref.fill_ref, bf16[4,2048,128]{2,1,0:T(8,128)(2,1)S(1)} %copy-done, ...), custom_call_target="tpu_custom_call" | custom-call | flops 1 | bytes 1 | tf_op jit(solution)/shard_map/pallas_call | solution.py:174
  55.9 1.6 %collective-permute-start.13 = (bf16[528,512]{1,0:T(8,128)(2,1)S(1)}, bf16[528,512]{1,0:T(8,128)(2,1)S(1)}, u32[]{:S(2)}, u32[]{:S(2)}) collective-permute-start(bf16[528,512]{1,0:T(8,128)(2,1)S(1)} %shard_map.154.after_ref), channel_id=1, source_target_pairs={{0,16},{2,18},{4,20},{6,22},{8,24},{10,26},{12,28},{14,30},{16,0},... | collective-permute-start | bytes 1622024 | tf_op jit(solution)/shard_map/ppermute | solution.py:397
  57.5 6.0 %shard_map.155 = (f32[512,512]{1,0:T(8,128)S(1)}, f32[2,4,128,128]{3,2,1,0:T(8,128)}) custom-call(s32[1]{0:T(128)} %bitcast.side_ref, f32[1,4]{1,0:T(1,128)S(1)} %copy-done.4, f32[1,4]{1,0:T(1,128)S(1)} %copy-done.5, f32[1,4]{1,0:T(1,128)S(1)} %copy-done.6, s32[1,8]{1,0:T(1,128)S(1)} %copy-done.7, bf16[528,512]{1,0:T(8,128)(2,1)S(1)} %shard_map.154.after_ref, ...), custom_call_target="tpu_custom_call" | custom-call | flops 1 | bytes 1 | tf_op jit(solution)/shard_map/pallas_call | solution.py:305
  63.4 1.5 %collective-permute-start.14 = (bf16[2,2048,128]{2,1,0:T(8,128)(2,1)S(1)}, bf16[2,2048,128]{2,1,0:T(8,128)(2,1)S(1)}, u32[]{:S(2)}, u32[]{:S(2)}) collective-permute-start(bf16[2,2048,128]{2,1,0:T(8,128)(2,1)S(1)} %copy-done.13), channel_id=1, source_target_pairs={{0,4},{2,6},{4,0},{6,2},{8,12},{10,14},{12,8},{14,10},{16,20},{18,... | collective-permute-start | bytes 3145736 | tf_op jit(solution)/shard_map/ppermute | solution.py:397
  65.1 1.7 %collective-permute-done.6.q_ref.fill_ref = bf16[544,512]{1,0:T(8,128)(2,1)S(1)} collective-permute-done((bf16[544,512]{1,0:T(8,128)(2,1)S(1)}, bf16[544,512]{1,0:T(8,128)(2,1)S(1)}, u32[]{:S(2)}, u32[]{:S(2)}) %collective-permute-start.6) | collective-permute-done | bytes 557088 | tf_op jit(solution)/shard_map/ppermute | solution.py:397
  67.0 5.8 %shard_map.158.refs_0_ = bf16[528,512]{1,0:T(8,128)(2,1)S(1)} custom-call(s32[4]{0:T(128)S(1)} %pad_add_fusion.1.at_ref, f32[8,128]{1,0:T(8,128)S(1)} %shard_map.156.after_ref, bf16[544,512]{1,0:T(8,128)(2,1)S(1)} %collective-permute-done.6.q_ref.fill_ref, bf16[544,512]{1,0:T(8,128)(2,1)S(1)} %collective-permute-done.6.q_ref.fill_ref, ...), custom_call_target="tpu_custom_call" | custom-call | flops 1 | bytes 1 | tf_op jit(solution)/shard_map/pallas_call | solution.py:174
  72.8 2.5 %collective-permute-start.16 = (bf16[528,512]{1,0:T(8,128)(2,1)S(1)}, bf16[528,512]{1,0:T(8,128)(2,1)S(1)}, u32[]{:S(2)}, u32[]{:S(2)}) collective-permute-start(bf16[528,512]{1,0:T(8,128)(2,1)S(1)} %shard_map.158.refs_0_), channel_id=1, source_target_pairs={{0,24},{2,26},{4,28},{6,30},{8,16},{10,18},{12,20},{14,22},{16,8},... | collective-permute-start | bytes 1622024 | tf_op jit(solution)/shard_map/ppermute | solution.py:397
  75.4 4.3 %collective-permute-done.11.from_ref.refs_2_ = bf16[2,2048,128]{2,1,0:T(8,128)(2,1)S(1)} collective-permute-done((bf16[2,2048,128]{2,1,0:T(8,128)(2,1)S(1)}, bf16[2,2048,128]{2,1,0:T(8,128)(2,1)S(1)}, u32[]{:S(2)}, u32[]{:S(2)}) %collective-permute-start.11) | collective-permute-done | bytes 1048608 | tf_op jit(solution)/shard_map/ppermute | solution.py:397
  80.5 1.3 %collective-permute-done.12.refs_3_ = bf16[1,2048,128]{2,1,0:T(8,128)(2,1)S(1)} collective-permute-done((bf16[1,2048,128]{2,1,0:T(8,128)(2,1)S(1)}, bf16[1,2048,128]{2,1,0:T(8,128)(2,1)S(1)}, u32[]{:S(2)}, u32[]{:S(2)}) %collective-permute-start.12) | collective-permute-done | bytes 524320 | tf_op jit(solution)/shard_map/ppermute | solution.py:397
  81.8 5.8 %shard_map.161.after_ref = bf16[528,512]{1,0:T(8,128)(2,1)S(1)} custom-call(s32[4]{0:T(128)S(1)} %pad_add_fusion.2.at_ref, f32[8,128]{1,0:T(8,128)S(1)} %shard_map.159.after_ref, bf16[528,512]{1,0:T(8,128)(2,1)S(1)} %fusion.21.q_ref.fill_ref, bf16[528,512]{1,0:T(8,128)(2,1)S(1)} %fusion.21.q_ref.fill_ref, bf16[4,2048,128]{2,1,0:T(8,128)(2,1)S(1)} %copy-done, ...), custom_call_target="tpu_custom_call" | custom-call | flops 1 | bytes 1 | tf_op jit(solution)/shard_map/pallas_call | solution.py:174
  88.2 3.9 %shard_map.162 = (f32[4,128,512]{2,1,0:T(8,128)S(1)}, f32[4,1,512]{2,1,0:T(1,128)S(1)}) custom-call(s32[2]{0:T(128)S(1)} %pad_add_fusion.3.at_ref, bf16[528,512]{1,0:T(8,128)(2,1)S(1)} %shard_map.161.after_ref, bf16[512,512]{1,0:T(8,128)(2,1)S(1)} %pad_maximum_fusion.q_ref, bf16[16,128]{1,0:T(8,128)(2,1)S(1)} %pad.27.fill_ref, ...), custom_call_target="tpu_custom_call" | custom-call | flops 1 | bytes 1 | tf_op jit(solution)/shard_map/pallas_call | solution.py:174
  92.0 3.2 %collective-permute-done.13.refs_1_.refs_8_.refs_9_ = bf16[528,512]{1,0:T(8,128)(2,1)S(1)} collective-permute-done((bf16[528,512]{1,0:T(8,128)(2,1)S(1)}, bf16[528,512]{1,0:T(8,128)(2,1)S(1)}, u32[]{:S(2)}, u32[]{:S(2)}) %collective-permute-start.13) | collective-permute-done | bytes 540704 | tf_op jit(solution)/shard_map/ppermute | solution.py:397
  95.2 6.2 %collective-permute-done.14.refs_0_ = bf16[2,2048,128]{2,1,0:T(8,128)(2,1)S(1)} collective-permute-done((bf16[2,2048,128]{2,1,0:T(8,128)(2,1)S(1)}, bf16[2,2048,128]{2,1,0:T(8,128)(2,1)S(1)}, u32[]{:S(2)}, u32[]{:S(2)}) %collective-permute-start.14) | collective-permute-done | bytes 1048608 | tf_op jit(solution)/shard_map/ppermute | solution.py:397
  101.5 2.3 %shard_map.164 = (f32[4,128,512]{2,1,0:T(8,128)S(1)}, f32[4,1,512]{2,1,0:T(1,128)S(1)}) custom-call(s32[1]{0:T(128)} %bitcast.7.at_ref, f32[8,128]{1,0:T(8,128)S(1)} %shard_map.163.after_ref, bf16[512,512]{1,0:T(8,128)(2,1)S(1)} %pad_maximum_fusion.q_ref, bf16[16,128]{1,0:T(8,128)(2,1)S(1)} %pad.27.fill_ref, ...), custom_call_target="tpu_custom_call" | custom-call | flops 1 | bytes 1 | tf_op jit(solution)/shard_map/pallas_call | solution.py:174
  103.8 2.3 %shard_map.165 = (f32[4,128,512]{2,1,0:T(8,128)S(1)}, f32[4,1,512]{2,1,0:T(1,128)S(1)}) custom-call(s32[1]{0:T(128)} %constant.66.clone.1.at_ref, f32[4,1,512]{2,1,0:T(1,128)S(1)} %get-tuple-element.48.after_ref.refs_5_, bf16[512,512]{1,0:T(8,128)(2,1)S(1)} %pad_maximum_fusion.q_ref, bf16[16,128]{1,0:T(8,128)(2,1)S(1)} %pad.27.fill_ref, ...), custom_call_target="tpu_custom_call" | custom-call | flops 1 | bytes 1 | tf_op jit(solution)/shard_map/pallas_call | solution.py:174
  106.1 1.4 %shard_map.166 = bf16[512,512]{1,0:T(8,128)(2,1)S(1)} custom-call(f32[4,128,512]{2,1,0:T(8,128)S(1)} %get-tuple-element.31.refs_0_, f32[4,1,512]{2,1,0:T(1,128)S(1)} %get-tuple-element.32.refs_0_.refs_1_, f32[4,128,512]{2,1,0:T(8,128)S(1)} %get-tuple-element.43.refs_2_, f32[4,1,512]{2,1,0:T(1,128)S(1)} %get-tuple-element.44.refs_0_.refs_3_, ...), custom_call_target="tpu_custom_call" | custom-call | flops 18350080 | bytes 8388608 | tf_op jit(solution)/shard_map/pallas_call | solution.py:350
  108.4 7.9 %collective-permute-done.18 = bf16[512,256]{1,0:T(8,128)(2,1)S(1)} collective-permute-done((bf16[512,256]{1,0:T(8,128)(2,1)S(1)}, bf16[512,256]{1,0:T(8,128)(2,1)S(1)}, u32[]{:S(2)}, u32[]{:S(2)}) %collective-permute-start.18) | collective-permute-done | bytes 262176 | tf_op jit(solution)/shard_map/ppermute | solution.py:400
  116.8 1.3 %fusion.6 = bf16[1,256,1024]{2,1,0:T(8,128)(2,1)} fusion(f32[256,1024]{1,0:T(8,128)S(1)} %fusion.2, bf16[512,1024]{1,0:T(8,128)(2,1)S(1)} %copy-done.12, bf16[512,512]{1,0:T(8,128)(2,1)S(1)} %shard_map.166), kind=kOutput, calls=%fused_computation.12 | convolution fusion | flops 269484032 | bytes 2883584 | tf_op jit(solution)/shard_map/dot_general | solution.py:30
  (99 shorter events, 9.0 us)
Async XLA Ops:
  0.6 18.7 %collective-permute-start = (bf16[256,1024]{1,0:T(8,128)(2,1)}, bf16[256,1024]{1,0:T(8,128)(2,1)S(1)}, u32[]{:S(2)}, u32[]{:S(2)}) collective-permute-start(bf16[256,1024]{1,0:T(8,128)(2,1)} %bitcast.46), channel_id=1, source_target_pairs={{0,1},{1,0},{2,3},{3,2},{4,5},{5,4},{6,7},{7,6},{8,9},{9,8},{10,11... | collective-permute-start | bytes 1572872 | tf_op jit(solution)/shard_map/ppermute | solution.py:400
  5.8 29.4 %collective-permute-start.4 = (bf16[2,2048,128]{2,1,0:T(8,128)(2,1)}, bf16[2,2048,128]{2,1,0:T(8,128)(2,1)S(1)}, u32[]{:S(2)}, u32[]{:S(2)}) collective-permute-start(bf16[2,2048,128]{2,1,0:T(8,128)(2,1)} %shard_map.149), channel_id=1, source_target_pairs={{0,4},{2,6},{4,0},{6,2},{8,12},{10,14},{12,8},{14,10},{16,20},{18,... | collective-permute-start | bytes 3145736 | tf_op jit(solution)/shard_map/ppermute | solution.py:397
  12.5 5.3 %copy-start.8 = (bf16[128,8,4,512]{3,1,2,0:T(8,128)(2,1)}, bf16[128,8,4,512]{3,1,2,0:T(8,128)(2,1)S(1)}, u32[]{:S(2)}) copy-start(bf16[128,8,4,512]{3,1,2,0:T(8,128)(2,1)S(1)} %copy.23) | copy-start | bytes 12582916
  14.4 22.3 %collective-permute-start.1 = (bf16[544,256]{1,0:T(8,128)(2,1)}, bf16[544,256]{1,0:T(8,128)(2,1)S(1)}, u32[]{:S(2)}, u32[]{:S(2)}) collective-permute-start(bf16[544,256]{1,0:T(8,128)(2,1)} %pad_maximum_fusion.1), channel_id=1, source_target_pairs={{0,16},{2,18},{4,20},{6,22},{8,24},{10,26},{12,28},{14,30},{16,0},... | collective-permute-start | bytes 835592 | tf_op jit(solution)/shard_map/ppermute | solution.py:397
  17.8 13.4 %collective-permute-start.9 = (bf16[528,256]{1,0:T(8,128)(2,1)}, bf16[528,256]{1,0:T(8,128)(2,1)}, u32[]{:S(2)}, u32[]{:S(2)}) collective-permute-start(bf16[528,256]{1,0:T(8,128)(2,1)} %pad_maximum_fusion.2), channel_id=1, source_target_pairs={{0,8},{2,10},{4,12},{6,14},{8,0},{10,2},{12,4},{14,6},{16,24},{18,... | collective-permute-start | bytes 811016 | tf_op jit(solution)/shard_map/ppermute | solution.py:397
  22.2 6.6 %copy-start.11 = (bf16[512,256]{1,0:T(8,128)(2,1)S(1)}, bf16[512,256]{1,0:T(8,128)(2,1)}, u32[]{:S(2)}) copy-start(bf16[512,256]{1,0:T(8,128)(2,1)} %convolution_convert_fusion.2.after_ref) | copy-start | bytes 786436
  22.2 7.0 %copy-start.9 = (bf16[128,8,4,512]{3,1,2,0:T(8,128)(2,1)S(1)}, bf16[128,8,4,512]{3,1,2,0:T(8,128)(2,1)}, u32[]{:S(2)}) copy-start(bf16[128,8,4,512]{3,1,2,0:T(8,128)(2,1)} %copy-done.8) | copy-start | bytes 12582916
  28.4 21.6 %collective-permute-start.3 = (bf16[4,2048,128]{2,1,0:T(8,128)(2,1)}, bf16[4,2048,128]{2,1,0:T(8,128)(2,1)S(1)}, u32[]{:S(2)}, u32[]{:S(2)}) collective-permute-start(bf16[4,2048,128]{2,1,0:T(8,128)(2,1)} %get-tuple-element.34), channel_id=1, source_target_pairs={{0,2},{2,0},{4,6},{6,4},{8,10},{10,8},{12,14},{14,12},{16,18},{18,... | collective-permute-start | bytes 6291464 | tf_op jit(solution)/shard_map/ppermute | solution.py:397
  28.8 15.2 %collective-permute-start.2 = (bf16[512,256]{1,0:T(8,128)(2,1)S(1)}, bf16[512,256]{1,0:T(8,128)(2,1)S(1)}, u32[]{:S(2)}, u32[]{:S(2)}) collective-permute-start(bf16[512,256]{1,0:T(8,128)(2,1)S(1)} %copy-done.11), channel_id=1, source_target_pairs={{0,16},{2,18},{4,20},{6,22},{8,24},{10,26},{12,28},{14,30},{16,0},... | collective-permute-start | bytes 786440 | tf_op jit(solution)/shard_map/ppermute | solution.py:397
  31.2 33.7 %collective-permute-start.7 = (bf16[2,2048,128]{2,1,0:T(8,128)(2,1)S(1)}, bf16[2,2048,128]{2,1,0:T(8,128)(2,1)S(1)}, u32[]{:S(2)}, u32[]{:S(2)}) collective-permute-start(bf16[2,2048,128]{2,1,0:T(8,128)(2,1)S(1)} %copy-done.15), channel_id=1, source_target_pairs={{0,4},{2,6},{4,0},{6,2},{8,12},{10,14},{12,8},{14,10},{16,20},{18,... | collective-permute-start | bytes 3145736 | tf_op jit(solution)/shard_map/ppermute | solution.py:397
  31.9 12.1 %copy-start.14 = (bf16[2,2048,128]{2,1,0:T(8,128)(2,1)S(1)}, bf16[2,2048,128]{2,1,0:T(8,128)(2,1)}, u32[]{:S(2)}) copy-start(bf16[2,2048,128]{2,1,0:T(8,128)(2,1)} %get-tuple-element.41) | copy-start | bytes 3145732
  35.2 13.7 %collective-permute-start.10 = (bf16[512,256]{1,0:T(8,128)(2,1)S(1)}, bf16[512,256]{1,0:T(8,128)(2,1)S(1)}, u32[]{:S(2)}, u32[]{:S(2)}) collective-permute-start(bf16[512,256]{1,0:T(8,128)(2,1)S(1)} %copy-done.11), channel_id=1, source_target_pairs={{0,8},{2,10},{4,12},{6,14},{8,0},{10,2},{12,4},{14,6},{16,24},{18,... | collective-permute-start | bytes 786440 | tf_op jit(solution)/shard_map/ppermute | solution.py:397
  36.7 13.2 %collective-permute-start.5 = (bf16[1,2048,128]{2,1,0:T(8,128)(2,1)S(1)}, bf16[1,2048,128]{2,1,0:T(8,128)(2,1)S(1)}, u32[]{:S(2)}, u32[]{:S(2)}) collective-permute-start(bf16[1,2048,128]{2,1,0:T(8,128)(2,1)S(1)} %shard_map.153), channel_id=1, source_target_pairs={{0,2},{2,0},{4,6},{6,4},{8,10},{10,8},{12,14},{14,12},{16,18},{18,... | collective-permute-start | bytes 1572872 | tf_op jit(solution)/shard_map/ppermute | solution.py:397
  44.0 35.7 %collective-permute-start.11 = (bf16[2,2048,128]{2,1,0:T(8,128)(2,1)S(1)}, bf16[2,2048,128]{2,1,0:T(8,128)(2,1)S(1)}, u32[]{:S(2)}, u32[]{:S(2)}) collective-permute-start(bf16[2,2048,128]{2,1,0:T(8,128)(2,1)S(1)} %copy-done.14), channel_id=1, source_target_pairs={{0,4},{2,6},{4,0},{6,2},{8,12},{10,14},{12,8},{14,10},{16,20},{18,... | collective-permute-start | bytes 3145736 | tf_op jit(solution)/shard_map/ppermute | solution.py:397
  44.5 5.4 %copy-start = (bf16[4,2048,128]{2,1,0:T(8,128)(2,1)S(1)}, bf16[4,2048,128]{2,1,0:T(8,128)(2,1)}, u32[]{:S(2)}) copy-start(bf16[4,2048,128]{2,1,0:T(8,128)(2,1)} %get-tuple-element.33.refs_0_) | copy-start | bytes 6291460
  48.9 17.9 %collective-permute-start.6 = (bf16[544,512]{1,0:T(8,128)(2,1)S(1)}, bf16[544,512]{1,0:T(8,128)(2,1)S(1)}, u32[]{:S(2)}, u32[]{:S(2)}) collective-permute-start(bf16[544,512]{1,0:T(8,128)(2,1)S(1)} %fusion.20.q_ref.fill_ref), channel_id=1, source_target_pairs={{0,8},{2,10},{4,12},{6,14},{8,0},{10,2},{12,4},{14,6},{16,24},{18,... | collective-permute-start | bytes 1671176 | tf_op jit(solution)/shard_map/ppermute | solution.py:397
  50.0 7.5 %copy-start.1 = (f32[2,1,4,128,128]{4,3,2,1,0:T(8,128)S(1)}, f32[2,1,4,128,128]{4,3,2,1,0:T(8,128)}, u32[]{:S(2)}) copy-start(f32[2,1,4,128,128]{4,3,2,1,0:T(8,128)} %param.23) | copy-start | bytes 1572868
  50.0 7.5 %copy-start.4 = (f32[1,4]{1,0:T(1,128)S(1)}, f32[1,4]{1,0:T(1,128)}, u32[]{:S(2)}) copy-start(f32[1,4]{1,0:T(1,128)} %retention_ref.1) | copy-start | bytes 52
  50.0 7.5 %copy-start.5 = (f32[1,4]{1,0:T(1,128)S(1)}, f32[1,4]{1,0:T(1,128)}, u32[]{:S(2)}) copy-start(f32[1,4]{1,0:T(1,128)} %momentum_ref.1) | copy-start | bytes 52
  50.0 7.5 %copy-start.6 = (f32[1,4]{1,0:T(1,128)S(1)}, f32[1,4]{1,0:T(1,128)}, u32[]{:S(2)}) copy-start(f32[1,4]{1,0:T(1,128)} %step_ref.1) | copy-start | bytes 52
  50.0 7.5 %copy-start.7 = (s32[1,8]{1,0:T(1,128)S(1)}, s32[1,8]{1,0:T(1,128)}, u32[]{:S(2)}) copy-start(s32[1,8]{1,0:T(1,128)} %halving_ref.1) | copy-start | bytes 100
  55.8 7.6 %copy-start.13 = (bf16[2,2048,128]{2,1,0:T(8,128)(2,1)S(1)}, bf16[2,2048,128]{2,1,0:T(8,128)(2,1)}, u32[]{:S(2)}) copy-start(bf16[2,2048,128]{2,1,0:T(8,128)(2,1)} %get-tuple-element.46) | copy-start | bytes 3145732
  55.9 39.4 %collective-permute-start.13 = (bf16[528,512]{1,0:T(8,128)(2,1)S(1)}, bf16[528,512]{1,0:T(8,128)(2,1)S(1)}, u32[]{:S(2)}, u32[]{:S(2)}) collective-permute-start(bf16[528,512]{1,0:T(8,128)(2,1)S(1)} %shard_map.154.after_ref), channel_id=1, source_target_pairs={{0,16},{2,18},{4,20},{6,22},{8,24},{10,26},{12,28},{14,30},{16,0},... | collective-permute-start | bytes 1622024 | tf_op jit(solution)/shard_map/ppermute | solution.py:397
  63.4 38.0 %collective-permute-start.14 = (bf16[2,2048,128]{2,1,0:T(8,128)(2,1)S(1)}, bf16[2,2048,128]{2,1,0:T(8,128)(2,1)S(1)}, u32[]{:S(2)}, u32[]{:S(2)}) collective-permute-start(bf16[2,2048,128]{2,1,0:T(8,128)(2,1)S(1)} %copy-done.13), channel_id=1, source_target_pairs={{0,4},{2,6},{4,0},{6,2},{8,12},{10,14},{12,8},{14,10},{16,20},{18,... | collective-permute-start | bytes 3145736 | tf_op jit(solution)/shard_map/ppermute | solution.py:397
  65.0 2.0 %collective-permute-start.8 = (bf16[1,2048,128]{2,1,0:T(8,128)(2,1)S(1)}, bf16[1,2048,128]{2,1,0:T(8,128)(2,1)S(1)}, u32[]{:S(2)}, u32[]{:S(2)}) collective-permute-start(bf16[1,2048,128]{2,1,0:T(8,128)(2,1)S(1)} %shard_map.157), channel_id=1, source_target_pairs={{0,2},{2,0},{4,6},{6,4},{8,10},{10,8},{12,14},{14,12},{16,18},{18,... | collective-permute-start | bytes 1572872 | tf_op jit(solution)/shard_map/ppermute | solution.py:397
  65.1 14.8 %copy-start.12 = (bf16[512,1024]{1,0:T(8,128)(2,1)S(1)}, bf16[512,1024]{1,0:T(8,128)(2,1)}, u32[]{:S(2)}) copy-start(bf16[512,1024]{1,0:T(8,128)(2,1)} %param.17) | copy-start | bytes 3145732
  72.8 33.3 %collective-permute-start.16 = (bf16[528,512]{1,0:T(8,128)(2,1)S(1)}, bf16[528,512]{1,0:T(8,128)(2,1)S(1)}, u32[]{:S(2)}, u32[]{:S(2)}) collective-permute-start(bf16[528,512]{1,0:T(8,128)(2,1)S(1)} %shard_map.158.refs_0_), channel_id=1, source_target_pairs={{0,24},{2,26},{4,28},{6,30},{8,16},{10,18},{12,20},{14,22},{16,8},... | collective-permute-start | bytes 1622024 | tf_op jit(solution)/shard_map/ppermute | solution.py:397
  79.8 2.0 %collective-permute-start.12 = (bf16[1,2048,128]{2,1,0:T(8,128)(2,1)S(1)}, bf16[1,2048,128]{2,1,0:T(8,128)(2,1)S(1)}, u32[]{:S(2)}, u32[]{:S(2)}) collective-permute-start(bf16[1,2048,128]{2,1,0:T(8,128)(2,1)S(1)} %shard_map.160), channel_id=1, source_target_pairs={{0,2},{2,0},{4,6},{6,4},{8,10},{10,8},{12,14},{14,12},{16,18},{18,... | collective-permute-start | bytes 1572872 | tf_op jit(solution)/shard_map/ppermute | solution.py:397
  79.9 28.5 %collective-permute-start.19 = (bf16[512,1024]{1,0:T(8,128)(2,1)S(1)}, bf16[512,1024]{1,0:T(8,128)(2,1)S(1)}, u32[]{:S(2)}, u32[]{:S(2)}) collective-permute-start(bf16[512,1024]{1,0:T(8,128)(2,1)S(1)} %copy-done.12), channel_id=1, source_target_pairs={{0,1},{1,0},{2,3},{3,2},{4,5},{5,4},{6,7},{7,6},{8,9},{9,8},{10,11... | collective-permute-start | bytes 3145736 | tf_op jit(solution)/shard_map/ppermute | solution.py:400
  87.6 18.5 %collective-permute-start.17 = (bf16[528,512]{1,0:T(8,128)(2,1)S(1)}, bf16[528,512]{1,0:T(8,128)(2,1)S(1)}, u32[]{:S(2)}, u32[]{:S(2)}) collective-permute-start(bf16[528,512]{1,0:T(8,128)(2,1)S(1)} %shard_map.161.after_ref), channel_id=1, source_target_pairs={{0,8},{2,10},{4,12},{6,14},{8,0},{10,2},{12,4},{14,6},{16,24},{18,... | collective-permute-start | bytes 1622024 | tf_op jit(solution)/shard_map/ppermute | solution.py:397
  101.5 2.4 %collective-permute-start.15 = (bf16[1,2048,128]{2,1,0:T(8,128)(2,1)S(1)}, bf16[1,2048,128]{2,1,0:T(8,128)(2,1)S(1)}, u32[]{:S(2)}, u32[]{:S(2)}) collective-permute-start(bf16[1,2048,128]{2,1,0:T(8,128)(2,1)S(1)} %constant_dynamic-slice_fusion), channel_id=1, source_target_pairs={{0,2},{2,0},{4,6},{6,4},{8,10},{10,8},{12,14},{14,12},{16,18},{18,... | collective-permute-start | bytes 1572872 | tf_op jit(solution)/shard_map/ppermute | solution.py:397
  107.6 8.8 %collective-permute-start.18 = (bf16[512,256]{1,0:T(8,128)(2,1)S(1)}, bf16[512,256]{1,0:T(8,128)(2,1)S(1)}, u32[]{:S(2)}, u32[]{:S(2)}) collective-permute-start(bf16[512,256]{1,0:T(8,128)(2,1)S(1)} %slice.55), channel_id=1, source_target_pairs={{0,1},{1,0},{2,3},{3,2},{4,5},{5,4},{6,7},{7,6},{8,9},{9,8},{10,11... | collective-permute-start | bytes 786440 | tf_op jit(solution)/shard_map/ppermute | solution.py:400
  (6 other events, 20.2 us)
